TPU v7x, 512 devices: a whole 4x8x8 slice. The times are simulated.
512 devices in a mesh: grp: 8 (over y_lo, x), dev: 64 (over z, y_hi, core).
Axes of the slice: x: 4, y: 8 (y_hi: 4, y_lo: 2; y = y_hi * 2 + y_lo), z: 8, core: 2. Of those that a mesh axis runs over, the one named last changes fastest.
Arguments:
- e_field: float32 [3, 64, 512, 640], P(None, 'grp', 'dev'), may hold values from -6 to 6
- h_field: float32 [3, 64, 512, 640], P(None, 'grp', 'dev'), may hold values from -6 to 6
- polar: float32 [2, 3, 64, 512, 640], P(None, None, 'grp', 'dev'), may hold values from -3 to 3
- material: int32 [64, 512], P('grp', 'dev'), may hold values from 0 to 3, as said below
- eps_table: float32 [4], replicated, may hold values from 1 to 4
- loss_table: float32 [4], replicated, may hold values from 0.02 to 0.4
- lorentz: float32 [3], replicated, may hold values from 0.3 to 1.2
- freqs: float32 [4], replicated, may hold values from 0.3 to 1.5
Outputs:
- e_final: float32 [3, 64, 512, 640], P(None, 'grp', 'dev')
- h_final: float32 [3, 64, 512, 640], P(None, 'grp', 'dev')
- polar_final: float32 [2, 3, 64, 512, 640], P(None, None, 'grp', 'dev')
- spectrum: float32 [4, 2, 3, 8, 512, 640], P(None, None, None, 'grp', 'dev')
Inputs may be any that keep to these rules, and one draw needn't show every extreme that they name: `material`: kind 3 names at most 32 of the 64 rows of one device's block, and exactly 32 rows in some device's block.
All inputs are finite; a program needn't handle non-finite values.
Results may differ from a plain program's by a relative error of at most 0.00002.
Values sent between devices are 32-bit elements; how exact they have to be, the bound alone decides.
No kernel may reach another device: no remote copies, remote signals or barrier semaphores. Data moves between devices by JAX's collectives and lax.ppermute only.
A program may use at most 64 MiB of HBM per device.

v0:
```python
import jax
import jax.numpy as jnp
from jax import lax
from jax.sharding import PartitionSpec as P

STEPS = 4
FREQS = 4


COURANT = 0.5


def from_behind(block, axis, distance):
    devices = range(lax.axis_size(axis))
    route = [(i - distance, i) for i in devices if i - distance in devices]
    return lax.ppermute(block, axis, route)


def lookup(material, table):
    total = jnp.zeros(material.shape, jnp.float32)
    for species in range(4):
        total = total + jnp.where(material == species, table[species], jnp.float32(0.0))
    return total[..., None]


def ahead(field, axis, border):
    inner = lax.slice_in_dim(field, 1, field.shape[axis], axis=axis)
    return jnp.concatenate([inner, border], axis=axis)


def behind(field, axis, border):
    inner = lax.slice_in_dim(field, 0, field.shape[axis] - 1, axis=axis)
    return jnp.concatenate([border, inner], axis=axis)


def curl_ahead(fields, upper_z, upper_x):
    border = jnp.zeros(fields.shape[1:3] + (1,), jnp.float32)
    first, second, third = (fields[0], fields[1], fields[2])
    return jnp.stack(
        [
            ahead(third, 2, border) - third - (ahead(second, 0, upper_z[1]) - second),
            ahead(first, 0, upper_z[0]) - first - (ahead(third, 1, upper_x[1]) - third),
            ahead(second, 1, upper_x[0]) - second - (ahead(first, 2, border) - first),
        ]
    )


def curl_behind(fields, lower_z, lower_x):
    border = jnp.zeros(fields.shape[1:3] + (1,), jnp.float32)
    first, second, third = (fields[0], fields[1], fields[2])
    return jnp.stack(
        [
            third - behind(third, 2, border) - (second - behind(second, 0, lower_z[1])),
            first - behind(first, 0, lower_z[0]) - (third - behind(third, 1, lower_x[1])),
            second - behind(second, 1, lower_x[0]) - (first - behind(first, 2, border)),
        ]
    )


def polar_step(current, previous, driver, params):
    resonance = params[0]
    damper = params[1]
    strength = params[2]
    return (
        (2.0 - resonance * resonance) * current
        - (1.0 - 0.5 * damper) * previous
        + strength * resonance * resonance * driver
    ) / (1.0 + 0.5 * damper)


def on_device(e_field, h_field, polar, material, eps_table, loss_table, lorentz, freqs):
    damping = lookup(material, loss_table)
    permittivity = lookup(material, eps_table)
    retain = (1.0 - damping) / (1.0 + damping)
    h_gain = COURANT / (1.0 + damping)
    e_gain = COURANT / (permittivity * (1.0 + damping))
    active = (material == 3)[..., None]
    current = polar[0]
    previous = polar[1]
    middle = e_field.shape[1] // 2
    spectrum = jnp.zeros((FREQS, 2, 3, 1) + e_field.shape[2:], jnp.float32)
    for step in range(STEPS):
        upper_z = from_behind(e_field[0:2, 0:1], "grp", -1)
        upper_x = from_behind(e_field[1:3, :, 0:1], "dev", -1)
        h_field = retain * h_field - h_gain * curl_ahead(e_field, upper_z, upper_x)
        updated = jnp.where(active, polar_step(current, previous, e_field, lorentz), current)
        previous = jnp.where(active, current, previous)
        lower_z = from_behind(h_field[0:2, -1:], "grp", 1)
        lower_x = from_behind(h_field[1:3, :, -1:], "dev", 1)
        e_field = (
            retain * e_field
            + e_gain * curl_behind(h_field, lower_z, lower_x)
            - (updated - current) / permittivity
        )
        current = updated
        angles = freqs * float(step + 1)
        weights = jnp.stack([jnp.cos(angles), -jnp.sin(angles)], axis=1)
        monitor = e_field[:, middle : middle + 1]
        spectrum = spectrum + weights[:, :, None, None, None, None] * monitor[None, None]
    return (e_field, h_field, jnp.stack([current, previous]), spectrum)


def solution(mesh):
    placed = (
        P(None, "grp", "dev", None),
        P(None, "grp", "dev", None),
        P(None, None, "grp", "dev", None),
        P("grp", "dev"),
        P(),
        P(),
        P(),
        P(),
    )
    return jax.shard_map(
        on_device,
        mesh=mesh,
        in_specs=placed,
        out_specs=(
            P(None, "grp", "dev", None),
            P(None, "grp", "dev", None),
            P(None, None, "grp", "dev", None),
            P(None, None, None, "grp", "dev", None),
        ),
        check_vma=False,
    )
```

profile of v0, /device:TPU:262, one launch (start us, length us, event | category | flops | bytes accessed | tf_op | source)
XLA Modules:
  0.0 113.8 jit_solution(13425340818719346765)
XLA Ops:
  0.6 1.0 slice.487
  1.6 4.7 %collective-permute-start.1 = (f32[2,8,1,640]{3,2,1,0:T(1,128)S(1)}, f32[2,8,1,640]{3,2,1,0:T(1,128)S(1)}, u32[]{:S(2)}, u32[]{:S(2)}) collective-permute-start(f32[2,8,1,640]{3,2,1,0:T(1,128)S(1)} %slice.487), channel_id=1, source_target_pairs={{1,0},{2,1},{3,2},{4,3},{5,4},{6,5},{7,6},{8,7},{9,8},{10,9},{11,1... | collective-permute-start | bytes 122888 | tf_op jit(solution)/shard_map/ppermute | solution.py:16
  7.1 2.7 %collective-permute-start = (f32[2,1,8,640]{3,2,1,0:T(8,128)S(1)}, f32[2,1,8,640]{3,2,1,0:T(8,128)S(1)}, u32[]{:S(2)}, u32[]{:S(2)}) collective-permute-start(f32[2,1,8,640]{3,2,1,0:T(8,128)S(1)} %slice.480), channel_id=1, source_target_pairs={{64,0},{128,64},{192,128},{256,192},{320,256},{384,320},{448,384},... | collective-permute-start | bytes 122888 | tf_op jit(solution)/shard_map/ppermute | solution.py:16
  9.8 0.9 slice_bitcast_fusion.31
  10.8 1.0 slice_bitcast_fusion.39
  13.9 5.0 %multiply_divide_fusion = (f32[8,8]{1,0:T(8,128)S(1)}, f32[8,8]{1,0:T(8,128)S(1)}, pred[8,8]{1,0:T(8,128)(4,1)S(1)}, pred[8,8]{1,0:T(8,128)(4,1)S(1)}, pred[8,8]{1,0:T(8,128)(4,1)S(1)}, /*index=5*/pred[8,8]{1,0:T(8,128)(4,1)S(1)}) fusion(f32[]{:T(128)} %bitcast.3, f32[]{:T(128)} %bitcast.2, f32[]{:T(128)} %bitcast.1, f32[]{:T(128)} %bitcast, f32[]{:T(128)} %bitcast.7, ...), kind=kLoop, calls=%fused_computation.170 | loop fusion | flops 1344 | bytes 1056 | tf_op jit(solution)/shard_map/div | solution.py:76
  19.0 2.5 %subtract_divide_fusion = (f32[8,8]{1,0:T(8,128)S(1)}, f32[8,8]{1,0:T(8,128)S(1)}) fusion(pred[8,8]{1,0:T(8,128)(4,1)S(1)} %get-tuple-element.17, f32[]{:T(128)} %bitcast.3, pred[8,8]{1,0:T(8,128)(4,1)S(1)} %get-tuple-element.16, f32[]{:T(128)} %bitcast.2, pred[8,8]{1,0:T(8,128)(4,1)S(1)} %get-tuple-element.15, f32[]{:T(128)} %bitcast.1, ...), kind=kLoop, calls=%fused_computation.172 | loop fusion | flops 704 | bytes 784 | tf_op jit(solution)/shard_map/div | solution.py:74
  26.3 0.9 copy-done.3
  27.4 5.2 %collective-permute-start.2 = (f32[2,1,8,640]{3,2,1,0:T(8,128)S(1)}, f32[2,1,8,640]{3,2,1,0:T(8,128)S(1)}, u32[]{:S(2)}, u32[]{:S(2)}) collective-permute-start(f32[2,1,8,640]{3,2,1,0:T(8,128)S(1)} %slice.624), channel_id=1, source_target_pairs={{0,64},{64,128},{128,192},{192,256},{256,320},{320,384},{384,448},... | collective-permute-start | bytes 122888 | tf_op jit(solution)/shard_map/ppermute | solution.py:16
  32.7 1.9 %collective-permute-start.3 = (f32[2,8,1,640]{3,2,1,0:T(1,128)S(1)}, f32[2,8,1,640]{3,2,1,0:T(1,128)S(1)}, u32[]{:S(2)}, u32[]{:S(2)}) collective-permute-start(f32[2,8,1,640]{3,2,1,0:T(1,128)S(1)} %slice.630), channel_id=1, source_target_pairs={{0,1},{1,2},{2,3},{3,4},{4,5},{5,6},{6,7},{7,8},{8,9},{9,10},{10,1... | collective-permute-start | bytes 122888 | tf_op jit(solution)/shard_map/ppermute | solution.py:16
  34.7 7.6 %collective-permute-done.3 = f32[2,8,1,640]{3,2,1,0:T(1,128)S(1)} collective-permute-done((f32[2,8,1,640]{3,2,1,0:T(1,128)S(1)}, f32[2,8,1,640]{3,2,1,0:T(1,128)S(1)}, u32[]{:S(2)}, u32[]{:S(2)}) %collective-permute-start.3) | collective-permute-done | bytes 40992 | tf_op jit(solution)/shard_map/ppermute | solution.py:16
  42.5 1.0 copy-done
  43.9 1.9 %collective-permute-start.4 = (f32[2,1,8,640]{3,2,1,0:T(8,128)S(1)}, f32[2,1,8,640]{3,2,1,0:T(8,128)S(1)}, u32[]{:S(2)}, u32[]{:S(2)}) collective-permute-start(f32[2,1,8,640]{3,2,1,0:T(8,128)S(1)} %slice.639), channel_id=1, source_target_pairs={{64,0},{128,64},{192,128},{256,192},{320,256},{384,320},{448,384},... | collective-permute-start | bytes 122888 | tf_op jit(solution)/shard_map/ppermute | solution.py:16
  46.0 1.9 %collective-permute-start.5 = (f32[2,8,1,640]{3,2,1,0:T(1,128)S(1)}, f32[2,8,1,640]{3,2,1,0:T(1,128)S(1)}, u32[]{:S(2)}, u32[]{:S(2)}) collective-permute-start(f32[2,8,1,640]{3,2,1,0:T(1,128)S(1)} %slice.646), channel_id=1, source_target_pairs={{1,0},{2,1},{3,2},{4,3},{5,4},{6,5},{7,6},{8,7},{9,8},{10,9},{11,1... | collective-permute-start | bytes 122888 | tf_op jit(solution)/shard_map/ppermute | solution.py:16
  47.9 4.0 %collective-permute-done.4 = f32[2,1,8,640]{3,2,1,0:T(8,128)S(1)} collective-permute-done((f32[2,1,8,640]{3,2,1,0:T(8,128)S(1)}, f32[2,1,8,640]{3,2,1,0:T(8,128)S(1)}, u32[]{:S(2)}, u32[]{:S(2)}) %collective-permute-start.4) | collective-permute-done | bytes 40992 | tf_op jit(solution)/shard_map/ppermute | solution.py:16
  52.4 3.7 %collective-permute-start.6 = (f32[2,1,8,640]{3,2,1,0:T(8,128)S(1)}, f32[2,1,8,640]{3,2,1,0:T(8,128)S(1)}, u32[]{:S(2)}, u32[]{:S(2)}) collective-permute-start(f32[2,1,8,640]{3,2,1,0:T(8,128)S(1)} %slice.654), channel_id=1, source_target_pairs={{0,64},{64,128},{128,192},{192,256},{256,320},{320,384},{384,448},... | collective-permute-start | bytes 122888 | tf_op jit(solution)/shard_map/ppermute | solution.py:16
  56.2 1.9 %collective-permute-start.7 = (f32[2,8,1,640]{3,2,1,0:T(1,128)S(1)}, f32[2,8,1,640]{3,2,1,0:T(1,128)S(1)}, u32[]{:S(2)}, u32[]{:S(2)}) collective-permute-start(f32[2,8,1,640]{3,2,1,0:T(1,128)S(1)} %slice.660), channel_id=1, source_target_pairs={{0,1},{1,2},{2,3},{3,4},{4,5},{5,6},{6,7},{7,8},{8,9},{9,10},{10,1... | collective-permute-start | bytes 122888 | tf_op jit(solution)/shard_map/ppermute | solution.py:16
  58.3 7.4 %collective-permute-done.7 = f32[2,8,1,640]{3,2,1,0:T(1,128)S(1)} collective-permute-done((f32[2,8,1,640]{3,2,1,0:T(1,128)S(1)}, f32[2,8,1,640]{3,2,1,0:T(1,128)S(1)}, u32[]{:S(2)}, u32[]{:S(2)}) %collective-permute-start.7) | collective-permute-done | bytes 40992 | tf_op jit(solution)/shard_map/ppermute | solution.py:16
  66.4 2.1 %collective-permute-start.8 = (f32[2,1,8,640]{3,2,1,0:T(8,128)S(1)}, f32[2,1,8,640]{3,2,1,0:T(8,128)S(1)}, u32[]{:S(2)}, u32[]{:S(2)}) collective-permute-start(f32[2,1,8,640]{3,2,1,0:T(8,128)S(1)} %slice.669), channel_id=1, source_target_pairs={{64,0},{128,64},{192,128},{256,192},{320,256},{384,320},{448,384},... | collective-permute-start | bytes 122888 | tf_op jit(solution)/shard_map/ppermute | solution.py:16
  68.7 1.9 %collective-permute-start.9 = (f32[2,8,1,640]{3,2,1,0:T(1,128)S(1)}, f32[2,8,1,640]{3,2,1,0:T(1,128)S(1)}, u32[]{:S(2)}, u32[]{:S(2)}) collective-permute-start(f32[2,8,1,640]{3,2,1,0:T(1,128)S(1)} %slice.676), channel_id=1, source_target_pairs={{1,0},{2,1},{3,2},{4,3},{5,4},{6,5},{7,6},{8,7},{9,8},{10,9},{11,1... | collective-permute-start | bytes 122888 | tf_op jit(solution)/shard_map/ppermute | solution.py:16
  70.7 3.8 %collective-permute-done.8 = f32[2,1,8,640]{3,2,1,0:T(8,128)S(1)} collective-permute-done((f32[2,1,8,640]{3,2,1,0:T(8,128)S(1)}, f32[2,1,8,640]{3,2,1,0:T(8,128)S(1)}, u32[]{:S(2)}, u32[]{:S(2)}) %collective-permute-start.8) | collective-permute-done | bytes 40992 | tf_op jit(solution)/shard_map/ppermute | solution.py:16
  75.0 3.7 %collective-permute-start.10 = (f32[2,1,8,640]{3,2,1,0:T(8,128)S(1)}, f32[2,1,8,640]{3,2,1,0:T(8,128)S(1)}, u32[]{:S(2)}, u32[]{:S(2)}) collective-permute-start(f32[2,1,8,640]{3,2,1,0:T(8,128)S(1)} %slice.684), channel_id=1, source_target_pairs={{0,64},{64,128},{128,192},{192,256},{256,320},{320,384},{384,448},... | collective-permute-start | bytes 122888 | tf_op jit(solution)/shard_map/ppermute | solution.py:16
  78.8 1.9 %collective-permute-start.11 = (f32[2,8,1,640]{3,2,1,0:T(1,128)S(1)}, f32[2,8,1,640]{3,2,1,0:T(1,128)S(1)}, u32[]{:S(2)}, u32[]{:S(2)}) collective-permute-start(f32[2,8,1,640]{3,2,1,0:T(1,128)S(1)} %slice.690), channel_id=1, source_target_pairs={{0,1},{1,2},{2,3},{3,4},{4,5},{5,6},{6,7},{7,8},{8,9},{9,10},{10,1... | collective-permute-start | bytes 122888 | tf_op jit(solution)/shard_map/ppermute | solution.py:16
  80.9 7.4 %collective-permute-done.11 = f32[2,8,1,640]{3,2,1,0:T(1,128)S(1)} collective-permute-done((f32[2,8,1,640]{3,2,1,0:T(1,128)S(1)}, f32[2,8,1,640]{3,2,1,0:T(1,128)S(1)}, u32[]{:S(2)}, u32[]{:S(2)}) %collective-permute-start.11) | collective-permute-done | bytes 40992 | tf_op jit(solution)/shard_map/ppermute | solution.py:16
  89.1 2.1 %collective-permute-start.12 = (f32[2,1,8,640]{3,2,1,0:T(8,128)S(1)}, f32[2,1,8,640]{3,2,1,0:T(8,128)S(1)}, u32[]{:S(2)}, u32[]{:S(2)}) collective-permute-start(f32[2,1,8,640]{3,2,1,0:T(8,128)S(1)} %slice.699), channel_id=1, source_target_pairs={{64,0},{128,64},{192,128},{256,192},{320,256},{384,320},{448,384},... | collective-permute-start | bytes 122888 | tf_op jit(solution)/shard_map/ppermute | solution.py:16
  91.4 1.9 %collective-permute-start.13 = (f32[2,8,1,640]{3,2,1,0:T(1,128)S(1)}, f32[2,8,1,640]{3,2,1,0:T(1,128)S(1)}, u32[]{:S(2)}, u32[]{:S(2)}) collective-permute-start(f32[2,8,1,640]{3,2,1,0:T(1,128)S(1)} %slice.706), channel_id=1, source_target_pairs={{1,0},{2,1},{3,2},{4,3},{5,4},{6,5},{7,6},{8,7},{9,8},{10,9},{11,1... | collective-permute-start | bytes 122888 | tf_op jit(solution)/shard_map/ppermute | solution.py:16
  93.4 3.8 %collective-permute-done.12 = f32[2,1,8,640]{3,2,1,0:T(8,128)S(1)} collective-permute-done((f32[2,1,8,640]{3,2,1,0:T(8,128)S(1)}, f32[2,1,8,640]{3,2,1,0:T(8,128)S(1)}, u32[]{:S(2)}, u32[]{:S(2)}) %collective-permute-start.12) | collective-permute-done | bytes 40992 | tf_op jit(solution)/shard_map/ppermute | solution.py:16
  97.7 3.7 %collective-permute-start.14 = (f32[2,1,8,640]{3,2,1,0:T(8,128)S(1)}, f32[2,1,8,640]{3,2,1,0:T(8,128)S(1)}, u32[]{:S(2)}, u32[]{:S(2)}) collective-permute-start(f32[2,1,8,640]{3,2,1,0:T(8,128)S(1)} %slice.714), channel_id=1, source_target_pairs={{0,64},{64,128},{128,192},{192,256},{256,320},{320,384},{384,448},... | collective-permute-start | bytes 122888 | tf_op jit(solution)/shard_map/ppermute | solution.py:16
  101.6 1.9 %collective-permute-start.15 = (f32[2,8,1,640]{3,2,1,0:T(1,128)S(1)}, f32[2,8,1,640]{3,2,1,0:T(1,128)S(1)}, u32[]{:S(2)}, u32[]{:S(2)}) collective-permute-start(f32[2,8,1,640]{3,2,1,0:T(1,128)S(1)} %slice.720), channel_id=1, source_target_pairs={{0,1},{1,2},{2,3},{3,4},{4,5},{5,6},{6,7},{7,8},{8,9},{9,10},{10,1... | collective-permute-start | bytes 122888 | tf_op jit(solution)/shard_map/ppermute | solution.py:16
  103.7 7.4 %collective-permute-done.15 = f32[2,8,1,640]{3,2,1,0:T(1,128)S(1)} collective-permute-done((f32[2,8,1,640]{3,2,1,0:T(1,128)S(1)}, f32[2,8,1,640]{3,2,1,0:T(1,128)S(1)}, u32[]{:S(2)}, u32[]{:S(2)}) %collective-permute-start.15) | collective-permute-done | bytes 40992 | tf_op jit(solution)/shard_map/ppermute | solution.py:16
  111.7 1.1 pad_maximum_fusion
  112.8 1.0 multiply_add_fusion
  (130 shorter events, 9.1 us)
Async XLA Ops:
  1.6 24.3 %collective-permute-start.1 = (f32[2,8,1,640]{3,2,1,0:T(1,128)S(1)}, f32[2,8,1,640]{3,2,1,0:T(1,128)S(1)}, u32[]{:S(2)}, u32[]{:S(2)}) collective-permute-start(f32[2,8,1,640]{3,2,1,0:T(1,128)S(1)} %slice.487), channel_id=1, source_target_pairs={{1,0},{2,1},{3,2},{4,3},{5,4},{6,5},{7,6},{8,7},{9,8},{10,9},{11,1... | collective-permute-start | bytes 122888 | tf_op jit(solution)/shard_map/ppermute | solution.py:16
  7.1 18.8 %collective-permute-start = (f32[2,1,8,640]{3,2,1,0:T(8,128)S(1)}, f32[2,1,8,640]{3,2,1,0:T(8,128)S(1)}, u32[]{:S(2)}, u32[]{:S(2)}) collective-permute-start(f32[2,1,8,640]{3,2,1,0:T(8,128)S(1)} %slice.480), channel_id=1, source_target_pairs={{64,0},{128,64},{192,128},{256,192},{320,256},{384,320},{448,384},... | collective-permute-start | bytes 122888 | tf_op jit(solution)/shard_map/ppermute | solution.py:16
  10.8 1.1 copy-start.7
  10.8 1.7 %copy-start.5 = (f32[4]{0:T(128)S(1)}, f32[4]{0:T(128)}, u32[]{:S(2)}) copy-start(f32[4]{0:T(128)} %param.12) | copy-start | bytes 52
  10.8 2.3 %copy-start.6 = (f32[4]{0:T(128)S(1)}, f32[4]{0:T(128)}, u32[]{:S(2)}) copy-start(f32[4]{0:T(128)} %param.13) | copy-start | bytes 52
  10.8 3.0 %copy-start.9 = (f32[4]{0:T(128)S(1)}, f32[4]{0:T(128)}, u32[]{:S(2)}) copy-start(f32[4]{0:T(128)} %param.15) | copy-start | bytes 52
  10.8 3.1 %copy-start.8 = (s32[8,8]{1,0:T(8,128)S(1)}, s32[8,8]{1,0:T(8,128)}, u32[]{:S(2)}) copy-start(s32[8,8]{1,0:T(8,128)} %param.11) | copy-start | bytes 772
  11.9 14.1 %copy-start.1 = (f32[3,8,8,640]{3,2,1,0:T(8,128)S(1)}, f32[3,8,8,640]{3,2,1,0:T(8,128)}, u32[]{:S(2)}) copy-start(f32[3,8,8,640]{3,2,1,0:T(8,128)} %param.8) | copy-start | bytes 1474564
  26.2 1.0 copy-start.3
  27.4 7.2 %collective-permute-start.2 = (f32[2,1,8,640]{3,2,1,0:T(8,128)S(1)}, f32[2,1,8,640]{3,2,1,0:T(8,128)S(1)}, u32[]{:S(2)}, u32[]{:S(2)}) collective-permute-start(f32[2,1,8,640]{3,2,1,0:T(8,128)S(1)} %slice.624), channel_id=1, source_target_pairs={{0,64},{64,128},{128,192},{192,256},{256,320},{320,384},{384,448},... | collective-permute-start | bytes 122888 | tf_op jit(solution)/shard_map/ppermute | solution.py:16
  32.7 9.5 %collective-permute-start.3 = (f32[2,8,1,640]{3,2,1,0:T(1,128)S(1)}, f32[2,8,1,640]{3,2,1,0:T(1,128)S(1)}, u32[]{:S(2)}, u32[]{:S(2)}) collective-permute-start(f32[2,8,1,640]{3,2,1,0:T(1,128)S(1)} %slice.630), channel_id=1, source_target_pairs={{0,1},{1,2},{2,3},{3,4},{4,5},{5,6},{6,7},{7,8},{8,9},{9,10},{10,1... | collective-permute-start | bytes 122888 | tf_op jit(solution)/shard_map/ppermute | solution.py:16
  42.3 1.2 %copy-start = (f32[2,3,8,8,640]{4,3,2,1,0:T(8,128)S(1)}, f32[2,3,8,8,640]{4,3,2,1,0:T(8,128)}, u32[]{:S(2)}) copy-start(f32[2,3,8,8,640]{4,3,2,1,0:T(8,128)} %param.10) | copy-start | bytes 2949124
  43.9 8.0 %collective-permute-start.4 = (f32[2,1,8,640]{3,2,1,0:T(8,128)S(1)}, f32[2,1,8,640]{3,2,1,0:T(8,128)S(1)}, u32[]{:S(2)}, u32[]{:S(2)}) collective-permute-start(f32[2,1,8,640]{3,2,1,0:T(8,128)S(1)} %slice.639), channel_id=1, source_target_pairs={{64,0},{128,64},{192,128},{256,192},{320,256},{384,320},{448,384},... | collective-permute-start | bytes 122888 | tf_op jit(solution)/shard_map/ppermute | solution.py:16
  46.0 5.9 %collective-permute-start.5 = (f32[2,8,1,640]{3,2,1,0:T(1,128)S(1)}, f32[2,8,1,640]{3,2,1,0:T(1,128)S(1)}, u32[]{:S(2)}, u32[]{:S(2)}) collective-permute-start(f32[2,8,1,640]{3,2,1,0:T(1,128)S(1)} %slice.646), channel_id=1, source_target_pairs={{1,0},{2,1},{3,2},{4,3},{5,4},{6,5},{7,6},{8,7},{9,8},{10,9},{11,1... | collective-permute-start | bytes 122888 | tf_op jit(solution)/shard_map/ppermute | solution.py:16
  52.4 5.9 %collective-permute-start.6 = (f32[2,1,8,640]{3,2,1,0:T(8,128)S(1)}, f32[2,1,8,640]{3,2,1,0:T(8,128)S(1)}, u32[]{:S(2)}, u32[]{:S(2)}) collective-permute-start(f32[2,1,8,640]{3,2,1,0:T(8,128)S(1)} %slice.654), channel_id=1, source_target_pairs={{0,64},{64,128},{128,192},{192,256},{256,320},{320,384},{384,448},... | collective-permute-start | bytes 122888 | tf_op jit(solution)/shard_map/ppermute | solution.py:16
  56.2 9.5 %collective-permute-start.7 = (f32[2,8,1,640]{3,2,1,0:T(1,128)S(1)}, f32[2,8,1,640]{3,2,1,0:T(1,128)S(1)}, u32[]{:S(2)}, u32[]{:S(2)}) collective-permute-start(f32[2,8,1,640]{3,2,1,0:T(1,128)S(1)} %slice.660), channel_id=1, source_target_pairs={{0,1},{1,2},{2,3},{3,4},{4,5},{5,6},{6,7},{7,8},{8,9},{9,10},{10,1... | collective-permute-start | bytes 122888 | tf_op jit(solution)/shard_map/ppermute | solution.py:16
  66.4 8.0 %collective-permute-start.8 = (f32[2,1,8,640]{3,2,1,0:T(8,128)S(1)}, f32[2,1,8,640]{3,2,1,0:T(8,128)S(1)}, u32[]{:S(2)}, u32[]{:S(2)}) collective-permute-start(f32[2,1,8,640]{3,2,1,0:T(8,128)S(1)} %slice.669), channel_id=1, source_target_pairs={{64,0},{128,64},{192,128},{256,192},{320,256},{384,320},{448,384},... | collective-permute-start | bytes 122888 | tf_op jit(solution)/shard_map/ppermute | solution.py:16
  68.7 5.7 %collective-permute-start.9 = (f32[2,8,1,640]{3,2,1,0:T(1,128)S(1)}, f32[2,8,1,640]{3,2,1,0:T(1,128)S(1)}, u32[]{:S(2)}, u32[]{:S(2)}) collective-permute-start(f32[2,8,1,640]{3,2,1,0:T(1,128)S(1)} %slice.676), channel_id=1, source_target_pairs={{1,0},{2,1},{3,2},{4,3},{5,4},{6,5},{7,6},{8,7},{9,8},{10,9},{11,1... | collective-permute-start | bytes 122888 | tf_op jit(solution)/shard_map/ppermute | solution.py:16
  75.0 5.9 %collective-permute-start.10 = (f32[2,1,8,640]{3,2,1,0:T(8,128)S(1)}, f32[2,1,8,640]{3,2,1,0:T(8,128)S(1)}, u32[]{:S(2)}, u32[]{:S(2)}) collective-permute-start(f32[2,1,8,640]{3,2,1,0:T(8,128)S(1)} %slice.684), channel_id=1, source_target_pairs={{0,64},{64,128},{128,192},{192,256},{256,320},{320,384},{384,448},... | collective-permute-start | bytes 122888 | tf_op jit(solution)/shard_map/ppermute | solution.py:16
  78.8 9.5 %collective-permute-start.11 = (f32[2,8,1,640]{3,2,1,0:T(1,128)S(1)}, f32[2,8,1,640]{3,2,1,0:T(1,128)S(1)}, u32[]{:S(2)}, u32[]{:S(2)}) collective-permute-start(f32[2,8,1,640]{3,2,1,0:T(1,128)S(1)} %slice.690), channel_id=1, source_target_pairs={{0,1},{1,2},{2,3},{3,4},{4,5},{5,6},{6,7},{7,8},{8,9},{9,10},{10,1... | collective-permute-start | bytes 122888 | tf_op jit(solution)/shard_map/ppermute | solution.py:16
  89.1 8.0 %collective-permute-start.12 = (f32[2,1,8,640]{3,2,1,0:T(8,128)S(1)}, f32[2,1,8,640]{3,2,1,0:T(8,128)S(1)}, u32[]{:S(2)}, u32[]{:S(2)}) collective-permute-start(f32[2,1,8,640]{3,2,1,0:T(8,128)S(1)} %slice.699), channel_id=1, source_target_pairs={{64,0},{128,64},{192,128},{256,192},{320,256},{384,320},{448,384},... | collective-permute-start | bytes 122888 | tf_op jit(solution)/shard_map/ppermute | solution.py:16
  91.4 5.7 %collective-permute-start.13 = (f32[2,8,1,640]{3,2,1,0:T(1,128)S(1)}, f32[2,8,1,640]{3,2,1,0:T(1,128)S(1)}, u32[]{:S(2)}, u32[]{:S(2)}) collective-permute-start(f32[2,8,1,640]{3,2,1,0:T(1,128)S(1)} %slice.706), channel_id=1, source_target_pairs={{1,0},{2,1},{3,2},{4,3},{5,4},{6,5},{7,6},{8,7},{9,8},{10,9},{11,1... | collective-permute-start | bytes 122888 | tf_op jit(solution)/shard_map/ppermute | solution.py:16
  97.7 13.5 %copy-start.2 = (f32[3,8,8,640]{3,2,1,0:T(8,128)}, f32[3,8,8,640]{3,2,1,0:T(8,128)S(1)}, u32[]{:S(2)}) copy-start(f32[3,8,8,640]{3,2,1,0:T(8,128)S(1)} %fusion.9) | copy-start | bytes 1474564
  97.7 5.9 %collective-permute-start.14 = (f32[2,1,8,640]{3,2,1,0:T(8,128)S(1)}, f32[2,1,8,640]{3,2,1,0:T(8,128)S(1)}, u32[]{:S(2)}, u32[]{:S(2)}) collective-permute-start(f32[2,1,8,640]{3,2,1,0:T(8,128)S(1)} %slice.714), channel_id=1, source_target_pairs={{0,64},{64,128},{128,192},{192,256},{256,320},{320,384},{384,448},... | collective-permute-start | bytes 122888 | tf_op jit(solution)/shard_map/ppermute | solution.py:16
  101.6 9.5 %collective-permute-start.15 = (f32[2,8,1,640]{3,2,1,0:T(1,128)S(1)}, f32[2,8,1,640]{3,2,1,0:T(1,128)S(1)}, u32[]{:S(2)}, u32[]{:S(2)}) collective-permute-start(f32[2,8,1,640]{3,2,1,0:T(1,128)S(1)} %slice.720), channel_id=1, source_target_pairs={{0,1},{1,2},{2,3},{3,4},{4,5},{5,6},{6,7},{7,8},{8,9},{9,10},{10,1... | collective-permute-start | bytes 122888 | tf_op jit(solution)/shard_map/ppermute | solution.py:16
  111.7 1.1 copy-start.4
where the time goes:
time: 115 us; the launch traced here: 114 us
  starting transfers between devices  43.4 us (38%)
  waiting for transfers between devices  41.9 us (36%)
  other arithmetic  13.5 us (12%)
  local copies, waits for them, and re-layouts  9.63 us (8%)
  between operations  5.36 us (5%)
    ppermute x16, starting transfers between devices, from_behind(): return lax.ppermute(block, axis, route)  43.4 us
    ppermute x16, waiting for transfers between devices, from_behind(): return lax.ppermute(block, axis, route)  41.9 us
    div x1, other arithmetic, on_device(): e_gain = COURANT / (permittivity * (1.0 + damping))  5.05 us
    div x1, other arithmetic, on_device(): retain = (1.0 - damping) / (1.0 + damping)  2.54 us
  transfers between devices with their start and end apart: 16, of which 10 were waited for; matrix products, arithmetic and copies ran while one was open for 12% of the time, Pallas kernels for 0%

commit v1 on v0

v1 whole, which is shorter than its diff:
```python
import functools

import jax
import jax.numpy as jnp
from jax import lax
from jax.experimental import pallas as pl
from jax.experimental.pallas import tpu as pltpu
from jax.sharding import PartitionSpec as P


STEPS = 4
FREQS = 4
COURANT = 0.5
N = 8
NY = 640
LANES = 128

ROWS = 17
Z0 = 5

X_TILES = 13
Z_TILES = 19


def ladder(first, count, start, way):
    return [(first + i, start + way * j) for i in range(count) for j in range(count - i)]


def ray_rows(entries, tile):
    out = {}
    for c in range(2):
        for kind, n, place in entries:
            k = len(out)
            out[(kind, n, c, place)] = (tile + k // 8, k % 8)
    return out


HX = ray_rows([("ze", n, x) for n, x in ladder(0, 3, 0, 1)] + [("zh", n, x) for n, x in ladder(1, 3, 0, 1)], 8)
LX = ray_rows([("ze", n, x) for n, x in ladder(0, 4, 7, -1)] + [("zh", n, x) for n, x in ladder(1, 3, 7, -1)], 8)
HZ = ray_rows(
    [("zeh", n, x) for n, x in ladder(0, 3, 0, 1)]
    + [("zel", n, x) for n, x in ladder(0, 4, 7, -1)]
    + [("xe", n, z) for n, z in ladder(0, 3, 0, 1)]
    + [("xh", n, z) for n, z in ladder(1, 2, 0, 1)]
    + [("xhl", n, z) for n, z in ladder(1, 3, 0, 1)]
    + [("xeh", n, z) for n, z in ladder(0, 3, 0, 1)],
    9,
)
LZ = ray_rows(
    [("zhh", n, x) for n, x in ladder(1, 3, 0, 1)]
    + [("zhl", n, x) for n, x in ladder(1, 3, 7, -1)]
    + [("xe", n, z) for n, z in ladder(0, 3, 7, -1)]
    + [("xh", n, z) for n, z in ladder(1, 3, 7, -1)]
    + [("xhl", n, z) for n, z in ladder(1, 3, 7, -1)]
    + [("xeh", n, z) for n, z in ladder(0, 4, 7, -1)],
    9,
)


def slot_e(n, c):
    return 2 * n + c


def slot_h(n, c):
    return 2 * (n - 1) + c


def wide(tile):
    return jnp.concatenate([tile] * (NY // LANES), axis=1)


def sublane(shape):
    return lax.broadcasted_iota(jnp.int32, shape, 0)


def lane(shape):
    return lax.broadcasted_iota(jnp.int32, shape, 1)


def y_ahead(v):
    r = pltpu.roll(v, NY - 1, 1)
    last = r[:, NY - LANES :]
    return jnp.concatenate([r[:, : NY - LANES], jnp.where(lane(last.shape) == LANES - 1, 0.0, last)], axis=1)


def y_behind(v):
    r = pltpu.roll(v, 1, 1)
    first = r[:, :LANES]
    return jnp.concatenate([jnp.where(lane(first.shape) == 0, 0.0, first), r[:, LANES:]], axis=1)


def x_up(v):
    return pltpu.roll(v, N - 1, 0)


def x_down(v):
    return pltpu.roll(v, 1, 0)


def kind_tables(eps_ref, loss_ref):
    out = []
    for k in range(4):
        damping = jnp.full((N, LANES), loss_ref[k], jnp.float32)
        permittivity = jnp.full((N, LANES), eps_ref[k], jnp.float32)
        scale = 1.0 / (1.0 + damping)
        inverse = 1.0 / permittivity
        out.append(((1.0 - damping) * scale, COURANT * scale, COURANT * scale * inverse, inverse))
    return out


def row_coefficients(kind, tables):
    out = []
    for j in range(4):
        total = jnp.zeros((N, LANES), jnp.float32)
        for k in range(4):
            total = jnp.where(kind == k + 1.0, tables[k][j], total)
        out.append(total)
    out.append(jnp.where(kind == 4.0, 1.0, 0.0))
    return out


def polar_scalars(lorentz_ref):
    shape = (N, LANES)
    a = jnp.full(shape, lorentz_ref[0], jnp.float32)
    g = jnp.full(shape, lorentz_ref[1], jnp.float32)
    s = jnp.full(shape, lorentz_ref[2], jnp.float32)
    scale = 1.0 / (1.0 + 0.5 * g)
    return (1.0 - a * a - 0.5 * g) * scale, (1.0 - 0.5 * g) * scale, s * a * a * scale


def own_kinds(material_ref):
    sub = sublane((N, LANES))
    out = []
    for z in range(N):
        kind = jnp.zeros((N, LANES), jnp.int32)
        for x in range(N):
            kind = jnp.where(sub == x, material_ref[z, x] + 1, kind)
        out.append(kind.astype(jnp.float32))
    return out


def e_update(curl, e, a, b, k, polar):
    retain, _, e_gain, inverse, active = k
    p, q, r = polar
    moved = active * (p * a - q * b + r * e)
    e_new = retain * e + e_gain * curl - inverse * moved
    return e_new, jnp.where(active > 0.5, a + moved, b)


def alone_kernel(
    e_hbm, h_hbm, p_hbm, material, eps, loss, lorentz, m0, m1, ze_out, zh_out, e, h, a, b, msg, ze, zh, coef, sems
):
    par = lax.rem(lax.axis_index("dev"), 2)
    to_high = par
    to_low = 1 - par
    copies = [
        pltpu.make_async_copy(e_hbm, e.at[:, 0:N], sems.at[0]),
        pltpu.make_async_copy(h_hbm, h.at[:, 1 : N + 1], sems.at[1]),
        pltpu.make_async_copy(p_hbm.at[0], a, sems.at[2]),
        pltpu.make_async_copy(p_hbm.at[1], b, sems.at[3]),
    ]
    for copy in copies:
        copy.start()
    none = jnp.zeros((N, NY), jnp.float32)
    for c in range(3):
        e[c, N] = none
        h[c, 0] = none
    tables = kind_tables(eps, loss)
    polar = [wide(v) for v in polar_scalars(lorentz)]
    ln = lane((N, LANES))
    packed = jnp.zeros((N, LANES), jnp.float32)
    for z, kind in enumerate(own_kinds(material)):
        packed = jnp.where(ln == z, kind, packed)
        for j, v in enumerate(row_coefficients(kind, tables)):
            coef[j, z] = v
    for s in range(2):
        msg[s, 12] = wide(packed)
    for copy in copies:
        copy.wait()

    @pl.loop(0, N)
    def _(z):
        for c in range(2):
            msg[to_low, z, pl.ds(slot_e(0, c), 1), :] = e[1 + c, z, 0:1, :]

    for c in range(2):
        ze[slot_e(0, c)] = e[c, 0]
    sub = sublane((N, NY))
    top = sub == N - 1
    bottom = sub == 0

    for n in range(1, STEPS + 1):
        old, new = (a, b) if n % 2 == 1 else (b, a)

        @pl.loop(0, N)
        def _(z):
            k = [wide(coef[j, z]) for j in range(5)]
            retain, h_gain = k[0], k[1]
            ex, ey, ez = (e[c, z] for c in range(3))
            e1x, e1y = (e[c, z + 1] for c in range(2))
            xa_y = jnp.where(top, 0.0, x_up(ey))
            xa_z = jnp.where(top, 0.0, x_up(ez))
            hx = retain * h[0, z + 1] - h_gain * ((y_ahead(ez) - ez) - (e1y - ey))
            hy = retain * h[1, z + 1] - h_gain * ((e1x - ex) - (xa_z - ez))
            hz = retain * h[2, z + 1] - h_gain * ((xa_y - ey) - (y_ahead(ex) - ex))
            h[0, z + 1] = hx
            h[1, z + 1] = hy
            h[2, z + 1] = hz
            msg[to_high, z, pl.ds(slot_h(n, 0), 1), :] = hy[N - 1 : N, :]
            msg[to_high, z, pl.ds(slot_h(n, 1), 1), :] = hz[N - 1 : N, :]
            if n < STEPS:
                lx, ly = (h[c, z] for c in range(2))
                xb_y = jnp.where(bottom, 0.0, x_down(hy))
                xb_z = jnp.where(bottom, 0.0, x_down(hz))
                curls = (
                    (hz - y_behind(hz)) - (hy - ly),
                    (hx - lx) - (hz - xb_z),
                    (hy - xb_y) - (hx - y_behind(hx)),
                )
                for c, (curl, field) in enumerate(zip(curls, (ex, ey, ez))):
                    e_new, p_new = e_update(curl, field, old[c, z], new[c, z], k, polar)
                    e[c, z] = e_new
                    new[c, z] = p_new
                    if c:
                        msg[to_low, z, pl.ds(slot_e(n, c - 1), 1), :] = e_new[0:1, :]

        for c in range(2):
            zh[slot_h(n, c)] = h[c, N]
            if n < STEPS:
                ze[slot_e(n, c)] = e[c, 0]

    for rays, to in ((HX, to_low), (LX, to_high)):
        for (kind, n, c, x), (tile, row) in rays.items():
            source = ze.at[slot_e(n, c)] if kind == "ze" else zh.at[slot_h(n, c)]
            msg[to, tile, row : row + 1, :] = source[x : x + 1, :]
    copies = [
        pltpu.make_async_copy(msg.at[0], m0, sems.at[0]),
        pltpu.make_async_copy(msg.at[1], m1, sems.at[1]),
        pltpu.make_async_copy(ze, ze_out, sems.at[2]),
        pltpu.make_async_copy(zh, zh_out, sems.at[3]),
    ]
    for copy in copies:
        copy.start()
    for copy in copies:
        copy.wait()


def forward_kernel(m0, m1, r0, r1, ze_in, zh_in, q0, q1, own, got, msg, sems):
    par = lax.rem(lax.axis_index("dev"), 2)
    to_high = lax.rem(lax.axis_index("grp"), 2)
    to_low = 1 - to_high
    copies = [
        pltpu.make_async_copy(m0, own.at[0], sems.at[0]),
        pltpu.make_async_copy(m1, own.at[1], sems.at[1]),
        pltpu.make_async_copy(r0, got.at[0], sems.at[2]),
        pltpu.make_async_copy(r1, got.at[1], sems.at[3]),
        pltpu.make_async_copy(ze_in, msg.at[to_low, 0:8], sems.at[4]),
        pltpu.make_async_copy(zh_in, msg.at[to_high, 0:8], sems.at[5]),
    ]
    for copy in copies:
        copy.start()
    for copy in copies:
        copy.wait()
    high, low = got.at[par], got.at[1 - par]
    mine_e, mine_h = own.at[1 - par], own.at[par]
    ghost = jnp.where(sublane((N, LANES)) < 4, high[12, :, 0:LANES], low[12, :, 0:LANES])
    packed = jnp.concatenate([own[0, 12, :, 0:LANES], ghost] + [ghost] * 3, axis=1)
    for s in range(2):
        msg[s, 8] = packed
    for rays, to in ((HZ, to_low), (LZ, to_high)):
        for (kind, n, c, place), (tile, row) in rays.items():
            if kind in ("zeh", "zhh"):
                t, r = HX[(kind[:2], n, c, place)]
                value = high[t, r : r + 1, :]
            elif kind in ("zel", "zhl"):
                t, r = LX[(kind[:2], n, c, place)]
                value = low[t, r : r + 1, :]
            else:
                r = slot_e(n, c) if kind[:2] == "xe" else slot_h(n, c)
                source = {"xe": mine_e, "xh": mine_h, "xeh": high, "xhl": low}[kind]
                value = source[place, r : r + 1, :]
            msg[to, tile, row : row + 1, :] = value
    copies = [
        pltpu.make_async_copy(msg.at[0], q0, sems.at[0]),
        pltpu.make_async_copy(msg.at[1], q1, sems.at[1]),
    ]
    for copy in copies:
        copy.start()
    for copy in copies:
        copy.wait()


def together_kernel(
    e_hbm, h_hbm, p_hbm, r0, r1, g0, g1, material, eps, loss, lorentz, weights,
    e_out, h_out, p_out, s_out,
    e, h, a, b, gx, gz, xe_hi, xe_lo, xh_lo, xh_hi, ze_hi, ze_lo, zh_lo, zh_hi, coef, spectrum, sems,
):
    par = lax.rem(lax.axis_index("dev"), 2)
    gpar = lax.rem(lax.axis_index("grp"), 2)
    mine = pl.ds(Z0, N)
    fields = [
        pltpu.make_async_copy(e_hbm, e.at[:, mine, 0], sems.at[0]),
        pltpu.make_async_copy(h_hbm, h.at[:, mine, 0], sems.at[1]),
        pltpu.make_async_copy(p_hbm.at[0], a.at[:, mine, 0], sems.at[2]),
        pltpu.make_async_copy(p_hbm.at[1], b.at[:, mine, 0], sems.at[3]),
        pltpu.make_async_copy(r0, gx.at[0], sems.at[4]),
        pltpu.make_async_copy(r1, gx.at[1], sems.at[5]),
        pltpu.make_async_copy(g0, gz.at[0], sems.at[6]),
        pltpu.make_async_copy(g1, gz.at[1], sems.at[7]),
    ]
    for copy in fields:
        copy.start()
    none = jnp.zeros((N, NY), jnp.float32)

    @pl.loop(0, ROWS)
    def _(z):
        for field in (e, h, a, b):
            for c in range(3):
                field[c, z, 1] = none
        for table in (xe_hi, xe_lo, xh_lo, xh_hi):
            table[z] = none

    for z in (*range(Z0), *range(Z0 + N, ROWS)):
        for field in (e, h, a, b):
            for c in range(3):
                field[c, z, 0] = none
    for i in range(2 * STEPS):
        ze_hi[i, 1] = none
        zh_lo[i, 1] = none
        ze_lo[i] = none
        zh_hi[i] = none

    tables = kind_tables(eps, loss)
    polar = [wide(v) for v in polar_scalars(lorentz)]
    for z, kind in enumerate(own_kinds(material)):
        for j, v in enumerate(row_coefficients(kind, tables)):
            coef[j, Z0 + z, 0] = v
    for copy in fields:
        copy.wait()

    high, low = gx.at[par], gx.at[1 - par]
    above, below = gz.at[gpar], gz.at[1 - gpar]
    sub = sublane((N, LANES))
    side = jnp.where(sub < 3, high[12, :, 0:LANES], jnp.where(sub > 3, low[12, :, 0:LANES], 0.0))
    for z in range(-4, N + 3):
        if z < 0 or z >= N:
            tile = below[8] if z < 0 else above[8]
            at = z % N
            both = [tile[:, at : at + 1], tile[:, LANES + at : LANES + at + 1]]
        else:
            both = [None, side[:, z : z + 1]]
        for half, column in enumerate(both):
            if column is None:
                continue
            kind = jnp.broadcast_to(column, (N, LANES))
            if half:
                kind = jnp.where(sub == 3, 0.0, kind)
            for j, v in enumerate(row_coefficients(kind, tables)):
                coef[j, Z0 + z, half] = v

    for z in range(N):
        xe_hi[Z0 + z] = high[z]
        xh_lo[Z0 + z] = low[z]
    for i in range(2 * STEPS):
        ze_hi[i, 0] = above[i]
        zh_lo[i, 0] = below[i]
    for source, rays in ((high, HX), (low, LX)):
        for (kind, n, c, x), (tile, row) in rays.items():
            target = ze_lo.at[slot_e(n, c)] if kind == "ze" else zh_hi.at[slot_h(n, c)]
            target[x : x + 1, :] = source[tile, row : row + 1, :]
    for source, rays, origin in ((above, HZ, Z0 + N), (below, LZ, Z0 - N)):
        for (kind, n, c, place), (tile, row) in rays.items():
            value = source[tile, row : row + 1, :]
            if kind[0] == "z":
                target = ze_hi.at[slot_e(n, c), 1] if kind[1] == "e" else zh_lo.at[slot_h(n, c), 1]
                target[place : place + 1, :] = value
            else:
                r = slot_e(n, c) if kind[1] == "e" else slot_h(n, c)
                target = {"xe": xe_lo, "xh": xh_hi, "xeh": xe_hi, "xhl": xh_lo}[kind]
                target[origin + place, r : r + 1, :] = value

    sub = sublane((N, NY))
    top = sub == N - 1
    bottom = sub == 0

    def across(v, shift, edge, s0, s1):
        v0, v1 = shift(v[0]), shift(v[1])
        return jnp.where(edge, v1 + s0, v0), jnp.where(edge, v0 + s1, v1)

    for n in range(1, STEPS + 1):
        old, new = (a, b) if n % 2 == 1 else (b, a)

        @pl.loop(Z0 - (5 - n), Z0 + N + (4 - n))
        def _(z):
            def rows(table, r):
                return [jnp.broadcast_to(table[z, r + c : r + c + 1, :], (N, NY)) for c in range(2)]

            def k_of(j, half):
                return wide(coef[j, z, half])

            ey = [e[1, z, half] for half in range(2)]
            ez = [e[2, z, half] for half in range(2)]
            s0 = rows(xe_hi, slot_e(n - 1, 0))
            s1 = rows(xe_lo, slot_e(n - 1, 0))
            xa_y = across(ey, x_up, top, s0[0], s1[0])
            xa_z = across(ez, x_up, top, s0[1], s1[1])
            for half in range(2):
                retain, h_gain = k_of(0, half), k_of(1, half)
                ex = e[0, z, half]
                e1x, e1y = e[0, z + 1, half], e[1, z + 1, half]
                h[0, z, half] = retain * h[0, z, half] - h_gain * ((y_ahead(ez[half]) - ez[half]) - (e1y - ey[half]))
                h[1, z, half] = retain * h[1, z, half] - h_gain * ((e1x - ex) - (xa_z[half] - ez[half]))
                h[2, z, half] = retain * h[2, z, half] - h_gain * ((xa_y[half] - ey[half]) - (y_ahead(ex) - ex))

            def h_border(half, sx, sy):
                h_gain = k_of(1, half)
                h[0, z, half] = h[0, z, half] + h_gain * sy
                h[1, z, half] = h[1, z, half] - h_gain * sx

            i = slot_e(n - 1, 0)

            @pl.when(z == Z0 + N - 1)
            def _():
                for half in range(2):
                    h_border(half, ze_hi[i, half], ze_hi[i + 1, half])

            @pl.when(z == Z0 - 1)
            def _():
                h_border(1, ze_lo[i], ze_lo[i + 1])

            hy = [h[1, z, half] for half in range(2)]
            hz = [h[2, z, half] for half in range(2)]
            j = slot_h(n, 0)
            s0 = rows(xh_lo, j)
            s1 = rows(xh_hi, j)
            xb_y = across(hy, x_down, bottom, s0[0], s1[0])
            xb_z = across(hz, x_down, bottom, s0[1], s1[1])
            halves = range(2 if n < STEPS else 1)
            for half in halves:
                k = [k_of(m, half) for m in range(5)]
                hx = h[0, z, half]
                lx, ly = h[0, z - 1, half], h[1, z - 1, half]
                curls = (
                    (hz[half] - y_behind(hz[half])) - (hy[half] - ly),
                    (hx - lx) - (hz[half] - xb_z[half]),
                    (hy[half] - xb_y[half]) - (hx - y_behind(hx)),
                )
                for c in range(3):
                    e_new, p_new = e_update(curls[c], e[c, z, half], old[c, z, half], new[c, z, half], k, polar)
                    e[c, z, half] = e_new
                    new[c, z, half] = p_new

            def e_border(half, sx, sy):
                e_gain = k_of(2, half)
                e[0, z, half] = e[0, z, half] + e_gain * sy
                e[1, z, half] = e[1, z, half] - e_gain * sx

            @pl.when(z == Z0)
            def _():
                for half in halves:
                    e_border(half, zh_lo[j, half], zh_lo[j + 1, half])

            @pl.when(z == Z0 + N)
            def _():
                for half in halves[1:]:
                    e_border(half, zh_hi[j], zh_hi[j + 1])

        for f in range(FREQS):
            for q in range(2):
                for c in range(3):
                    term = weights[n - 1, f, q] * e[c, Z0 + N // 2, 0]
                    spectrum[f, q, c, 0] = term if n == 1 else spectrum[f, q, c, 0] + term

    outs = [
        pltpu.make_async_copy(e.at[:, mine, 0], e_out, sems.at[0]),
        pltpu.make_async_copy(h.at[:, mine, 0], h_out, sems.at[1]),
        pltpu.make_async_copy(a.at[:, mine, 0], p_out.at[0], sems.at[2]),
        pltpu.make_async_copy(b.at[:, mine, 0], p_out.at[1], sems.at[3]),
        pltpu.make_async_copy(spectrum, s_out, sems.at[4]),
    ]
    for copy in outs:
        copy.start()
    for copy in outs:
        copy.wait()


ANY = pl.BlockSpec(memory_space=pl.ANY)
SMEM = pl.BlockSpec(memory_space=pltpu.SMEM)


def f32(*shape):
    return jax.ShapeDtypeStruct(shape, jnp.float32)


def vmem(*shape):
    return pltpu.VMEM(shape, jnp.float32)


def params():
    return pltpu.CompilerParams(vmem_limit_bytes=40 * 1024 * 1024)


def swap(block, axis, parity):
    size = lax.axis_size(axis)
    route = []
    for i in range(parity, size - 1, 2):
        route += [(i, i + 1), (i + 1, i)]
    return lax.ppermute(block, axis, route)


def on_device(e_field, h_field, polar, material, eps_table, loss_table, lorentz, freqs):
    plane = (2 * STEPS, N, NY)
    m0, m1, ze, zh = pl.pallas_call(
        alone_kernel,
        out_shape=[f32(X_TILES, N, NY), f32(X_TILES, N, NY), f32(*plane), f32(*plane)],
        in_specs=[ANY] * 3 + [SMEM] * 4,
        out_specs=[ANY] * 4,
        scratch_shapes=[
            vmem(3, N + 1, N, NY), vmem(3, N + 1, N, NY), vmem(3, N, N, NY), vmem(3, N, N, NY),
            vmem(2, X_TILES, N, NY), vmem(*plane), vmem(*plane), vmem(5, N, N, LANES), pltpu.SemaphoreType.DMA((4,)),
        ],
        compiler_params=params(),
        name="alone",
    )(e_field, h_field, polar, material, eps_table, loss_table, lorentz)
    r1 = swap(m1, "dev", 1)
    r0 = swap(m0, "dev", 0)
    q0, q1 = pl.pallas_call(
        forward_kernel,
        out_shape=[f32(Z_TILES, N, NY)] * 2,
        in_specs=[ANY] * 6,
        out_specs=[ANY] * 2,
        scratch_shapes=[vmem(2, X_TILES, N, NY), vmem(2, X_TILES, N, NY), vmem(2, Z_TILES, N, NY), pltpu.SemaphoreType.DMA((6,))],
        compiler_params=params(),
        name="forward",
    )(m0, m1, r0, r1, ze, zh)
    g1 = swap(q1, "grp", 1)
    g0 = swap(q0, "grp", 0)
    angles = freqs * jnp.arange(1, STEPS + 1, dtype=jnp.float32)[:, None]
    weights = jnp.stack([jnp.cos(angles), -jnp.sin(angles)], axis=2)
    fields = [vmem(3, ROWS, 2, N, NY)] * 4
    return tuple(
        pl.pallas_call(
            together_kernel,
            out_shape=[f32(3, N, N, NY), f32(3, N, N, NY), f32(2, 3, N, N, NY), f32(FREQS, 2, 3, 1, N, NY)],
            in_specs=[ANY] * 7 + [SMEM] * 5,
            out_specs=[ANY] * 4,
            scratch_shapes=fields + [vmem(2, X_TILES, N, NY), vmem(2, Z_TILES, N, NY)] + [vmem(ROWS, N, NY)] * 4 + [
                vmem(2 * STEPS, 2, N, NY), vmem(*plane), vmem(2 * STEPS, 2, N, NY), vmem(*plane),
                vmem(5, ROWS, 2, N, LANES), vmem(FREQS, 2, 3, 1, N, NY), pltpu.SemaphoreType.DMA((8,)),
            ],
            compiler_params=params(),
            name="together",
        )(e_field, h_field, polar, r0, r1, g0, g1, material, eps_table, loss_table, lorentz, weights)
    )


def solution(mesh):
    placed = (
        P(None, "grp", "dev", None),
        P(None, "grp", "dev", None),
        P(None, None, "grp", "dev", None),
        P("grp", "dev"),
        P(),
        P(),
        P(),
        P(),
    )
    return jax.shard_map(
        on_device,
        mesh=mesh,
        in_specs=placed,
        out_specs=(
            P(None, "grp", "dev", None),
            P(None, "grp", "dev", None),
            P(None, None, "grp", "dev", None),
            P(None, None, None, "grp", "dev", None),
        ),
        check_vma=False,
    )
```

time: 115 us -> 61.7 us (0.54)
  the two profiles are of different devices: /device:TPU:262 before, /device:TPU:249 now
where the time goes in v1:
time: 61.7 us; the launch traced here: 61.4 us
  Pallas kernels  21.8 us (35%)
  starting transfers between devices  17.2 us (28%)
  waiting for transfers between devices  15.4 us (25%)
  local copies, waits for them, and re-layouts  5.95 us (10%)
  between operations  0.81 us (1%)
    ppermute x4, starting transfers between devices, swap(): return lax.ppermute(block, axis, route)  17.2 us
    ppermute x4, waiting for transfers between devices, swap(): return lax.ppermute(block, axis, route)  15.4 us
    pallas_call x1, Pallas kernels, on_device(): pl.pallas_call(together_kernel, out_shape=[f32(3, N, N, NY), f32(3, N, N,...  13.9 us
    pallas_call x1, Pallas kernels, on_device(): pl.pallas_call(alone_kernel, out_shape=[f32(X_TILES, N, NY), f32(X_TILES,...  6.72 us
    unnamed x30, local copies, waits for them, and re-layouts  5.95 us
  transfers between devices with their start and end apart: 4, of which 3 were waited for; matrix products, arithmetic and copies ran while one was open for 0% of the time, Pallas kernels for 0%

profile of v1, /device:TPU:249, one launch (start us, length us, event | category | flops | bytes accessed | tf_op | source)
XLA Modules:
  0.0 61.4 jit_solution(4685229379802779095)
XLA Ops:
  0.6 0.0 copy-start
  0.6 1.2 %copy-done = f32[2,3,8,8,640]{4,3,2,1,0:T(8,128)S(1)} copy-done((f32[2,3,8,8,640]{4,3,2,1,0:T(8,128)S(1)}, f32[2,3,8,8,640]{4,3,2,1,0:T(8,128)}, u32[]{:S(2)}) %copy-start) | copy-done | bytes 983064
  1.8 1.0 %copy-done.2 = f32[3,8,8,640]{3,2,1,0:T(8,128)S(1)} copy-done((f32[3,8,8,640]{3,2,1,0:T(8,128)S(1)}, f32[3,8,8,640]{3,2,1,0:T(8,128)}, u32[]{:S(2)}) %copy-start.2) | copy-done | bytes 491544
  2.9 1.0 %copy-done.4 = f32[3,8,8,640]{3,2,1,0:T(8,128)S(1)} copy-done((f32[3,8,8,640]{3,2,1,0:T(8,128)S(1)}, f32[3,8,8,640]{3,2,1,0:T(8,128)}, u32[]{:S(2)}) %copy-start.4) | copy-done | bytes 491544
  3.9 0.7 %copy-done.6 = s32[8,8]{1,0:T(8,128)S(1)} copy-done((s32[8,8]{1,0:T(8,128)S(1)}, s32[8,8]{1,0:T(8,128)}, u32[]{:S(2)}) %copy-start.6) | copy-done | bytes 280
  4.6 0.7 %copy-done.8 = f32[4]{0:T(128)S(1)} copy-done((f32[4]{0:T(128)S(1)}, f32[4]{0:T(128)}, u32[]{:S(2)}) %copy-start.8) | copy-done | bytes 40
  5.2 0.7 %copy-done.10 = f32[4]{0:T(128)S(1)} copy-done((f32[4]{0:T(128)S(1)}, f32[4]{0:T(128)}, u32[]{:S(2)}) %copy-start.10) | copy-done | bytes 40
  5.9 0.7 %copy-done.12 = f32[3]{0:T(128)S(1)} copy-done((f32[3]{0:T(128)S(1)}, f32[3]{0:T(128)}, u32[]{:S(2)}) %copy-start.12) | copy-done | bytes 36
  6.6 6.7 %alone.1 = (f32[13,8,640]{2,1,0:T(8,128)S(1)}, f32[13,8,640]{2,1,0:T(8,128)S(1)}, f32[8,8,640]{2,1,0:T(8,128)S(1)}, f32[8,8,640]{2,1,0:T(8,128)S(1)}) custom-call(f32[3,8,8,640]{3,2,1,0:T(8,128)S(1)} %copy-done.2, f32[3,8,8,640]{3,2,1,0:T(8,128)S(1)} %copy-done.4, f32[2,3,8,8,640]{4,3,2,1,0:T(8,128)S(1)} %copy-done, s32[8,8]{1,0:T(8,128)S(1)} %copy-done.6, ...), custom_call_target="tpu_custom_call" | custom-call | tf_op jit(solution)/shard_map/alone/pallas_call | solution.py:513
  13.3 0.0 copy-start.1
  13.3 2.7 %collective-permute-start = (f32[13,8,640]{2,1,0:T(8,128)S(1)}, f32[13,8,640]{2,1,0:T(8,128)S(1)}, u32[]{:S(2)}, u32[]{:S(2)}) collective-permute-start(f32[13,8,640]{2,1,0:T(8,128)S(1)} %get-tuple-element.10.m0), channel_id=1, source_target_pairs={{0,1},{1,0},{2,3},{3,2},{4,5},{5,4},{6,7},{7,6},{8,9},{9,8},{10,11... | collective-permute-start | bytes 798728 | tf_op jit(solution)/shard_map/ppermute | solution.py:508
  16.0 5.3 %collective-permute-start.1 = (f32[13,8,640]{2,1,0:T(8,128)S(1)}, f32[13,8,640]{2,1,0:T(8,128)S(1)}, u32[]{:S(2)}, u32[]{:S(2)}) collective-permute-start(f32[13,8,640]{2,1,0:T(8,128)S(1)} %get-tuple-element.11.m1), channel_id=1, source_target_pairs={{1,2},{2,1},{3,4},{4,3},{5,6},{6,5},{7,8},{8,7},{9,10},{10,9},{11,... | collective-permute-start | bytes 798728 | tf_op jit(solution)/shard_map/ppermute | solution.py:508
  21.4 0.0 collective-permute-done.r0
  21.4 7.9 %collective-permute-done.1.r1 = f32[13,8,640]{2,1,0:T(8,128)S(1)} collective-permute-done((f32[13,8,640]{2,1,0:T(8,128)S(1)}, f32[13,8,640]{2,1,0:T(8,128)S(1)}, u32[]{:S(2)}, u32[]{:S(2)}) %collective-permute-start.1) | collective-permute-done | bytes 266272 | tf_op jit(solution)/shard_map/ppermute | solution.py:508
  29.3 1.1 %forward.1 = (f32[19,8,640]{2,1,0:T(8,128)S(1)}, f32[19,8,640]{2,1,0:T(8,128)S(1)}) custom-call(f32[13,8,640]{2,1,0:T(8,128)S(1)} %get-tuple-element.10.m0, f32[13,8,640]{2,1,0:T(8,128)S(1)} %get-tuple-element.11.m1, f32[13,8,640]{2,1,0:T(8,128)S(1)} %collective-permute-done.r0, f32[13,8,640]{2,1,0:T(8,128)S(1)} %collective-permute-done.1.r1, ...), custom_call_target="tpu_custom_call" | custom-call | tf_op jit(solution)/shard_map/forward/pallas_call | solution.py:527
  30.4 3.1 %collective-permute-start.2 = (f32[19,8,640]{2,1,0:T(8,128)S(1)}, f32[19,8,640]{2,1,0:T(8,128)S(1)}, u32[]{:S(2)}, u32[]{:S(2)}) collective-permute-start(f32[19,8,640]{2,1,0:T(8,128)S(1)} %get-tuple-element.14), channel_id=1, source_target_pairs={{0,64},{64,0},{128,192},{192,128},{256,320},{320,256},{384,448},{4... | collective-permute-start | bytes 1167368 | tf_op jit(solution)/shard_map/ppermute | solution.py:508
  33.5 0.0 copy-start.14
  33.5 6.1 %collective-permute-start.3 = (f32[19,8,640]{2,1,0:T(8,128)S(1)}, f32[19,8,640]{2,1,0:T(8,128)S(1)}, u32[]{:S(2)}, u32[]{:S(2)}) collective-permute-start(f32[19,8,640]{2,1,0:T(8,128)S(1)} %get-tuple-element.15), channel_id=1, source_target_pairs={{64,128},{128,64},{192,256},{256,192},{320,384},{384,320},{65,129}... | collective-permute-start | bytes 1167368 | tf_op jit(solution)/shard_map/ppermute | solution.py:508
  39.6 0.0 copy-done.14
  39.6 0.1 multiply_cosine_fusion
  39.8 0.0 copy-start.7
  39.8 0.0 copy-start.9
  39.8 0.0 copy-start.11
  39.8 0.0 copy-start.13
  39.8 0.1 pad_maximum_fusion.weights
  39.9 2.2 %collective-permute-done.2.g0 = f32[19,8,640]{2,1,0:T(8,128)S(1)} collective-permute-done((f32[19,8,640]{2,1,0:T(8,128)S(1)}, f32[19,8,640]{2,1,0:T(8,128)S(1)}, u32[]{:S(2)}, u32[]{:S(2)}) %collective-permute-start.2) | collective-permute-done | bytes 389152 | tf_op jit(solution)/shard_map/ppermute | solution.py:508
  42.1 5.2 %collective-permute-done.3.g1 = f32[19,8,640]{2,1,0:T(8,128)S(1)} collective-permute-done((f32[19,8,640]{2,1,0:T(8,128)S(1)}, f32[19,8,640]{2,1,0:T(8,128)S(1)}, u32[]{:S(2)}, u32[]{:S(2)}) %collective-permute-start.3) | collective-permute-done | bytes 389152 | tf_op jit(solution)/shard_map/ppermute | solution.py:508
  47.4 0.0 copy-done.7
  47.4 0.0 copy-done.9
  47.4 0.0 copy-done.11
  47.4 0.0 copy-done.13
  47.4 13.9 %together.1 = (f32[3,8,8,640]{3,2,1,0:T(8,128)}, f32[3,8,8,640]{3,2,1,0:T(8,128)}, f32[2,3,8,8,640]{4,3,2,1,0:T(8,128)}, f32[4,2,3,1,8,640]{5,4,3,2,1,0:T(8,128)}) custom-call(f32[3,8,8,640]{3,2,1,0:T(8,128)S(1)} %copy-done.3, f32[3,8,8,640]{3,2,1,0:T(8,128)S(1)} %copy-done.5, f32[2,3,8,8,640]{4,3,2,1,0:T(8,128)S(1)} %copy-done.1, ...), custom_call_target="tpu_custom_call" | custom-call | tf_op jit(solution)/shard_map/together/pallas_call | solution.py:542
  (12 shorter events, 0.0 us)
Async XLA Ops:
  0.6 1.2 %copy-start = (f32[2,3,8,8,640]{4,3,2,1,0:T(8,128)S(1)}, f32[2,3,8,8,640]{4,3,2,1,0:T(8,128)}, u32[]{:S(2)}) copy-start(f32[2,3,8,8,640]{4,3,2,1,0:T(8,128)} %p_hbm.3) | copy-start | bytes 2949124
  1.8 1.0 %copy-start.2 = (f32[3,8,8,640]{3,2,1,0:T(8,128)S(1)}, f32[3,8,8,640]{3,2,1,0:T(8,128)}, u32[]{:S(2)}) copy-start(f32[3,8,8,640]{3,2,1,0:T(8,128)} %e_hbm.3) | copy-start | bytes 1474564
  2.9 1.0 %copy-start.4 = (f32[3,8,8,640]{3,2,1,0:T(8,128)S(1)}, f32[3,8,8,640]{3,2,1,0:T(8,128)}, u32[]{:S(2)}) copy-start(f32[3,8,8,640]{3,2,1,0:T(8,128)} %h_hbm.3) | copy-start | bytes 1474564
  3.9 0.7 %copy-start.6 = (s32[8,8]{1,0:T(8,128)S(1)}, s32[8,8]{1,0:T(8,128)}, u32[]{:S(2)}) copy-start(s32[8,8]{1,0:T(8,128)} %material.3) | copy-start | bytes 772
  4.6 0.7 %copy-start.8 = (f32[4]{0:T(128)S(1)}, f32[4]{0:T(128)}, u32[]{:S(2)}) copy-start(f32[4]{0:T(128)} %eps.3) | copy-start | bytes 52
  5.2 0.7 %copy-start.10 = (f32[4]{0:T(128)S(1)}, f32[4]{0:T(128)}, u32[]{:S(2)}) copy-start(f32[4]{0:T(128)} %loss.3) | copy-start | bytes 52
  5.9 0.7 %copy-start.12 = (f32[3]{0:T(128)S(1)}, f32[3]{0:T(128)}, u32[]{:S(2)}) copy-start(f32[3]{0:T(128)} %lorentz.3) | copy-start | bytes 40
  6.6 40.8 %copy-start.3 = (f32[3,8,8,640]{3,2,1,0:T(8,128)S(1)}, f32[3,8,8,640]{3,2,1,0:T(8,128)}, u32[]{:S(2)}) copy-start(f32[3,8,8,640]{3,2,1,0:T(8,128)} %e_hbm.3) | copy-start | bytes 1474564
  6.6 40.8 %copy-start.5 = (f32[3,8,8,640]{3,2,1,0:T(8,128)S(1)}, f32[3,8,8,640]{3,2,1,0:T(8,128)}, u32[]{:S(2)}) copy-start(f32[3,8,8,640]{3,2,1,0:T(8,128)} %h_hbm.3) | copy-start | bytes 1474564
  13.3 34.1 %copy-start.1 = (f32[2,3,8,8,640]{4,3,2,1,0:T(8,128)S(1)}, f32[2,3,8,8,640]{4,3,2,1,0:T(8,128)}, u32[]{:S(2)}) copy-start(f32[2,3,8,8,640]{4,3,2,1,0:T(8,128)} %p_hbm.3) | copy-start | bytes 2949124
  13.3 8.1 %collective-permute-start = (f32[13,8,640]{2,1,0:T(8,128)S(1)}, f32[13,8,640]{2,1,0:T(8,128)S(1)}, u32[]{:S(2)}, u32[]{:S(2)}) collective-permute-start(f32[13,8,640]{2,1,0:T(8,128)S(1)} %get-tuple-element.10.m0), channel_id=1, source_target_pairs={{0,1},{1,0},{2,3},{3,2},{4,5},{5,4},{6,7},{7,6},{8,9},{9,8},{10,11... | collective-permute-start | bytes 798728 | tf_op jit(solution)/shard_map/ppermute | solution.py:508
  16.0 13.2 %collective-permute-start.1 = (f32[13,8,640]{2,1,0:T(8,128)S(1)}, f32[13,8,640]{2,1,0:T(8,128)S(1)}, u32[]{:S(2)}, u32[]{:S(2)}) collective-permute-start(f32[13,8,640]{2,1,0:T(8,128)S(1)} %get-tuple-element.11.m1), channel_id=1, source_target_pairs={{1,2},{2,1},{3,4},{4,3},{5,6},{6,5},{7,8},{8,7},{9,10},{10,9},{11,... | collective-permute-start | bytes 798728 | tf_op jit(solution)/shard_map/ppermute | solution.py:508
  30.4 11.8 %collective-permute-start.2 = (f32[19,8,640]{2,1,0:T(8,128)S(1)}, f32[19,8,640]{2,1,0:T(8,128)S(1)}, u32[]{:S(2)}, u32[]{:S(2)}) collective-permute-start(f32[19,8,640]{2,1,0:T(8,128)S(1)} %get-tuple-element.14), channel_id=1, source_target_pairs={{0,64},{64,0},{128,192},{192,128},{256,320},{320,256},{384,448},{4... | collective-permute-start | bytes 1167368 | tf_op jit(solution)/shard_map/ppermute | solution.py:508
  33.5 6.1 %copy-start.14 = (f32[4]{0:T(128)S(1)}, f32[4]{0:T(128)}, u32[]{:S(2)}) copy-start(f32[4]{0:T(128)} %param.15) | copy-start | bytes 52
  33.5 13.9 %collective-permute-start.3 = (f32[19,8,640]{2,1,0:T(8,128)S(1)}, f32[19,8,640]{2,1,0:T(8,128)S(1)}, u32[]{:S(2)}, u32[]{:S(2)}) collective-permute-start(f32[19,8,640]{2,1,0:T(8,128)S(1)} %get-tuple-element.15), channel_id=1, source_target_pairs={{64,128},{128,64},{192,256},{256,192},{320,384},{384,320},{65,129}... | collective-permute-start | bytes 1167368 | tf_op jit(solution)/shard_map/ppermute | solution.py:508
  39.8 7.6 %copy-start.7 = (s32[8,8]{1,0:T(8,128)S(1)}, s32[8,8]{1,0:T(8,128)}, u32[]{:S(2)}) copy-start(s32[8,8]{1,0:T(8,128)} %material.3) | copy-start | bytes 772
  39.8 7.6 %copy-start.9 = (f32[4]{0:T(128)S(1)}, f32[4]{0:T(128)}, u32[]{:S(2)}) copy-start(f32[4]{0:T(128)} %eps.3) | copy-start | bytes 52
  39.8 7.6 %copy-start.11 = (f32[4]{0:T(128)S(1)}, f32[4]{0:T(128)}, u32[]{:S(2)}) copy-start(f32[4]{0:T(128)} %loss.3) | copy-start | bytes 52
  39.8 7.6 %copy-start.13 = (f32[3]{0:T(128)S(1)}, f32[3]{0:T(128)}, u32[]{:S(2)}) copy-start(f32[3]{0:T(128)} %lorentz.3) | copy-start | bytes 40

commit v2 on v0

v2 whole, which is shorter than its diff:
```python
import jax
import jax.numpy as jnp
from jax import lax
from jax.experimental import pallas as pl
from jax.experimental.pallas import tpu as pltpu
from jax.sharding import PartitionSpec as P


STEPS = 4
FREQS = 4
COURANT = 0.5
N = 8
NY = 640
LANES = 128

ROWS = 17
Z0 = 5

X_TILES = 13
OWN_TILES = 12
FAR_TILES = 8


def ladder(first, count, start, way):
    return [(first + i, start + way * j) for i in range(count) for j in range(count - i)]


def ray_rows(entries, tile):
    out = {}
    for c in range(2):
        for kind, n, place in entries:
            k = len(out)
            out[(kind, n, c, place)] = (tile + k // 8, k % 8)
    return out


def named(kind, pairs):
    return [(kind, n, place) for n, place in pairs]


HX = ray_rows(named("ze", ladder(0, 3, 0, 1)) + named("zh", ladder(1, 3, 0, 1)), 8)
LX = ray_rows(named("ze", ladder(0, 4, 7, -1)) + named("zh", ladder(1, 3, 7, -1)), 8)
HZ = ray_rows(named("xe", ladder(0, 3, 0, 1)) + named("xh", ladder(1, 2, 0, 1)), 9)
LZ = ray_rows(named("xe", ladder(0, 3, 7, -1)) + named("xh", ladder(1, 3, 7, -1)), 9)
HF = ray_rows(named("xhl", ladder(1, 3, 0, 1)) + named("xeh", ladder(0, 3, 0, 1)), 4)
LF = ray_rows(named("xhl", ladder(1, 3, 7, -1)) + named("xeh", ladder(0, 4, 7, -1)), 3)


def ghost_place(kind, n, c, x):
    if kind == "ze":
        return {0: (c, x), 3: (c, (x + 4) % N), 1: (2 + c, x), 2: (2 + c, (x + 4) % N)}[n]
    return {1: (c, x), 3: (c, (x + 4) % N), 2: (2, (x + 4 * c) % N)}[n]


def ghost_tile(ref, kind, n, c):
    tile, row = ghost_place(kind, n, c, 0)
    value = ref[tile]
    return pltpu.roll(value, 4, 0) if row == 4 else value


def slot_e(n, c):
    return 2 * n + c


def slot_h(n, c):
    return 2 * (n - 1) + c


def wide(tile):
    return jnp.concatenate([tile] * (NY // LANES), axis=1)


def sublane(shape):
    return lax.broadcasted_iota(jnp.int32, shape, 0)


def lane(shape):
    return lax.broadcasted_iota(jnp.int32, shape, 1)


def add(x, y):
    return y if x is None else x if y is None else x + y


def sub(x, y):
    return x if y is None else -y if x is None else x - y


def mul(k, x):
    return None if x is None else k * x


def y_ahead(v):
    if v is None:
        return None
    r = pltpu.roll(v, NY - 1, 1)
    last = r[:, NY - LANES :]
    return jnp.concatenate([r[:, : NY - LANES], jnp.where(lane(last.shape) == LANES - 1, 0.0, last)], axis=1)


def y_behind(v):
    if v is None:
        return None
    r = pltpu.roll(v, 1, 1)
    first = r[:, :LANES]
    return jnp.concatenate([jnp.where(lane(first.shape) == 0, 0.0, first), r[:, LANES:]], axis=1)


def x_up(v):
    return None if v is None else pltpu.roll(v, N - 1, 0)


def x_down(v):
    return None if v is None else pltpu.roll(v, 1, 0)


def choose(edge, x, y):
    if x is None and y is None:
        return None
    return jnp.where(edge, 0.0 if x is None else x, 0.0 if y is None else y)


def kind_tables(eps_ref, loss_ref):
    out = []
    for k in range(4):
        damping = jnp.full((N, LANES), loss_ref[k], jnp.float32)
        permittivity = jnp.full((N, LANES), eps_ref[k], jnp.float32)
        scale = 1.0 / (1.0 + damping)
        inverse = 1.0 / permittivity
        out.append(((1.0 - damping) * scale, COURANT * scale, COURANT * scale * inverse, inverse))
    return out


def row_coefficients(kind, tables):
    masks = [kind == k + 1.0 for k in range(4)]
    out = []
    for j in range(4):
        total = jnp.zeros((N, LANES), jnp.float32)
        for k in range(4):
            total = jnp.where(masks[k], tables[k][j], total)
        out.append(total)
    out.append(jnp.where(masks[3], 1.0, 0.0))
    return out


def polar_scalars(lorentz_ref):
    shape = (N, LANES)
    a = jnp.full(shape, lorentz_ref[0], jnp.float32)
    g = jnp.full(shape, lorentz_ref[1], jnp.float32)
    s = jnp.full(shape, lorentz_ref[2], jnp.float32)
    scale = 1.0 / (1.0 + 0.5 * g)
    return (1.0 - a * a - 0.5 * g) * scale, (1.0 - 0.5 * g) * scale, s * a * a * scale


def own_kinds(material_ref):
    row = sublane((N, LANES))
    out = []
    for z in range(N):
        kind = jnp.zeros((N, LANES), jnp.int32)
        for x in range(N):
            kind = jnp.where(row == x, material_ref[z, x] + 1, kind)
        out.append(kind.astype(jnp.float32))
    return out


def e_update(curl, e, a, b, k, polar):
    retain, _, e_gain, inverse, active = k
    p, q, r = polar
    moved = mul(active, add(sub(mul(p, a), mul(q, b)), mul(r, e)))
    e_new = sub(add(mul(retain, e), mul(e_gain, curl)), mul(inverse, moved))
    p_new = add(a, moved)
    if b is None:
        return e_new, mul(active, p_new)
    return e_new, jnp.where(active > 0.5, p_new, b)


def start_all(pairs, sems):
    copies = [pltpu.make_async_copy(source, target, sems.at[i]) for i, (source, target) in enumerate(pairs)]
    for copy in copies:
        copy.start()
    return copies


def wait_all(copies):
    for copy in copies:
        copy.wait()


def alone_kernel(
    e_hbm, h_hbm, p_hbm, material_hbm, eps_hbm, loss_hbm, lorentz_hbm,
    m0, m1, w0, w1,
    e, h, a, b, ze, zh, xe, xh, rays, coef, material, eps, loss, lorentz, sems,
):
    high_first = lax.rem(lax.axis_index("dev"), 2) == 0
    above_first = lax.rem(lax.axis_index("grp"), 2) == 0
    small = start_all(
        [(material_hbm, material), (eps_hbm, eps), (loss_hbm, loss), (lorentz_hbm, lorentz)], sems.at[pl.ds(0, 4)]
    )
    large = start_all(
        [(e_hbm, e), (h_hbm, h), (p_hbm.at[0], a), (p_hbm.at[1], b)], sems.at[pl.ds(4, 4)]
    )
    wait_all(small)
    tables = kind_tables(eps, loss)
    polar = [wide(v) for v in polar_scalars(lorentz)]
    ln = lane((N, LANES))
    packed = jnp.zeros((N, LANES), jnp.float32)
    for z, kind in enumerate(own_kinds(material)):
        packed = jnp.where(ln == z, kind, packed)
        for j, v in enumerate(row_coefficients(kind, tables)):
            coef[j, z] = v
    packed = wide(packed)
    m0[12] = packed
    m1[12] = packed
    w0[8] = packed
    w1[8] = packed
    wait_all(large)
    row = sublane((N, NY))
    top = row == N - 1
    bottom = row == 0

    for n in range(1, STEPS + 1):
        old, new = (a, b) if n % 2 == 1 else (b, a)
        for c in range(2):
            ze[slot_e(n - 1, c)] = e[c, 0]
        for z in range(N):
            k = [wide(coef[j, z]) for j in range(5)]
            retain, h_gain = k[0], k[1]
            ex, ey, ez = (e[c, z] for c in range(3))
            e1x, e1y = (e[c, z + 1] if z < N - 1 else None for c in range(2))
            r = slot_e(n - 1, 0)
            xe[z, r : r + 1, :] = ey[0:1, :]
            xe[z, r + 1 : r + 2, :] = ez[0:1, :]
            xa_y = choose(top, None, x_up(ey))
            xa_z = choose(top, None, x_up(ez))
            hx = retain * h[0, z] - h_gain * ((y_ahead(ez) - ez) - sub(e1y, ey))
            hy = retain * h[1, z] - h_gain * (sub(e1x, ex) - (xa_z - ez))
            hz = retain * h[2, z] - h_gain * ((xa_y - ey) - (y_ahead(ex) - ex))
            h[0, z] = hx
            h[1, z] = hy
            h[2, z] = hz
            r = slot_h(n, 0)
            xh[z, r : r + 1, :] = hy[N - 1 : N, :]
            xh[z, r + 1 : r + 2, :] = hz[N - 1 : N, :]
            if n < STEPS:
                lx, ly = (h[c, z - 1] if z else None for c in range(2))
                xb_y = choose(bottom, None, x_down(hy))
                xb_z = choose(bottom, None, x_down(hz))
                curls = (
                    (hz - y_behind(hz)) - sub(hy, ly),
                    sub(hx, lx) - (hz - xb_z),
                    (hy - xb_y) - (hx - y_behind(hx)),
                )
                for c, (curl, field) in enumerate(zip(curls, (ex, ey, ez))):
                    e[c, z], new[c, z] = e_update(curl, field, old[c, z], new[c, z], k, polar)
        for c in range(2):
            zh[slot_h(n, c)] = h[c, N - 1]

    for i, table in enumerate((HX, LX)):
        for (kind, n, c, x), (tile, r) in table.items():
            source = ze.at[slot_e(n, c)] if kind == "ze" else zh.at[slot_h(n, c)]
            rays[i, tile - 8, r : r + 1, :] = source[x : x + 1, :]
    for i, table in enumerate((HZ, LZ)):
        for (kind, n, c, z), (tile, r) in table.items():
            at = slot_e(n, c) if kind == "xe" else slot_h(n, c)
            source = xe if kind == "xe" else xh
            rays[2 + i, tile - 9, r : r + 1, :] = source[z, at : at + 1, :]

    def deal(first, one, other, tile, for_above, for_below):
        one[tile] = jnp.where(first, for_above, for_below)
        other[tile] = jnp.where(first, for_below, for_above)

    for i in range(N):
        deal(high_first, m0, m1, i, xh[i], xe[i])
        deal(above_first, w0, w1, i, zh[i], ze[i])
    for i in range(4):
        deal(high_first, m0, m1, 8 + i, rays[1, i], rays[0, i])
    for i in range(3):
        deal(above_first, w0, w1, 9 + i, rays[3, i], rays[2, i])


def forward_kernel(r0, r1, v0, v1, high, low, ghosts, rays):
    high_first = lax.rem(lax.axis_index("dev"), 2) == 0
    above_first = lax.rem(lax.axis_index("grp"), 2) == 0
    for i in range(X_TILES):
        one, other = r0[i], r1[i]
        high[i] = jnp.where(high_first, one, other)
        low[i] = jnp.where(high_first, other, one)
    row = sublane((N, NY))
    packed = jnp.where(row < 3, high[12], jnp.where(row > 3, low[12], 0.0))
    rays[0, 7] = packed
    rays[1, 7] = packed
    for x, source, table in [(x, high, HX) for x in range(3)] + [(x, low, LX) for x in range(4, N)]:
        for (kind, n, c, place), (tile, r) in table.items():
            if place == x:
                to, at = ghost_place(kind, n, c, x)
                rays[0 if kind == "ze" else 1, to, at : at + 1, :] = source[tile, r : r + 1, :]
    for i, table in enumerate((HF, LF)):
        for (kind, n, c, z), (tile, r) in table.items():
            at = slot_e(n, c) if kind == "xeh" else slot_h(n, c)
            source = high if kind == "xeh" else low
            rays[i, tile, r : r + 1, :] = source[z, at : at + 1, :]
    for i in range(4):
        ghosts[i] = rays[0, i]
    for i in range(3):
        ghosts[4 + i] = rays[1, i]
    for i in range(FAR_TILES):
        below, above = rays[0, i], rays[1, i]
        v0[i] = jnp.where(above_first, above, below)
        v1[i] = jnp.where(above_first, below, above)


def plan():
    mine = {(c, z, 0) for c in range(3) for z in range(N)}
    need_h, need_e = {STEPS: set(mine)}, {STEPS: set(mine)}
    for n in range(STEPS, 0, -1):
        for c, z, s in need_e[n]:
            t = 1 - s
            need_h[n] |= {
                0: {(2, z, s), (1, z, s), (1, z - 1, s)},
                1: {(0, z, s), (0, z - 1, s), (2, z, s), (2, z, t)},
                2: {(1, z, s), (1, z, t), (0, z, s)},
            }[c]
        need_e[n - 1] = set(need_e[n])
        need_h[n - 1] = set(need_h[n])
        for c, z, s in need_h[n]:
            t = 1 - s
            need_e[n - 1] |= {
                0: {(2, z, s), (1, z, s), (1, z + 1, s)},
                1: {(0, z, s), (0, z + 1, s), (2, z, s), (2, z, t)},
                2: {(1, z, s), (1, z, t), (0, z, s)},
            }[c]
    return need_h, need_e


def together_kernel(
    e_hbm, h_hbm, p_hbm, material_hbm, eps_hbm, loss_hbm, lorentz_hbm,
    high, low, ghosts, g0, g1, f0, f1, weights,
    e_out, h_out, p_out, s_out,
    e, h, a, b, own, far, coef, seen, spectrum, material, eps, loss, lorentz, sems,
):
    above_first = lax.rem(lax.axis_index("grp"), 2) == 0
    mine = pl.ds(Z0, N)
    small = start_all(
        [(material_hbm, material), (eps_hbm, eps), (loss_hbm, loss), (lorentz_hbm, lorentz)], sems.at[pl.ds(0, 4)]
    )
    large = start_all(
        [
            (e_hbm, e.at[:, mine, 0]),
            (h_hbm, h.at[:, mine, 0]),
            (p_hbm.at[0], a.at[:, mine, 0]),
            (p_hbm.at[1], b.at[:, mine, 0]),
        ],
        sems.at[pl.ds(4, 4)],
    )
    for target, one, other, tiles in ((own, g0, g1, OWN_TILES), (far, f0, f1, FAR_TILES)):
        for i in range(tiles):
            x, y = one[i], other[i]
            target[0, i] = jnp.where(above_first, x, y)
            target[1, i] = jnp.where(above_first, y, x)
    above, below = own.at[0], own.at[1]
    far_above, far_below = far.at[0], far.at[1]
    wait_all(small)
    tables = kind_tables(eps, loss)
    polar = [wide(v) for v in polar_scalars(lorentz)]
    narrow = sublane((N, LANES))
    kinds = {(z, 0): kind for z, kind in enumerate(own_kinds(material))}
    side = jnp.where(narrow < 3, high[12, :, 0:LANES], jnp.where(narrow > 3, low[12, :, 0:LANES], 0.0))
    columns = [(z, 1, side, z) for z in range(N)]
    for z in (*range(-4, 0), *range(N, N + 3)):
        near, corner = (below, far_below) if z < 0 else (above, far_above)
        columns += [(z, 0, near[8, :, 0:LANES], z % N), (z, 1, corner[7, :, 0:LANES], z % N)]
    for z, s, tile, at in columns:
        kinds[(z, s)] = jnp.broadcast_to(tile[:, at : at + 1], (N, LANES))
    for (z, s), kind in kinds.items():
        for j, v in enumerate(row_coefficients(kind, tables)):
            coef[j, Z0 + z, s] = v
    wait_all(large)

    row = sublane((N, NY))
    top = row == N - 1
    bottom = row == 0

    def lookup(table, near, far_table, far_near, kind, n, c, z):
        for t, ref in ((table, near), (far_table, far_near)):
            if (kind, n, c, z) in t:
                tile, r = t[(kind, n, c, z)]
                return ref[tile, r : r + 1, :]
        return None

    def x_source(kind, n, c, z):
        if 0 <= z < N:
            if kind in ("xe", "xh"):
                return None
            r = slot_e(n, c) if kind == "xeh" else slot_h(n, c)
            return (high if kind == "xeh" else low)[z, r : r + 1, :]
        if z >= N:
            found = lookup(HZ, above, HF, far_above, kind, n, c, z - N)
        else:
            found = lookup(LZ, below, LF, far_below, kind, n, c, z + N)
        return found

    def z_source(kind, n, c, z, s):
        if kind == "ze" and z == N:
            return above[slot_e(n, c)] if s == 0 else ghost_tile(far_above, "ze", n, c)
        if kind == "ze" and z == 0 and s == 1 and n < 3:
            return ghost_tile(ghosts, "ze", n, c)
        if kind == "zh" and z == -1:
            if s == 0:
                return below[slot_h(n, c)]
            return ghost_tile(far_below, "zh", n, c) if n < 4 else None
        if kind == "zh" and z == N - 1 and s == 1 and n < 4:
            return ghost_tile(ghosts.at[pl.ds(4, 3)], "zh", n, c)
        return None

    def across(v, shift, edge, s0, s1):
        v0, v1 = shift(v[0]), shift(v[1])
        return choose(edge, add(v1, s0), v0), choose(edge, add(v0, s1), v1)

    need_h, need_e = plan()
    live = {(f, c, z, 0) for f in range(4) for c in range(3) for z in range(N)}

    def get(f, c, z, s):
        return (e, h, a, b)[f][c, Z0 + z, s] if (f, c, z, s) in live else None

    def put(f, c, z, s, value):
        if value is not None:
            (e, h, a, b)[f][c, Z0 + z, s] = value
            live.add((f, c, z, s))

    outs = []
    for n in range(1, STEPS + 1):
        old, new = (2, 3) if n % 2 == 1 else (3, 2)
        for z in range(-4, N + 3):
            todo = {(c, s) for c, at, s in need_h[n] if at == z}
            ey = [get(0, 1, z, s) for s in range(2)]
            ez = [get(0, 2, z, s) for s in range(2)]
            xa_y = xa_z = (None, None)
            if todo:
                xa_y = across(ey, x_up, top, x_source("xeh", n - 1, 0, z), x_source("xe", n - 1, 0, z))
                xa_z = across(ez, x_up, top, x_source("xeh", n - 1, 1, z), x_source("xe", n - 1, 1, z))
            for s in range(2):
                if not any((c, s) in todo for c in range(3)):
                    continue
                k = [wide(coef[j, Z0 + z, s]) for j in range(2)]
                ex = get(0, 0, z, s)
                e1x = add(get(0, 0, z + 1, s), z_source("ze", n - 1, 0, z + 1, s))
                e1y = add(get(0, 1, z + 1, s), z_source("ze", n - 1, 1, z + 1, s))
                curls = (
                    lambda: sub(sub(y_ahead(ez[s]), ez[s]), sub(e1y, ey[s])),
                    lambda: sub(sub(e1x, ex), sub(xa_z[s], ez[s])),
                    lambda: sub(sub(xa_y[s], ey[s]), sub(y_ahead(ex), ex)),
                )
                for c in range(3):
                    if (c, s) in todo:
                        put(1, c, z, s, sub(mul(k[0], get(1, c, z, s)), mul(k[1], curls[c]())))
            todo = {(c, s) for c, at, s in need_e[n] if at == z}
            if not todo:
                continue
            hy = [get(1, 1, z, s) for s in range(2)]
            hz = [get(1, 2, z, s) for s in range(2)]
            xb_y = across(hy, x_down, bottom, x_source("xhl", n, 0, z), x_source("xh", n, 0, z))
            xb_z = across(hz, x_down, bottom, x_source("xhl", n, 1, z), x_source("xh", n, 1, z))
            for s in range(2):
                if not any((c, s) in todo for c in range(3)):
                    continue
                k = [wide(coef[j, Z0 + z, s]) for j in range(5)]
                hx = get(1, 0, z, s)
                lx = add(get(1, 0, z - 1, s), z_source("zh", n, 0, z - 1, s))
                ly = add(get(1, 1, z - 1, s), z_source("zh", n, 1, z - 1, s))
                curls = (
                    lambda: sub(sub(hz[s], y_behind(hz[s])), sub(hy[s], ly)),
                    lambda: sub(sub(hx, lx), sub(hz[s], xb_z[s])),
                    lambda: sub(sub(hy[s], xb_y[s]), sub(hx, y_behind(hx))),
                )
                for c in range(3):
                    if (c, s) in todo:
                        e_new, p_new = e_update(
                            curls[c](), get(0, c, z, s), get(old, c, z, s), get(new, c, z, s), k, polar
                        )
                        put(0, c, z, s, e_new)
                        if n < STEPS or s == 0:
                            put(new, c, z, s, p_new)
            if z == N // 2:
                for c in range(3):
                    seen[n - 1, c] = e[c, Z0 + z, 0]
            if n == STEPS:
                at = Z0 + z
                outs += start_all(
                    [
                        (e.at[:, at, 0], e_out.at[:, z]),
                        (h.at[:, at, 0], h_out.at[:, z]),
                        (a.at[:, at, 0], p_out.at[0, :, z]),
                        (b.at[:, at, 0], p_out.at[1, :, z]),
                    ],
                    sems.at[pl.ds(8 + 4 * z, 4)],
                )
                if z == N // 2:
                    for c in range(3):
                        planes = [seen[i, c] for i in range(STEPS)]
                        for f in range(FREQS):
                            for q in range(2):
                                total = weights[0, f, q] * planes[0]
                                for i in range(1, STEPS):
                                    total = total + weights[i, f, q] * planes[i]
                                spectrum[f, q, c, 0] = total
                    outs += start_all([(spectrum, s_out)], sems.at[pl.ds(40, 1)])
    wait_all(outs)


HBM = pl.BlockSpec(memory_space=pltpu.HBM)
VMEM = pl.BlockSpec(memory_space=pltpu.VMEM)
SMEM = pl.BlockSpec(memory_space=pltpu.SMEM)


def f32(*shape):
    return jax.ShapeDtypeStruct(shape, jnp.float32)


def vmem(*shape):
    return pltpu.VMEM(shape, jnp.float32)


def small_tables():
    return [pltpu.SMEM((N, N), jnp.int32), pltpu.SMEM((4,), jnp.float32), pltpu.SMEM((4,), jnp.float32), pltpu.SMEM((3,), jnp.float32)]


def params():
    return pltpu.CompilerParams(vmem_limit_bytes=32 * 1024 * 1024)


def swap(block, axis, parity):
    size = lax.axis_size(axis)
    route = []
    for i in range(parity, size - 1, 2):
        route += [(i, i + 1), (i + 1, i)]
    return lax.ppermute(block, axis, route)


def call_alone(inputs):
    plane = (2 * STEPS, N, NY)
    return pl.pallas_call(
        alone_kernel,
        out_shape=[f32(X_TILES, N, NY)] * 2 + [f32(OWN_TILES, N, NY)] * 2,
        in_specs=[HBM] * 7,
        out_specs=[VMEM] * 4,
        scratch_shapes=[vmem(3, N, N, NY)] * 4
        + [vmem(*plane)] * 4
        + [vmem(4, 4, N, NY), vmem(5, N, N, LANES)]
        + small_tables()
        + [pltpu.SemaphoreType.DMA((8,))],
        compiler_params=params(),
        name="alone",
    )(*inputs)


def call_forward(r0, r1):
    return pl.pallas_call(
        forward_kernel,
        out_shape=[f32(FAR_TILES, N, NY)] * 2 + [f32(X_TILES, N, NY)] * 2 + [f32(7, N, NY)],
        in_specs=[VMEM] * 2,
        out_specs=[VMEM] * 5,
        scratch_shapes=[vmem(2, FAR_TILES, N, NY)],
        compiler_params=params(),
        name="forward",
    )(r0, r1)


def call_together(inputs, received, weights):
    return pl.pallas_call(
        together_kernel,
        out_shape=[f32(3, N, N, NY), f32(3, N, N, NY), f32(2, 3, N, N, NY), f32(FREQS, 2, 3, 1, N, NY)],
        in_specs=[HBM] * 7 + [VMEM] * 7 + [SMEM],
        out_specs=[HBM] * 4,
        scratch_shapes=[vmem(3, ROWS, 2, N, NY)] * 4
        + [
            vmem(2, OWN_TILES, N, NY),
            vmem(2, FAR_TILES, N, NY),
            vmem(5, ROWS, 2, N, LANES),
            vmem(STEPS, 3, N, NY),
            vmem(FREQS, 2, 3, 1, N, NY),
        ]
        + small_tables()
        + [pltpu.SemaphoreType.DMA((41,))],
        compiler_params=params(),
        name="together",
    )(*inputs, *received, weights)


def on_device(e_field, h_field, polar, material, eps_table, loss_table, lorentz, freqs):
    inputs = (e_field, h_field, polar, material, eps_table, loss_table, lorentz)
    m0, m1, w0, w1 = call_alone(inputs)
    r1 = swap(m1, "dev", 1)
    r0 = swap(m0, "dev", 0)
    g1 = swap(w1, "grp", 1)
    g0 = swap(w0, "grp", 0)
    v0, v1, high, low, ghosts = call_forward(r0, r1)
    f1 = swap(v1, "grp", 1)
    f0 = swap(v0, "grp", 0)
    angles = freqs * jnp.arange(1, STEPS + 1, dtype=jnp.float32)[:, None]
    weights = jnp.stack([jnp.cos(angles), -jnp.sin(angles)], axis=2)
    return tuple(call_together(inputs, (high, low, ghosts, g0, g1, f0, f1), weights))


def solution(mesh):
    placed = (
        P(None, "grp", "dev", None),
        P(None, "grp", "dev", None),
        P(None, None, "grp", "dev", None),
        P("grp", "dev"),
        P(),
        P(),
        P(),
        P(),
    )
    return jax.shard_map(
        on_device,
        mesh=mesh,
        in_specs=placed,
        out_specs=(
            P(None, "grp", "dev", None),
            P(None, "grp", "dev", None),
            P(None, None, "grp", "dev", None),
            P(None, None, None, "grp", "dev", None),
        ),
        check_vma=False,
    )
```

time: 115 us -> 47 us (0.41)
  the two profiles are of different devices: /device:TPU:262 before, /device:TPU:264 now
where the time goes in v2:
time: 47 us; the launch traced here: 46.6 us
  starting transfers between devices  21.2 us (45%)
  Pallas kernels  10.5 us (22%)
  waiting for transfers between devices  7.97 us (17%)
  local copies, waits for them, and re-layouts  5.92 us (13%)
  between operations  0.76 us (2%)
    ppermute x6, starting transfers between devices, swap(): return lax.ppermute(block, axis, route)  21.2 us
    ppermute x6, waiting for transfers between devices, swap(): return lax.ppermute(block, axis, route)  7.97 us
    pallas_call x1, Pallas kernels, call_together(): pl.pallas_call(together_kernel, out_shape=[f32(3, N, N, NY), f32(3, N, N,...  6.78 us
    unnamed x22, local copies, waits for them, and re-layouts  5.92 us
    pallas_call x1, Pallas kernels, call_alone(): pl.pallas_call(alone_kernel, out_shape=[f32(X_TILES, N, NY)] * 2 + [f32(O...  3.51 us
  transfers between devices with their start and end apart: 6, of which 3 were waited for; matrix products, arithmetic and copies ran while one was open for 0% of the time, Pallas kernels for 0%

profile of v2, /device:TPU:264, one launch (start us, length us, event | category | flops | bytes accessed | tf_op | source)
XLA Modules:
  0.0 46.6 jit_solution(9593841819399586259)
XLA Ops:
  0.6 0.0 copy-start
  0.6 1.2 %copy-done = f32[2,3,8,8,640]{4,3,2,1,0:T(8,128)S(1)} copy-done((f32[2,3,8,8,640]{4,3,2,1,0:T(8,128)S(1)}, f32[2,3,8,8,640]{4,3,2,1,0:T(8,128)}, u32[]{:S(2)}) %copy-start) | copy-done | bytes 983064
  1.8 0.0 copy-start.2
  1.8 1.0 %copy-done.2 = f32[3,8,8,640]{3,2,1,0:T(8,128)S(1)} copy-done((f32[3,8,8,640]{3,2,1,0:T(8,128)S(1)}, f32[3,8,8,640]{3,2,1,0:T(8,128)}, u32[]{:S(2)}) %copy-start.2) | copy-done | bytes 491544
  2.9 1.0 %copy-done.4 = f32[3,8,8,640]{3,2,1,0:T(8,128)S(1)} copy-done((f32[3,8,8,640]{3,2,1,0:T(8,128)S(1)}, f32[3,8,8,640]{3,2,1,0:T(8,128)}, u32[]{:S(2)}) %copy-start.4) | copy-done | bytes 491544
  3.9 0.7 %copy-done.6 = s32[8,8]{1,0:T(8,128)S(1)} copy-done((s32[8,8]{1,0:T(8,128)S(1)}, s32[8,8]{1,0:T(8,128)}, u32[]{:S(2)}) %copy-start.6) | copy-done | bytes 280
  4.6 0.7 %copy-done.7 = f32[4]{0:T(128)S(1)} copy-done((f32[4]{0:T(128)S(1)}, f32[4]{0:T(128)}, u32[]{:S(2)}) %copy-start.7) | copy-done | bytes 40
  5.2 0.7 %copy-done.8 = f32[4]{0:T(128)S(1)} copy-done((f32[4]{0:T(128)S(1)}, f32[4]{0:T(128)}, u32[]{:S(2)}) %copy-start.8) | copy-done | bytes 40
  5.9 0.7 %copy-done.9 = f32[3]{0:T(128)S(1)} copy-done((f32[3]{0:T(128)S(1)}, f32[3]{0:T(128)}, u32[]{:S(2)}) %copy-start.9) | copy-done | bytes 36
  6.6 3.5 %alone.1 = (f32[13,8,640]{2,1,0:T(8,128)S(1)}, f32[13,8,640]{2,1,0:T(8,128)S(1)}, f32[12,8,640]{2,1,0:T(8,128)S(1)}, f32[12,8,640]{2,1,0:T(8,128)S(1)}) custom-call(f32[3,8,8,640]{3,2,1,0:T(8,128)S(1)} %copy-done.2, f32[3,8,8,640]{3,2,1,0:T(8,128)S(1)} %copy-done.4, f32[2,3,8,8,640]{4,3,2,1,0:T(8,128)S(1)} %copy-done, s32[8,8]{1,0:T(8,128)S(1)} %copy-done.6, ...), custom_call_target="tpu_custom_call" | custom-call | tf_op jit(solution)/shard_map/alone/pallas_call | solution.py:541
  10.1 0.0 copy-start.3
  10.1 2.1 %collective-permute-start = (f32[13,8,640]{2,1,0:T(8,128)S(1)}, f32[13,8,640]{2,1,0:T(8,128)S(1)}, u32[]{:S(2)}, u32[]{:S(2)}) collective-permute-start(f32[13,8,640]{2,1,0:T(8,128)S(1)} %get-tuple-element.13), channel_id=1, source_target_pairs={{0,1},{1,0},{2,3},{3,2},{4,5},{5,4},{6,7},{7,6},{8,9},{9,8},{10,11... | collective-permute-start | bytes 798728 | tf_op jit(solution)/shard_map/ppermute | solution.py:536
  12.1 4.5 %collective-permute-start.1 = (f32[13,8,640]{2,1,0:T(8,128)S(1)}, f32[13,8,640]{2,1,0:T(8,128)S(1)}, u32[]{:S(2)}, u32[]{:S(2)}) collective-permute-start(f32[13,8,640]{2,1,0:T(8,128)S(1)} %get-tuple-element.14), channel_id=1, source_target_pairs={{1,2},{2,1},{3,4},{4,3},{5,6},{6,5},{7,8},{8,7},{9,10},{10,9},{11,... | collective-permute-start | bytes 798728 | tf_op jit(solution)/shard_map/ppermute | solution.py:536
  16.6 3.4 %collective-permute-start.2 = (f32[12,8,640]{2,1,0:T(8,128)S(1)}, f32[12,8,640]{2,1,0:T(8,128)S(1)}, u32[]{:S(2)}, u32[]{:S(2)}) collective-permute-start(f32[12,8,640]{2,1,0:T(8,128)S(1)} %get-tuple-element.18), channel_id=1, source_target_pairs={{0,64},{64,0},{128,192},{192,128},{256,320},{320,256},{384,448},{4... | collective-permute-start | bytes 737288 | tf_op jit(solution)/shard_map/ppermute | solution.py:536
  20.0 4.8 %collective-permute-start.3 = (f32[12,8,640]{2,1,0:T(8,128)S(1)}, f32[12,8,640]{2,1,0:T(8,128)S(1)}, u32[]{:S(2)}, u32[]{:S(2)}) collective-permute-start(f32[12,8,640]{2,1,0:T(8,128)S(1)} %get-tuple-element.19), channel_id=1, source_target_pairs={{64,128},{128,64},{192,256},{256,192},{320,384},{384,320},{65,129}... | collective-permute-start | bytes 737288 | tf_op jit(solution)/shard_map/ppermute | solution.py:536
  24.8 0.0 collective-permute-done.r0
  24.8 2.0 %collective-permute-done.1.r1 = f32[13,8,640]{2,1,0:T(8,128)S(1)} collective-permute-done((f32[13,8,640]{2,1,0:T(8,128)S(1)}, f32[13,8,640]{2,1,0:T(8,128)S(1)}, u32[]{:S(2)}, u32[]{:S(2)}) %collective-permute-start.1) | collective-permute-done | bytes 266272 | tf_op jit(solution)/shard_map/ppermute | solution.py:536
  26.8 0.2 forward.1
  27.0 0.0 copy-start.10
  27.0 3.4 %collective-permute-start.4 = (f32[8,8,640]{2,1,0:T(8,128)S(1)}, f32[8,8,640]{2,1,0:T(8,128)S(1)}, u32[]{:S(2)}, u32[]{:S(2)}) collective-permute-start(f32[8,8,640]{2,1,0:T(8,128)S(1)} %get-tuple-element.20), channel_id=1, source_target_pairs={{0,64},{64,0},{128,192},{192,128},{256,320},{320,256},{384,448},{4... | collective-permute-start | bytes 491528 | tf_op jit(solution)/shard_map/ppermute | solution.py:536
  30.5 3.1 %collective-permute-start.5 = (f32[8,8,640]{2,1,0:T(8,128)S(1)}, f32[8,8,640]{2,1,0:T(8,128)S(1)}, u32[]{:S(2)}, u32[]{:S(2)}) collective-permute-start(f32[8,8,640]{2,1,0:T(8,128)S(1)} %get-tuple-element.21), channel_id=1, source_target_pairs={{64,128},{128,64},{192,256},{256,192},{320,384},{384,320},{65,129}... | collective-permute-start | bytes 491528 | tf_op jit(solution)/shard_map/ppermute | solution.py:536
  33.6 0.0 copy-done.10
  33.6 0.1 multiply_cosine_fusion
  33.7 0.1 pad_maximum_fusion.weights
  33.8 0.0 collective-permute-done.2.g0
  33.8 0.0 collective-permute-done.3.g1
  33.8 0.4 collective-permute-done.4.f0
  34.3 5.5 %collective-permute-done.5.f1 = f32[8,8,640]{2,1,0:T(8,128)S(1)} collective-permute-done((f32[8,8,640]{2,1,0:T(8,128)S(1)}, f32[8,8,640]{2,1,0:T(8,128)S(1)}, u32[]{:S(2)}, u32[]{:S(2)}) %collective-permute-start.5) | collective-permute-done | bytes 163872 | tf_op jit(solution)/shard_map/ppermute | solution.py:536
  39.8 0.0 copy-done.1
  39.8 0.0 copy-done.5
  39.8 0.0 copy-done.3
  39.8 6.8 %together.1 = (f32[3,8,8,640]{3,2,1,0:T(8,128)}, f32[3,8,8,640]{3,2,1,0:T(8,128)}, f32[2,3,8,8,640]{4,3,2,1,0:T(8,128)}, f32[4,2,3,1,8,640]{5,4,3,2,1,0:T(8,128)}) custom-call(f32[3,8,8,640]{3,2,1,0:T(8,128)S(1)} %copy-done.3, f32[3,8,8,640]{3,2,1,0:T(8,128)S(1)} %copy-done.5, f32[2,3,8,8,640]{4,3,2,1,0:T(8,128)S(1)} %copy-done.1, s32[8,8]{1,0:T(8,128)S(1)} %copy-done.6, ...), custom_call_target="tpu_custom_call" | custom-call | tf_op jit(solution)/shard_map/together/pallas_call | solution.py:569
  (8 shorter events, 0.0 us)
Async XLA Ops:
  0.6 1.2 %copy-start = (f32[2,3,8,8,640]{4,3,2,1,0:T(8,128)S(1)}, f32[2,3,8,8,640]{4,3,2,1,0:T(8,128)}, u32[]{:S(2)}) copy-start(f32[2,3,8,8,640]{4,3,2,1,0:T(8,128)} %p_hbm.3) | copy-start | bytes 2949124
  1.8 1.0 %copy-start.2 = (f32[3,8,8,640]{3,2,1,0:T(8,128)S(1)}, f32[3,8,8,640]{3,2,1,0:T(8,128)}, u32[]{:S(2)}) copy-start(f32[3,8,8,640]{3,2,1,0:T(8,128)} %e_hbm.3) | copy-start | bytes 1474564
  2.9 1.0 %copy-start.4 = (f32[3,8,8,640]{3,2,1,0:T(8,128)S(1)}, f32[3,8,8,640]{3,2,1,0:T(8,128)}, u32[]{:S(2)}) copy-start(f32[3,8,8,640]{3,2,1,0:T(8,128)} %h_hbm.3) | copy-start | bytes 1474564
  3.9 0.7 %copy-start.6 = (s32[8,8]{1,0:T(8,128)S(1)}, s32[8,8]{1,0:T(8,128)}, u32[]{:S(2)}) copy-start(s32[8,8]{1,0:T(8,128)} %material_hbm.3) | copy-start | bytes 772
  4.6 0.7 %copy-start.7 = (f32[4]{0:T(128)S(1)}, f32[4]{0:T(128)}, u32[]{:S(2)}) copy-start(f32[4]{0:T(128)} %eps_hbm.3) | copy-start | bytes 52
  5.2 0.7 %copy-start.8 = (f32[4]{0:T(128)S(1)}, f32[4]{0:T(128)}, u32[]{:S(2)}) copy-start(f32[4]{0:T(128)} %loss_hbm.3) | copy-start | bytes 52
  5.9 0.7 %copy-start.9 = (f32[3]{0:T(128)S(1)}, f32[3]{0:T(128)}, u32[]{:S(2)}) copy-start(f32[3]{0:T(128)} %lorentz_hbm.3) | copy-start | bytes 40
  6.6 33.2 %copy-start.1 = (f32[2,3,8,8,640]{4,3,2,1,0:T(8,128)S(1)}, f32[2,3,8,8,640]{4,3,2,1,0:T(8,128)}, u32[]{:S(2)}) copy-start(f32[2,3,8,8,640]{4,3,2,1,0:T(8,128)} %p_hbm.3) | copy-start | bytes 2949124
  6.6 33.2 %copy-start.5 = (f32[3,8,8,640]{3,2,1,0:T(8,128)S(1)}, f32[3,8,8,640]{3,2,1,0:T(8,128)}, u32[]{:S(2)}) copy-start(f32[3,8,8,640]{3,2,1,0:T(8,128)} %h_hbm.3) | copy-start | bytes 1474564
  10.1 29.7 %copy-start.3 = (f32[3,8,8,640]{3,2,1,0:T(8,128)S(1)}, f32[3,8,8,640]{3,2,1,0:T(8,128)}, u32[]{:S(2)}) copy-start(f32[3,8,8,640]{3,2,1,0:T(8,128)} %e_hbm.3) | copy-start | bytes 1474564
  10.1 14.7 %collective-permute-start = (f32[13,8,640]{2,1,0:T(8,128)S(1)}, f32[13,8,640]{2,1,0:T(8,128)S(1)}, u32[]{:S(2)}, u32[]{:S(2)}) collective-permute-start(f32[13,8,640]{2,1,0:T(8,128)S(1)} %get-tuple-element.13), channel_id=1, source_target_pairs={{0,1},{1,0},{2,3},{3,2},{4,5},{5,4},{6,7},{7,6},{8,9},{9,8},{10,11... | collective-permute-start | bytes 798728 | tf_op jit(solution)/shard_map/ppermute | solution.py:536
  12.1 14.7 %collective-permute-start.1 = (f32[13,8,640]{2,1,0:T(8,128)S(1)}, f32[13,8,640]{2,1,0:T(8,128)S(1)}, u32[]{:S(2)}, u32[]{:S(2)}) collective-permute-start(f32[13,8,640]{2,1,0:T(8,128)S(1)} %get-tuple-element.14), channel_id=1, source_target_pairs={{1,2},{2,1},{3,4},{4,3},{5,6},{6,5},{7,8},{8,7},{9,10},{10,9},{11,... | collective-permute-start | bytes 798728 | tf_op jit(solution)/shard_map/ppermute | solution.py:536
  16.6 17.2 %collective-permute-start.2 = (f32[12,8,640]{2,1,0:T(8,128)S(1)}, f32[12,8,640]{2,1,0:T(8,128)S(1)}, u32[]{:S(2)}, u32[]{:S(2)}) collective-permute-start(f32[12,8,640]{2,1,0:T(8,128)S(1)} %get-tuple-element.18), channel_id=1, source_target_pairs={{0,64},{64,0},{128,192},{192,128},{256,320},{320,256},{384,448},{4... | collective-permute-start | bytes 737288 | tf_op jit(solution)/shard_map/ppermute | solution.py:536
  20.0 13.8 %collective-permute-start.3 = (f32[12,8,640]{2,1,0:T(8,128)S(1)}, f32[12,8,640]{2,1,0:T(8,128)S(1)}, u32[]{:S(2)}, u32[]{:S(2)}) collective-permute-start(f32[12,8,640]{2,1,0:T(8,128)S(1)} %get-tuple-element.19), channel_id=1, source_target_pairs={{64,128},{128,64},{192,256},{256,192},{320,384},{384,320},{65,129}... | collective-permute-start | bytes 737288 | tf_op jit(solution)/shard_map/ppermute | solution.py:536
  27.0 6.5 %copy-start.10 = (f32[4]{0:T(128)S(1)}, f32[4]{0:T(128)}, u32[]{:S(2)}) copy-start(f32[4]{0:T(128)} %param.15) | copy-start | bytes 52
  27.0 7.2 %collective-permute-start.4 = (f32[8,8,640]{2,1,0:T(8,128)S(1)}, f32[8,8,640]{2,1,0:T(8,128)S(1)}, u32[]{:S(2)}, u32[]{:S(2)}) collective-permute-start(f32[8,8,640]{2,1,0:T(8,128)S(1)} %get-tuple-element.20), channel_id=1, source_target_pairs={{0,64},{64,0},{128,192},{192,128},{256,320},{320,256},{384,448},{4... | collective-permute-start | bytes 491528 | tf_op jit(solution)/shard_map/ppermute | solution.py:536
  30.5 9.3 %collective-permute-start.5 = (f32[8,8,640]{2,1,0:T(8,128)S(1)}, f32[8,8,640]{2,1,0:T(8,128)S(1)}, u32[]{:S(2)}, u32[]{:S(2)}) collective-permute-start(f32[8,8,640]{2,1,0:T(8,128)S(1)} %get-tuple-element.21), channel_id=1, source_target_pairs={{64,128},{128,64},{192,256},{256,192},{320,384},{384,320},{65,129}... | collective-permute-start | bytes 491528 | tf_op jit(solution)/shard_map/ppermute | solution.py:536

commit v3 on v2

--- a/solution.py
+++ b/solution.py
@@ -1,3 +1,5 @@
+import functools
+
 import jax
 import jax.numpy as jnp
 from jax import lax
@@ -188,8 +190,8 @@
 
 def alone_kernel(
     e_hbm, h_hbm, p_hbm, material_hbm, eps_hbm, loss_hbm, lorentz_hbm,
-    m0, m1, w0, w1,
-    e, h, a, b, ze, zh, xe, xh, rays, coef, material, eps, loss, lorentz, sems,
+    m0, m1, w0, w1, coef, shared,
+    e, h, a, b, ze, zh, xe, xh, rays, material, eps, loss, lorentz, sems,
 ):
     high_first = lax.rem(lax.axis_index("dev"), 2) == 0
     above_first = lax.rem(lax.axis_index("grp"), 2) == 0
@@ -201,7 +203,10 @@
     )
     wait_all(small)
     tables = kind_tables(eps, loss)
-    polar = [wide(v) for v in polar_scalars(lorentz)]
+    polar = polar_scalars(lorentz)
+    for i, v in enumerate([v for table in tables for v in table] + list(polar)):
+        shared[i] = v
+    polar = [wide(v) for v in polar]
     ln = lane((N, LANES))
     packed = jnp.zeros((N, LANES), jnp.float32)
     for z, kind in enumerate(own_kinds(material)):
@@ -278,7 +283,7 @@
         deal(above_first, w0, w1, 9 + i, rays[3, i], rays[2, i])
 
 
-def forward_kernel(r0, r1, v0, v1, high, low, ghosts, rays):
+def forward_kernel(r1, r0, v1, v0, high, low, ghosts, rays):
     high_first = lax.rem(lax.axis_index("dev"), 2) == 0
     above_first = lax.rem(lax.axis_index("grp"), 2) == 0
     for i in range(X_TILES):
@@ -309,40 +314,202 @@
         v1[i] = jnp.where(above_first, below, above)
 
 
+def h_inputs(c, z, s):
+    if c == 0:
+        return [(2, z, s), (1, z, s), (1, z + 1, s)], [("z", 1)]
+    if c == 1:
+        return [(0, z, s), (0, z + 1, s), (2, z, s), (2, z, 1 - s)], [("z", 0), ("x", 1)]
+    return [(1, z, s), (1, z, 1 - s), (0, z, s)], [("x", 0)]
+
+
+def e_inputs(c, z, s):
+    if c == 0:
+        return [(2, z, s), (1, z, s), (1, z - 1, s)], [("z", 1)]
+    if c == 1:
+        return [(0, z, s), (0, z - 1, s), (2, z, s), (2, z, 1 - s)], [("z", 0), ("x", 1)]
+    return [(1, z, s), (1, z, 1 - s), (0, z, s)], [("x", 0)]
+
+
+def x_source(kind, n, c, z):
+    if 0 <= z < N:
+        r = slot_e(n, c) if kind == "xeh" else slot_h(n, c)
+        return {"xeh": ("high", z, r), "xhl": ("low", z, r)}.get(kind)
+    near, far, place = (HZ, HF, z - N) if z >= N else (LZ, LF, z + N)
+    for name, table in (("own", near), ("far", far)):
+        if (kind, n, c, place) in table:
+            return (name, 0 if z >= N else 1, *table[(kind, n, c, place)])
+    return None
+
+
+def z_source(kind, n, c, z, s):
+    if kind == "ze" and z == N:
+        return ("own", 0, slot_e(n, c)) if s == 0 else ("far", 0, kind, n, c)
+    if kind == "ze" and z == 0 and s == 1 and n < STEPS - 1:
+        return ("ghosts", kind, n, c)
+    if kind == "zh" and z == -1 and (s == 0 or n < STEPS):
+        return ("own", 1, slot_h(n, c)) if s == 0 else ("far", 1, kind, n, c)
+    if kind == "zh" and z == N - 1 and s == 1 and n < STEPS:
+        return ("ghosts", kind, n, c)
+    return None
+
+
+def sources(field, n, z, s, wanted):
+    out = []
+    for border, c in wanted:
+        if field == "h":
+            at = x_source("xe" if s else "xeh", n - 1, c, z) if border == "x" else z_source("ze", n - 1, c, z + 1, s)
+        else:
+            at = x_source("xh" if s else "xhl", n, c, z) if border == "x" else z_source("zh", n, c, z - 1, s)
+        out.append(at)
+    return [at for at in out if at is not None]
+
+
 def plan():
     mine = {(c, z, 0) for c in range(3) for z in range(N)}
-    need_h, need_e = {STEPS: set(mine)}, {STEPS: set(mine)}
+    need = {("h", STEPS): set(mine), ("e", STEPS): set(mine)}
     for n in range(STEPS, 0, -1):
-        for c, z, s in need_e[n]:
-            t = 1 - s
-            need_h[n] |= {
-                0: {(2, z, s), (1, z, s), (1, z - 1, s)},
-                1: {(0, z, s), (0, z - 1, s), (2, z, s), (2, z, t)},
-                2: {(1, z, s), (1, z, t), (0, z, s)},
-            }[c]
-        need_e[n - 1] = set(need_e[n])
-        need_h[n - 1] = set(need_h[n])
-        for c, z, s in need_h[n]:
-            t = 1 - s
-            need_e[n - 1] |= {
-                0: {(2, z, s), (1, z, s), (1, z + 1, s)},
-                1: {(0, z, s), (0, z + 1, s), (2, z, s), (2, z, t)},
-                2: {(1, z, s), (1, z, t), (0, z, s)},
-            }[c]
-    return need_h, need_e
-
-
-def together_kernel(
-    e_hbm, h_hbm, p_hbm, material_hbm, eps_hbm, loss_hbm, lorentz_hbm,
-    high, low, ghosts, g0, g1, f0, f1, weights,
-    e_out, h_out, p_out, s_out,
-    e, h, a, b, own, far, coef, seen, spectrum, material, eps, loss, lorentz, sems,
+        for key in need[("e", n)]:
+            need[("h", n)] |= set(e_inputs(*key)[0])
+        need[("e", n - 1)] = set(need[("e", n)])
+        need[("h", n - 1)] = set(need[("h", n)])
+        for key in need[("h", n)]:
+            need[("e", n - 1)] |= set(h_inputs(*key)[0])
+    late = {("e", 0): set(), ("h", 0): set()}
+    for n in range(1, STEPS + 1):
+        for field, other, inputs, back in (("h", "e", h_inputs, n - 1), ("e", "h", e_inputs, n)):
+            late[(field, n)] = set()
+            for key in need[(field, n)]:
+                before, wanted = inputs(*key)
+                c, z, s = key
+                if (
+                    (s == 1 and not 0 <= z < N)
+                    or key in late[(field, n - 1)]
+                    or any(k in late[(other, back)] for k in before)
+                    or any(at[0] == "far" for at in sources(field, n, z, s, wanted))
+                ):
+                    late[(field, n)].add(key)
+    return need, late
+
+
+NEED, LATE = plan()
+FIELDS = {"e": 0, "h": 1, 0: 2, 1: 3}
+
+
+class Pass:
+    def __init__(self, second, live, stores, coefs, polar, places, row):
+        self.second, self.live, self.stores = second, live, stores
+        self.coefs, self.polar, self.places = coefs, polar, places
+        self.top, self.bottom = row == N - 1, row == 0
+        self.memo = {}
+
+    def once(self, key, make):
+        if key not in self.memo:
+            self.memo[key] = make()
+        return self.memo[key]
+
+    def store(self, field, c, z, s, n):
+        late = n > 0 and (c, z, s) in LATE[("h" if field == "h" else "e", n)]
+        return self.stores[late][FIELDS[field]]
+
+    def get(self, field, c, z, s, n):
+        key = (field, c, z, s)
+        if self.live.get(key, STEPS + 1) > n:
+            return None
+        made = n if field in ("e", "h") else n - 1 if (n - 1) % 2 == field else n - 2
+        return self.once((*key, n), lambda: self.store(field, c, z, s, made)[c, Z0 + z, s])
+
+    def put(self, field, c, z, s, n, value):
+        if value is None:
+            return
+        self.store(field, c, z, s, n)[c, Z0 + z, s] = value
+        self.live.setdefault((field, c, z, s), n)
+        self.memo[(field, c, z, s, n)] = value
+
+    def source(self, at):
+        if at is None:
+            return None
+        if at[0] == "ghosts" or len(at) == 5:
+            ref = self.places[at[0]] if at[0] == "ghosts" else self.places["far"].at[at[1]]
+            kind, n, c = at[-3:]
+            if at[0] == "ghosts" and kind == "zh":
+                ref = ref.at[pl.ds(4, 3)]
+            return ghost_tile(ref, kind, n, c)
+        ref = self.places[at[0]]
+        if at[0] in ("high", "low"):
+            return ref[at[1], at[2] : at[2] + 1, :]
+        if len(at) == 3:
+            return ref[at[1], at[2]]
+        return ref[at[1], at[2], at[3] : at[3] + 1, :]
+
+    def k(self, j, z, s):
+        coef = self.coefs[s == 1 and not 0 <= z < N]
+        return self.once(("k", j, z, s), lambda: wide(coef[j, Z0 + z, s]))
+
+    def x_neighbour(self, field, c, z, s, n):
+        shift, edge = (x_up, self.top) if field == "e" else (x_down, self.bottom)
+
+        def moved(half):
+            return self.once(("x", field, c, z, half, n), lambda: shift(self.get(field, c, z, half, n)))
+
+        kinds = ("xeh", "xe") if field == "e" else ("xhl", "xh")
+        from_block = self.source(x_source(kinds[s], n, c - 1, z))
+        return choose(edge, add(moved(1 - s), from_block), moved(s))
+
+    def y_neighbour(self, field, c, z, s, n):
+        shift = y_ahead if field == "e" else y_behind
+        return self.once(("y", field, c, z, s, n), lambda: shift(self.get(field, c, z, s, n)))
+
+    def z_neighbour(self, field, c, z, s, n):
+        kind, at = ("ze", z + 1) if field == "e" else ("zh", z - 1)
+        return add(self.get(field, c, at, s, n), self.source(z_source(kind, n, c, at, s)))
+
+    def step_h(self, n, c, z, s):
+        m = n - 1
+        ex, ey, ez = (lambda c=c: self.get("e", c, z, s, m) for c in range(3))
+        if c == 0:
+            curl = sub(sub(self.y_neighbour("e", 2, z, s, m), ez()), sub(self.z_neighbour("e", 1, z, s, m), ey()))
+        elif c == 1:
+            curl = sub(sub(self.z_neighbour("e", 0, z, s, m), ex()), sub(self.x_neighbour("e", 2, z, s, m), ez()))
+        else:
+            curl = sub(sub(self.x_neighbour("e", 1, z, s, m), ey()), sub(self.y_neighbour("e", 0, z, s, m), ex()))
+        value = sub(mul(self.k(0, z, s), self.get("h", c, z, s, m)), mul(self.k(1, z, s), curl))
+        self.put("h", c, z, s, n, value)
+
+    def step_e(self, n, c, z, s):
+        hx, hy, hz = (lambda c=c: self.get("h", c, z, s, n) for c in range(3))
+        if c == 0:
+            curl = sub(sub(hz(), self.y_neighbour("h", 2, z, s, n)), sub(hy(), self.z_neighbour("h", 1, z, s, n)))
+        elif c == 1:
+            curl = sub(sub(hx(), self.z_neighbour("h", 0, z, s, n)), sub(hz(), self.x_neighbour("h", 2, z, s, n)))
+        else:
+            curl = sub(sub(hy(), self.x_neighbour("h", 1, z, s, n)), sub(hx(), self.y_neighbour("h", 0, z, s, n)))
+        old, new = (n - 1) % 2, n % 2
+        k = [self.k(j, z, s) for j in range(5)]
+        e_new, p_new = e_update(
+            curl, self.get("e", c, z, s, n - 1), self.get(old, c, z, s, n), self.get(new, c, z, s, n), k, self.polar
+        )
+        self.put("e", c, z, s, n, e_new)
+        if n < STEPS or s == 0:
+            self.put(new, c, z, s, n, p_new)
+
+    def row(self, n, z, seen):
+        for field, step in (("h", self.step_h), ("e", self.step_e)):
+            for s in range(2):
+                for c in range(3):
+                    if (c, z, s) in NEED[(field, n)] and ((c, z, s) in LATE[(field, n)]) == self.second:
+                        step(n, c, z, s)
+                        if field == "e" and (c, z, s) == (c, N // 2, 0):
+                            seen[n - 1, c] = self.get("e", c, z, s, n)
+        self.memo = {}
+
+
+def near_kernel(
+    live, e_hbm, h_hbm, p_hbm, coef_in, tables, high, low, ghosts, g1, g0,
+    e, h, a, b, coef, own, seen,
+    sems,
 ):
     above_first = lax.rem(lax.axis_index("grp"), 2) == 0
     mine = pl.ds(Z0, N)
-    small = start_all(
-        [(material_hbm, material), (eps_hbm, eps), (loss_hbm, loss), (lorentz_hbm, lorentz)], sems.at[pl.ds(0, 4)]
-    )
     large = start_all(
         [
             (e_hbm, e.at[:, mine, 0]),
@@ -350,140 +517,63 @@
             (p_hbm.at[0], a.at[:, mine, 0]),
             (p_hbm.at[1], b.at[:, mine, 0]),
         ],
-        sems.at[pl.ds(4, 4)],
+        sems,
     )
-    for target, one, other, tiles in ((own, g0, g1, OWN_TILES), (far, f0, f1, FAR_TILES)):
-        for i in range(tiles):
-            x, y = one[i], other[i]
-            target[0, i] = jnp.where(above_first, x, y)
-            target[1, i] = jnp.where(above_first, y, x)
-    above, below = own.at[0], own.at[1]
-    far_above, far_below = far.at[0], far.at[1]
-    wait_all(small)
-    tables = kind_tables(eps, loss)
-    polar = [wide(v) for v in polar_scalars(lorentz)]
+    for i in range(OWN_TILES):
+        x, y = g0[i], g1[i]
+        own[0, i] = jnp.where(above_first, x, y)
+        own[1, i] = jnp.where(above_first, y, x)
     narrow = sublane((N, LANES))
-    kinds = {(z, 0): kind for z, kind in enumerate(own_kinds(material))}
     side = jnp.where(narrow < 3, high[12, :, 0:LANES], jnp.where(narrow > 3, low[12, :, 0:LANES], 0.0))
     columns = [(z, 1, side, z) for z in range(N)]
-    for z in (*range(-4, 0), *range(N, N + 3)):
-        near, corner = (below, far_below) if z < 0 else (above, far_above)
-        columns += [(z, 0, near[8, :, 0:LANES], z % N), (z, 1, corner[7, :, 0:LANES], z % N)]
+    columns += [(z, 0, own[1 if z < 0 else 0, 8, :, 0:LANES], z % N) for z in (*range(-4, 0), *range(N, N + 3))]
+    fill_coefficients(coef, columns, tables)
+    for z in range(N):
+        for j in range(5):
+            coef[j, Z0 + z, 0] = coef_in[j, z]
+    polar = [wide(tables[16 + j]) for j in range(3)]
+    wait_all(large)
+    live.update({(field, c, z, 0): 0 for field in FIELDS for c in range(3) for z in range(N)})
+    places = {"own": own, "high": high, "low": low, "ghosts": ghosts}
+    run = Pass(False, live, [(e, h, a, b)] * 2, [coef, None], polar, places, sublane((N, NY)))
+    for n in range(1, STEPS + 1):
+        for z in range(-4, N + 3):
+            run.row(n, z, seen)
+
+
+def fill_coefficients(coef, columns, tables):
+    stacked = [[tables[4 * k + j] for j in range(4)] for k in range(4)]
     for z, s, tile, at in columns:
-        kinds[(z, s)] = jnp.broadcast_to(tile[:, at : at + 1], (N, LANES))
-    for (z, s), kind in kinds.items():
-        for j, v in enumerate(row_coefficients(kind, tables)):
+        kind = jnp.broadcast_to(tile[:, at : at + 1], (N, LANES))
+        for j, v in enumerate(row_coefficients(kind, stacked)):
             coef[j, Z0 + z, s] = v
-    wait_all(large)
-
-    row = sublane((N, NY))
-    top = row == N - 1
-    bottom = row == 0
-
-    def lookup(table, near, far_table, far_near, kind, n, c, z):
-        for t, ref in ((table, near), (far_table, far_near)):
-            if (kind, n, c, z) in t:
-                tile, r = t[(kind, n, c, z)]
-                return ref[tile, r : r + 1, :]
-        return None
-
-    def x_source(kind, n, c, z):
-        if 0 <= z < N:
-            if kind in ("xe", "xh"):
-                return None
-            r = slot_e(n, c) if kind == "xeh" else slot_h(n, c)
-            return (high if kind == "xeh" else low)[z, r : r + 1, :]
-        if z >= N:
-            found = lookup(HZ, above, HF, far_above, kind, n, c, z - N)
-        else:
-            found = lookup(LZ, below, LF, far_below, kind, n, c, z + N)
-        return found
-
-    def z_source(kind, n, c, z, s):
-        if kind == "ze" and z == N:
-            return above[slot_e(n, c)] if s == 0 else ghost_tile(far_above, "ze", n, c)
-        if kind == "ze" and z == 0 and s == 1 and n < 3:
-            return ghost_tile(ghosts, "ze", n, c)
-        if kind == "zh" and z == -1:
-            if s == 0:
-                return below[slot_h(n, c)]
-            return ghost_tile(far_below, "zh", n, c) if n < 4 else None
-        if kind == "zh" and z == N - 1 and s == 1 and n < 4:
-            return ghost_tile(ghosts.at[pl.ds(4, 3)], "zh", n, c)
-        return None
-
-    def across(v, shift, edge, s0, s1):
-        v0, v1 = shift(v[0]), shift(v[1])
-        return choose(edge, add(v1, s0), v0), choose(edge, add(v0, s1), v1)
-
-    need_h, need_e = plan()
-    live = {(f, c, z, 0) for f in range(4) for c in range(3) for z in range(N)}
-
-    def get(f, c, z, s):
-        return (e, h, a, b)[f][c, Z0 + z, s] if (f, c, z, s) in live else None
-
-    def put(f, c, z, s, value):
-        if value is not None:
-            (e, h, a, b)[f][c, Z0 + z, s] = value
-            live.add((f, c, z, s))
-
+
+
+def far_kernel(
+    live, e_in, h_in, a_in, b_in, coef_in, own, seen_in, tables, high, low, ghosts, f1, f0, weights,
+    e_out, h_out, p_out, s_out,
+    e, h, a, b, coef, seen, far, spectrum, sems,
+):
+    above_first = lax.rem(lax.axis_index("grp"), 2) == 0
+    for i in range(FAR_TILES):
+        x, y = f0[i], f1[i]
+        far[0, i] = jnp.where(above_first, x, y)
+        far[1, i] = jnp.where(above_first, y, x)
+    columns = [(z, 1, far[1 if z < 0 else 0, 7, :, 0:LANES], z % N) for z in (*range(-4, 0), *range(N, N + 3))]
+    fill_coefficients(coef, columns, tables)
+    polar = [wide(tables[16 + j]) for j in range(3)]
+    places = {"own": own, "far": far, "high": high, "low": low, "ghosts": ghosts}
+    run = Pass(True, live, [(e_in, h_in, a_in, b_in), (e, h, a, b)], [coef_in, coef], polar, places, sublane((N, NY)))
+    for field, n, last, made in ((0, STEPS, a, a_in), (1, STEPS - 1, b, b_in), ("e", STEPS, e, e_in), ("h", STEPS, h, h_in)):
+        for c in range(3):
+            for z in range(N):
+                if (c, z, 0) not in LATE[("h" if field == "h" else "e", n)]:
+                    last[c, Z0 + z, 0] = made[c, Z0 + z, 0]
     outs = []
     for n in range(1, STEPS + 1):
-        old, new = (2, 3) if n % 2 == 1 else (3, 2)
         for z in range(-4, N + 3):
-            todo = {(c, s) for c, at, s in need_h[n] if at == z}
-            ey = [get(0, 1, z, s) for s in range(2)]
-            ez = [get(0, 2, z, s) for s in range(2)]
-            xa_y = xa_z = (None, None)
-            if todo:
-                xa_y = across(ey, x_up, top, x_source("xeh", n - 1, 0, z), x_source("xe", n - 1, 0, z))
-                xa_z = across(ez, x_up, top, x_source("xeh", n - 1, 1, z), x_source("xe", n - 1, 1, z))
-            for s in range(2):
-                if not any((c, s) in todo for c in range(3)):
-                    continue
-                k = [wide(coef[j, Z0 + z, s]) for j in range(2)]
-                ex = get(0, 0, z, s)
-                e1x = add(get(0, 0, z + 1, s), z_source("ze", n - 1, 0, z + 1, s))
-                e1y = add(get(0, 1, z + 1, s), z_source("ze", n - 1, 1, z + 1, s))
-                curls = (
-                    lambda: sub(sub(y_ahead(ez[s]), ez[s]), sub(e1y, ey[s])),
-                    lambda: sub(sub(e1x, ex), sub(xa_z[s], ez[s])),
-                    lambda: sub(sub(xa_y[s], ey[s]), sub(y_ahead(ex), ex)),
-                )
-                for c in range(3):
-                    if (c, s) in todo:
-                        put(1, c, z, s, sub(mul(k[0], get(1, c, z, s)), mul(k[1], curls[c]())))
-            todo = {(c, s) for c, at, s in need_e[n] if at == z}
-            if not todo:
-                continue
-            hy = [get(1, 1, z, s) for s in range(2)]
-            hz = [get(1, 2, z, s) for s in range(2)]
-            xb_y = across(hy, x_down, bottom, x_source("xhl", n, 0, z), x_source("xh", n, 0, z))
-            xb_z = across(hz, x_down, bottom, x_source("xhl", n, 1, z), x_source("xh", n, 1, z))
-            for s in range(2):
-                if not any((c, s) in todo for c in range(3)):
-                    continue
-                k = [wide(coef[j, Z0 + z, s]) for j in range(5)]
-                hx = get(1, 0, z, s)
-                lx = add(get(1, 0, z - 1, s), z_source("zh", n, 0, z - 1, s))
-                ly = add(get(1, 1, z - 1, s), z_source("zh", n, 1, z - 1, s))
-                curls = (
-                    lambda: sub(sub(hz[s], y_behind(hz[s])), sub(hy[s], ly)),
-                    lambda: sub(sub(hx, lx), sub(hz[s], xb_z[s])),
-                    lambda: sub(sub(hy[s], xb_y[s]), sub(hx, y_behind(hx))),
-                )
-                for c in range(3):
-                    if (c, s) in todo:
-                        e_new, p_new = e_update(
-                            curls[c](), get(0, c, z, s), get(old, c, z, s), get(new, c, z, s), k, polar
-                        )
-                        put(0, c, z, s, e_new)
-                        if n < STEPS or s == 0:
-                            put(new, c, z, s, p_new)
-            if z == N // 2:
-                for c in range(3):
-                    seen[n - 1, c] = e[c, Z0 + z, 0]
-            if n == STEPS:
+            run.row(n, z, seen)
+            if n == STEPS and 0 <= z < N:
                 at = Z0 + z
                 outs += start_all(
                     [
@@ -492,18 +582,20 @@
                         (a.at[:, at, 0], p_out.at[0, :, z]),
                         (b.at[:, at, 0], p_out.at[1, :, z]),
                     ],
-                    sems.at[pl.ds(8 + 4 * z, 4)],
+                    sems.at[pl.ds(4 * z, 4)],
                 )
                 if z == N // 2:
                     for c in range(3):
-                        planes = [seen[i, c] for i in range(STEPS)]
+                        planes = [
+                            (seen if (c, z, 0) in LATE[("e", i + 1)] else seen_in)[i, c] for i in range(STEPS)
+                        ]
                         for f in range(FREQS):
                             for q in range(2):
                                 total = weights[0, f, q] * planes[0]
                                 for i in range(1, STEPS):
                                     total = total + weights[i, f, q] * planes[i]
                                 spectrum[f, q, c, 0] = total
-                    outs += start_all([(spectrum, s_out)], sems.at[pl.ds(40, 1)])
+                    outs += start_all([(spectrum, s_out)], sems.at[pl.ds(4 * N, 1)])
     wait_all(outs)
 
 
@@ -540,12 +632,12 @@
     plane = (2 * STEPS, N, NY)
     return pl.pallas_call(
         alone_kernel,
-        out_shape=[f32(X_TILES, N, NY)] * 2 + [f32(OWN_TILES, N, NY)] * 2,
+        out_shape=[f32(X_TILES, N, NY)] * 2 + [f32(OWN_TILES, N, NY)] * 2 + [f32(5, N, N, LANES), f32(19, N, LANES)],
         in_specs=[HBM] * 7,
-        out_specs=[VMEM] * 4,
+        out_specs=[VMEM] * 6,
         scratch_shapes=[vmem(3, N, N, NY)] * 4
         + [vmem(*plane)] * 4
-        + [vmem(4, 4, N, NY), vmem(5, N, N, LANES)]
+        + [vmem(4, 4, N, NY)]
         + small_tables()
         + [pltpu.SemaphoreType.DMA((8,))],
         compiler_params=params(),
@@ -553,7 +645,7 @@
     )(*inputs)
 
 
-def call_forward(r0, r1):
+def call_forward(r1, r0):
     return pl.pallas_call(
         forward_kernel,
         out_shape=[f32(FAR_TILES, N, NY)] * 2 + [f32(X_TILES, N, NY)] * 2 + [f32(7, N, NY)],
@@ -562,43 +654,59 @@
         scratch_shapes=[vmem(2, FAR_TILES, N, NY)],
         compiler_params=params(),
         name="forward",
-    )(r0, r1)
-
-
-def call_together(inputs, received, weights):
+    )(r1, r0)
+
+
+def call_near(live, fields, coef, tables, received):
+    state = f32(3, ROWS, 2, N, NY)
     return pl.pallas_call(
-        together_kernel,
+        functools.partial(near_kernel, live),
+        out_shape=[state] * 4
+        + [f32(5, ROWS, 2, N, LANES), f32(2, OWN_TILES, N, NY), f32(STEPS, 3, N, NY)],
+        in_specs=[HBM] * 3 + [VMEM] * 7,
+        out_specs=[VMEM] * 7,
+        scratch_shapes=[pltpu.SemaphoreType.DMA((4,))],
+        compiler_params=params(),
+        cost_estimate=pl.CostEstimate(flops=20_000_000, bytes_accessed=20_000_000, transcendentals=0),
+        name="near",
+    )(*fields, coef, tables, *received)
+
+
+def call_far(live, state, tables, received, weights):
+    return pl.pallas_call(
+        functools.partial(far_kernel, live),
         out_shape=[f32(3, N, N, NY), f32(3, N, N, NY), f32(2, 3, N, N, NY), f32(FREQS, 2, 3, 1, N, NY)],
-        in_specs=[HBM] * 7 + [VMEM] * 7 + [SMEM],
+        in_specs=[VMEM] * 13 + [SMEM],
         out_specs=[HBM] * 4,
         scratch_shapes=[vmem(3, ROWS, 2, N, NY)] * 4
         + [
-            vmem(2, OWN_TILES, N, NY),
-            vmem(2, FAR_TILES, N, NY),
             vmem(5, ROWS, 2, N, LANES),
             vmem(STEPS, 3, N, NY),
+            vmem(2, FAR_TILES, N, NY),
             vmem(FREQS, 2, 3, 1, N, NY),
-        ]
-        + small_tables()
-        + [pltpu.SemaphoreType.DMA((41,))],
+            pltpu.SemaphoreType.DMA((4 * N + 1,)),
+        ],
         compiler_params=params(),
-        name="together",
-    )(*inputs, *received, weights)
+        name="far",
+    )(*state, tables, *received, weights)
 
 
 def on_device(e_field, h_field, polar, material, eps_table, loss_table, lorentz, freqs):
     inputs = (e_field, h_field, polar, material, eps_table, loss_table, lorentz)
-    m0, m1, w0, w1 = call_alone(inputs)
+    inputs = tuple(pltpu.with_memory_space_constraint(x, pltpu.HBM) for x in inputs)
+    m0, m1, w0, w1, coef, tables = call_alone(inputs)
     r1 = swap(m1, "dev", 1)
     r0 = swap(m0, "dev", 0)
     g1 = swap(w1, "grp", 1)
     g0 = swap(w0, "grp", 0)
-    v0, v1, high, low, ghosts = call_forward(r0, r1)
+    v1, v0, high, low, ghosts = call_forward(r1, r0)
     f1 = swap(v1, "grp", 1)
     f0 = swap(v0, "grp", 0)
     angles = freqs * jnp.arange(1, STEPS + 1, dtype=jnp.float32)[:, None]
     weights = jnp.stack([jnp.cos(angles), -jnp.sin(angles)], axis=2)
-    return tuple(call_together(inputs, (high, low, ghosts, g0, g1, f0, f1), weights))
+    live = {}
+    state = call_near(live, inputs[:3], coef, tables, (high, low, ghosts, g1, g0))
+    return tuple(call_far(live, state, tables, (high, low, ghosts, f1, f0), weights))
 
 
 def solution(mesh):

time: 47 us -> 36 us (0.77)
  the two profiles are of different devices: /device:TPU:264 before, /device:TPU:249 now
where the time goes in v3:
time: 36 us; the launch traced here: 35.7 us
  starting transfers between devices  21.8 us (61%)
  Pallas kernels  11.9 us (33%)
  waiting for transfers between devices  0.92 us (3%)
  between operations  0.75 us (2%)
    ppermute x6, starting transfers between devices, swap(): return lax.ppermute(block, axis, route)  21.8 us
    pallas_call x1, Pallas kernels, call_far(): pl.pallas_call(functools.partial(far_kernel, live), out_shape=[f32(3, N,...  4.53 us
    pallas_call x1, Pallas kernels, call_alone(): pl.pallas_call(alone_kernel, out_shape=[f32(X_TILES, N, NY)] * 2 + [f32(O...  3.65 us
    pallas_call x1, Pallas kernels, call_near(): pl.pallas_call(functools.partial(near_kernel, live), out_shape=[state] *...  3.56 us
    ppermute x6, waiting for transfers between devices, swap(): return lax.ppermute(block, axis, route)  0.92 us
  transfers between devices with their start and end apart: 6, of which 1 were waited for; matrix products, arithmetic and copies ran while one was open for 1% of the time, Pallas kernels for 11%

profile of v3, /device:TPU:249, one launch (start us, length us, event | category | flops | bytes accessed | tf_op | source)
XLA Modules:
  0.0 35.7 jit_solution(13758767206172843715)
XLA Ops:
  0.6 0.0 copy-start
  0.6 3.6 %alone.1 = (f32[13,8,640]{2,1,0:T(8,128)S(1)}, f32[13,8,640]{2,1,0:T(8,128)S(1)}, f32[12,8,640]{2,1,0:T(8,128)S(1)}, f32[12,8,640]{2,1,0:T(8,128)S(1)}, f32[5,8,...) custom-call(f32[3,8,8,640]{3,2,1,0:T(8,128)} %e_hbm.3, f32[3,8,8,640]{3,2,1,0:T(8,128)} %h_hbm.3, ...), custom_call_target="tpu_custom_call" | custom-call | tf_op jit(solution)/shard_map/alone/pallas_call | solution.py:633
  4.3 6.0 %collective-permute-start = (f32[13,8,640]{2,1,0:T(8,128)S(1)}, f32[13,8,640]{2,1,0:T(8,128)S(1)}, u32[]{:S(2)}, u32[]{:S(2)}) collective-permute-start(f32[13,8,640]{2,1,0:T(8,128)S(1)} %get-tuple-element.24), channel_id=1, source_target_pairs={{1,2},{2,1},{3,4},{4,3},{5,6},{6,5},{7,8},{8,7},{9,10},{10,9},{11,... | collective-permute-start | bytes 798728 | tf_op jit(solution)/shard_map/ppermute | solution.py:628
  10.3 1.9 %collective-permute-start.1 = (f32[13,8,640]{2,1,0:T(8,128)S(1)}, f32[13,8,640]{2,1,0:T(8,128)S(1)}, u32[]{:S(2)}, u32[]{:S(2)}) collective-permute-start(f32[13,8,640]{2,1,0:T(8,128)S(1)} %get-tuple-element.25), channel_id=1, source_target_pairs={{0,1},{1,0},{2,3},{3,2},{4,5},{5,4},{6,7},{7,6},{8,9},{9,8},{10,11... | collective-permute-start | bytes 798728 | tf_op jit(solution)/shard_map/ppermute | solution.py:628
  12.2 4.3 %collective-permute-start.2 = (f32[12,8,640]{2,1,0:T(8,128)S(1)}, f32[12,8,640]{2,1,0:T(8,128)S(1)}, u32[]{:S(2)}, u32[]{:S(2)}) collective-permute-start(f32[12,8,640]{2,1,0:T(8,128)S(1)} %get-tuple-element.29), channel_id=1, source_target_pairs={{64,128},{128,64},{192,256},{256,192},{320,384},{384,320},{65,129}... | collective-permute-start | bytes 737288 | tf_op jit(solution)/shard_map/ppermute | solution.py:628
  16.5 2.0 %collective-permute-start.3 = (f32[12,8,640]{2,1,0:T(8,128)S(1)}, f32[12,8,640]{2,1,0:T(8,128)S(1)}, u32[]{:S(2)}, u32[]{:S(2)}) collective-permute-start(f32[12,8,640]{2,1,0:T(8,128)S(1)} %get-tuple-element.30), channel_id=1, source_target_pairs={{0,64},{64,0},{128,192},{192,128},{256,320},{320,256},{384,448},{4... | collective-permute-start | bytes 737288 | tf_op jit(solution)/shard_map/ppermute | solution.py:628
  18.5 0.0 collective-permute-done.r1
  18.5 0.0 collective-permute-done.1.r0
  18.5 0.2 forward.1
  18.7 5.8 %collective-permute-start.4 = (f32[8,8,640]{2,1,0:T(8,128)S(1)}, f32[8,8,640]{2,1,0:T(8,128)S(1)}, u32[]{:S(2)}, u32[]{:S(2)}) collective-permute-start(f32[8,8,640]{2,1,0:T(8,128)S(1)} %get-tuple-element.38), channel_id=1, source_target_pairs={{64,128},{128,64},{192,256},{256,192},{320,384},{384,320},{65,129}... | collective-permute-start | bytes 491528 | tf_op jit(solution)/shard_map/ppermute | solution.py:628
  24.5 1.9 %collective-permute-start.5 = (f32[8,8,640]{2,1,0:T(8,128)S(1)}, f32[8,8,640]{2,1,0:T(8,128)S(1)}, u32[]{:S(2)}, u32[]{:S(2)}) collective-permute-start(f32[8,8,640]{2,1,0:T(8,128)S(1)} %get-tuple-element.39), channel_id=1, source_target_pairs={{0,64},{64,0},{128,192},{192,128},{256,320},{320,256},{384,448},{4... | collective-permute-start | bytes 491528 | tf_op jit(solution)/shard_map/ppermute | solution.py:628
  26.4 0.0 copy-done
  26.4 0.1 multiply_cosine_fusion
  26.6 0.1 pad_maximum_fusion.weights
  26.6 0.0 collective-permute-done.2.g1
  26.6 0.0 collective-permute-done.3.g0
  26.7 3.6 %near.1 = (f32[3,17,2,8,640]{4,3,2,1,0:T(8,128)S(1)}, f32[3,17,2,8,640]{4,3,2,1,0:T(8,128)S(1)}, f32[3,17,2,8,640]{4,3,2,1,0:T(8,128)S(1)}, f32[3,17,2,8,640]{4,...) custom-call(f32[3,8,8,640]{3,2,1,0:T(8,128)} %e_hbm.3, ...), custom_call_target="tpu_custom_call" | custom-call | flops 20000000 | bytes 20000000 | tf_op jit(solution)/shard_map/near/pallas_call | solution.py:662
  30.2 0.0 collective-permute-done.4.f1
  30.2 0.9 %collective-permute-done.5.f0 = f32[8,8,640]{2,1,0:T(8,128)S(1)} collective-permute-done((f32[8,8,640]{2,1,0:T(8,128)S(1)}, f32[8,8,640]{2,1,0:T(8,128)S(1)}, u32[]{:S(2)}, u32[]{:S(2)}) %collective-permute-start.5) | collective-permute-done | bytes 163872 | tf_op jit(solution)/shard_map/ppermute | solution.py:628
  31.1 4.5 %far.1 = (f32[3,8,8,640]{3,2,1,0:T(8,128)}, f32[3,8,8,640]{3,2,1,0:T(8,128)}, f32[2,3,8,8,640]{4,3,2,1,0:T(8,128)}, f32[4,2,3,1,8,640]{5,4,3,2,1,0:T(8,128)}) custom-call(f32[3,17,2,8,640]{4,3,2,1,0:T(8,128)S(1)} %get-tuple-element.31.e_in, f32[3,17,2,8,640]{4,3,2,1,0:T(8,128)S(1)} %get-tuple-element.32.h_in, ...), custom_call_target="tpu_custom_call" | custom-call | tf_op jit(solution)/shard_map/far/pallas_call | solution.py:676
  (1 shorter events, 0.0 us)
Async XLA Ops:
  0.6 25.8 %copy-start = (f32[4]{0:T(128)S(1)}, f32[4]{0:T(128)}, u32[]{:S(2)}) copy-start(f32[4]{0:T(128)} %param.15) | copy-start | bytes 52
  4.3 14.2 %collective-permute-start = (f32[13,8,640]{2,1,0:T(8,128)S(1)}, f32[13,8,640]{2,1,0:T(8,128)S(1)}, u32[]{:S(2)}, u32[]{:S(2)}) collective-permute-start(f32[13,8,640]{2,1,0:T(8,128)S(1)} %get-tuple-element.24), channel_id=1, source_target_pairs={{1,2},{2,1},{3,4},{4,3},{5,6},{6,5},{7,8},{8,7},{9,10},{10,9},{11,... | collective-permute-start | bytes 798728 | tf_op jit(solution)/shard_map/ppermute | solution.py:628
  10.3 8.2 %collective-permute-start.1 = (f32[13,8,640]{2,1,0:T(8,128)S(1)}, f32[13,8,640]{2,1,0:T(8,128)S(1)}, u32[]{:S(2)}, u32[]{:S(2)}) collective-permute-start(f32[13,8,640]{2,1,0:T(8,128)S(1)} %get-tuple-element.25), channel_id=1, source_target_pairs={{0,1},{1,0},{2,3},{3,2},{4,5},{5,4},{6,7},{7,6},{8,9},{9,8},{10,11... | collective-permute-start | bytes 798728 | tf_op jit(solution)/shard_map/ppermute | solution.py:628
  12.2 14.4 %collective-permute-start.2 = (f32[12,8,640]{2,1,0:T(8,128)S(1)}, f32[12,8,640]{2,1,0:T(8,128)S(1)}, u32[]{:S(2)}, u32[]{:S(2)}) collective-permute-start(f32[12,8,640]{2,1,0:T(8,128)S(1)} %get-tuple-element.29), channel_id=1, source_target_pairs={{64,128},{128,64},{192,256},{256,192},{320,384},{384,320},{65,129}... | collective-permute-start | bytes 737288 | tf_op jit(solution)/shard_map/ppermute | solution.py:628
  16.5 10.1 %collective-permute-start.3 = (f32[12,8,640]{2,1,0:T(8,128)S(1)}, f32[12,8,640]{2,1,0:T(8,128)S(1)}, u32[]{:S(2)}, u32[]{:S(2)}) collective-permute-start(f32[12,8,640]{2,1,0:T(8,128)S(1)} %get-tuple-element.30), channel_id=1, source_target_pairs={{0,64},{64,0},{128,192},{192,128},{256,320},{320,256},{384,448},{4... | collective-permute-start | bytes 737288 | tf_op jit(solution)/shard_map/ppermute | solution.py:628
  18.7 11.5 %collective-permute-start.4 = (f32[8,8,640]{2,1,0:T(8,128)S(1)}, f32[8,8,640]{2,1,0:T(8,128)S(1)}, u32[]{:S(2)}, u32[]{:S(2)}) collective-permute-start(f32[8,8,640]{2,1,0:T(8,128)S(1)} %get-tuple-element.38), channel_id=1, source_target_pairs={{64,128},{128,64},{192,256},{256,192},{320,384},{384,320},{65,129}... | collective-permute-start | bytes 491528 | tf_op jit(solution)/shard_map/ppermute | solution.py:628
  24.5 6.6 %collective-permute-start.5 = (f32[8,8,640]{2,1,0:T(8,128)S(1)}, f32[8,8,640]{2,1,0:T(8,128)S(1)}, u32[]{:S(2)}, u32[]{:S(2)}) collective-permute-start(f32[8,8,640]{2,1,0:T(8,128)S(1)} %get-tuple-element.39), channel_id=1, source_target_pairs={{0,64},{64,0},{128,192},{192,128},{256,320},{320,256},{384,448},{4... | collective-permute-start | bytes 491528 | tf_op jit(solution)/shard_map/ppermute | solution.py:628

commit v4 on v3

--- a/solution.py
+++ b/solution.py
@@ -18,34 +18,52 @@
 ROWS = 17
 Z0 = 5
 
-X_TILES = 13
+X_TILES = 12
 OWN_TILES = 12
-FAR_TILES = 8
-
-
-def ladder(first, count, start, way):
-    return [(first + i, start + way * j) for i in range(count) for j in range(count - i)]
-
-
-def ray_rows(entries, tile):
-    out = {}
-    for c in range(2):
-        for kind, n, place in entries:
-            k = len(out)
-            out[(kind, n, c, place)] = (tile + k // 8, k % 8)
-    return out
-
-
-def named(kind, pairs):
-    return [(kind, n, place) for n, place in pairs]
-
-
-HX = ray_rows(named("ze", ladder(0, 3, 0, 1)) + named("zh", ladder(1, 3, 0, 1)), 8)
-LX = ray_rows(named("ze", ladder(0, 4, 7, -1)) + named("zh", ladder(1, 3, 7, -1)), 8)
-HZ = ray_rows(named("xe", ladder(0, 3, 0, 1)) + named("xh", ladder(1, 2, 0, 1)), 9)
-LZ = ray_rows(named("xe", ladder(0, 3, 7, -1)) + named("xh", ladder(1, 3, 7, -1)), 9)
-HF = ray_rows(named("xhl", ladder(1, 3, 0, 1)) + named("xeh", ladder(0, 3, 0, 1)), 4)
-LF = ray_rows(named("xhl", ladder(1, 3, 7, -1)) + named("xeh", ladder(0, 4, 7, -1)), 3)
+FAR_TILES = 7
+
+
+def ladder(kind, c, first, count, start, way):
+    return [(kind, first + i, c, start + way * j) for i in range(count) for j in range(count - i)]
+
+
+def materials(places):
+    return [("mat", 0, 0, x) for x in places]
+
+
+def ray_rows(entries, tile, spare=()):
+    free = [*spare, *((tile + k // N, k % N) for k in range(len(entries)))]
+    return dict(zip(entries, free))
+
+
+HIGH = (0, 1, 2)
+LOW = (4, 5, 6, 7)
+HX = ray_rows(
+    ladder("ze", 0, 0, 3, 0, 1) + ladder("ze", 1, 0, 3, 0, 1) + ladder("zh", 0, 1, 3, 0, 1) + ladder("zh", 1, 1, 2, 0, 1) + materials(HIGH),
+    8,
+)
+LX = ray_rows(
+    ladder("ze", 0, 0, 4, 7, -1) + ladder("ze", 1, 0, 3, 7, -1) + ladder("zh", 0, 1, 3, 7, -1) + ladder("zh", 1, 1, 3, 7, -1) + materials(LOW),
+    8,
+)
+HZ = ray_rows(
+    ladder("xe", 0, 0, 3, 0, 1) + ladder("xe", 1, 0, 3, 0, 1) + ladder("xh", 0, 1, 2, 0, 1) + ladder("xh", 1, 1, 2, 0, 1), 9
+)
+LZ = ray_rows(
+    ladder("xe", 0, 0, 3, 7, -1) + ladder("xe", 1, 0, 3, 7, -1) + ladder("xh", 0, 1, 3, 7, -1) + ladder("xh", 1, 1, 2, 7, -1), 9
+)
+HF = ray_rows(
+    ladder("xhl", 0, 1, 2, 0, 1) + ladder("xhl", 1, 1, 3, 0, 1) + ladder("xeh", 0, 0, 3, 0, 1) + ladder("xeh", 1, 0, 3, 0, 1)
+    + materials(HIGH + LOW),
+    4,
+    ((1, 3), (1, 4), (3, 2), (3, 5)),
+)
+LF = ray_rows(
+    ladder("xhl", 0, 1, 3, 7, -1) + ladder("xhl", 1, 1, 3, 7, -1) + ladder("xeh", 0, 0, 3, 7, -1) + ladder("xeh", 1, 0, 4, 7, -1)
+    + materials(HIGH + LOW),
+    3,
+    ((1, 2), (1, 4), (2, 5)),
+)
 
 
 def ghost_place(kind, n, c, x):
@@ -214,11 +232,9 @@
         for j, v in enumerate(row_coefficients(kind, tables)):
             coef[j, z] = v
     packed = wide(packed)
-    m0[12] = packed
-    m1[12] = packed
     w0[8] = packed
     w1[8] = packed
-    wait_all(large)
+    wait_all(large[:2])
     row = sublane((N, NY))
     top = row == N - 1
     bottom = row == 0
@@ -246,23 +262,31 @@
             r = slot_h(n, 0)
             xh[z, r : r + 1, :] = hy[N - 1 : N, :]
             xh[z, r + 1 : r + 2, :] = hz[N - 1 : N, :]
-            if n < STEPS:
-                lx, ly = (h[c, z - 1] if z else None for c in range(2))
-                xb_y = choose(bottom, None, x_down(hy))
-                xb_z = choose(bottom, None, x_down(hz))
-                curls = (
-                    (hz - y_behind(hz)) - sub(hy, ly),
-                    sub(hx, lx) - (hz - xb_z),
-                    (hy - xb_y) - (hx - y_behind(hx)),
-                )
-                for c, (curl, field) in enumerate(zip(curls, (ex, ey, ez))):
-                    e[c, z], new[c, z] = e_update(curl, field, old[c, z], new[c, z], k, polar)
+        if n == 1:
+            wait_all(large[2:])
+        for z in range(N if n < STEPS else 0):
+            k = [wide(coef[j, z]) for j in range(5)]
+            ex, ey, ez = (e[c, z] for c in range(3))
+            hx, hy, hz = (h[c, z] for c in range(3))
+            lx, ly = (h[c, z - 1] if z else None for c in range(2))
+            xb_y = choose(bottom, None, x_down(hy))
+            xb_z = choose(bottom, None, x_down(hz))
+            curls = (
+                (hz - y_behind(hz)) - sub(hy, ly),
+                sub(hx, lx) - (hz - xb_z),
+                (hy - xb_y) - (hx - y_behind(hx)),
+            )
+            for c, (curl, field) in enumerate(zip(curls, (ex, ey, ez))):
+                e[c, z], new[c, z] = e_update(curl, field, old[c, z], new[c, z], k, polar)
         for c in range(2):
             zh[slot_h(n, c)] = h[c, N - 1]
 
     for i, table in enumerate((HX, LX)):
         for (kind, n, c, x), (tile, r) in table.items():
-            source = ze.at[slot_e(n, c)] if kind == "ze" else zh.at[slot_h(n, c)]
+            if kind == "mat":
+                source = w0.at[8]
+            else:
+                source = ze.at[slot_e(n, c)] if kind == "ze" else zh.at[slot_h(n, c)]
             rays[i, tile - 8, r : r + 1, :] = source[x : x + 1, :]
     for i, table in enumerate((HZ, LZ)):
         for (kind, n, c, z), (tile, r) in table.items():
@@ -290,20 +314,22 @@
         one, other = r0[i], r1[i]
         high[i] = jnp.where(high_first, one, other)
         low[i] = jnp.where(high_first, other, one)
-    row = sublane((N, NY))
-    packed = jnp.where(row < 3, high[12], jnp.where(row > 3, low[12], 0.0))
-    rays[0, 7] = packed
-    rays[1, 7] = packed
-    for x, source, table in [(x, high, HX) for x in range(3)] + [(x, low, LX) for x in range(4, N)]:
-        for (kind, n, c, place), (tile, r) in table.items():
-            if place == x:
+    for source, table in ((high, HX), (low, LX)):
+        for (kind, n, c, x), (tile, r) in table.items():
+            value = source[tile, r : r + 1, :]
+            if kind == "mat":
+                for i, far in enumerate((HF, LF)):
+                    to, at = far[(kind, n, c, x)]
+                    rays[i, to, at : at + 1, :] = value
+            else:
                 to, at = ghost_place(kind, n, c, x)
-                rays[0 if kind == "ze" else 1, to, at : at + 1, :] = source[tile, r : r + 1, :]
+                rays[0 if kind == "ze" else 1, to, at : at + 1, :] = value
     for i, table in enumerate((HF, LF)):
         for (kind, n, c, z), (tile, r) in table.items():
-            at = slot_e(n, c) if kind == "xeh" else slot_h(n, c)
-            source = high if kind == "xeh" else low
-            rays[i, tile, r : r + 1, :] = source[z, at : at + 1, :]
+            if kind != "mat":
+                at = slot_e(n, c) if kind == "xeh" else slot_h(n, c)
+                source = high if kind == "xeh" else low
+                rays[i, tile, r : r + 1, :] = source[z, at : at + 1, :]
     for i in range(4):
         ghosts[i] = rays[0, i]
     for i in range(3):
@@ -342,13 +368,13 @@
 
 
 def z_source(kind, n, c, z, s):
-    if kind == "ze" and z == N:
-        return ("own", 0, slot_e(n, c)) if s == 0 else ("far", 0, kind, n, c)
-    if kind == "ze" and z == 0 and s == 1 and n < STEPS - 1:
-        return ("ghosts", kind, n, c)
-    if kind == "zh" and z == -1 and (s == 0 or n < STEPS):
-        return ("own", 1, slot_h(n, c)) if s == 0 else ("far", 1, kind, n, c)
-    if kind == "zh" and z == N - 1 and s == 1 and n < STEPS:
+    if s == 0:
+        if (kind, z) == ("ze", N):
+            return ("own", 0, slot_e(n, c))
+        return ("own", 1, slot_h(n, c)) if (kind, z) == ("zh", -1) else None
+    if (kind, z) in (("ze", N), ("zh", -1)) and any(k[:3] == (kind, n, c) for k in (*HX, *LX)):
+        return ("far", 0 if z == N else 1, kind, n, c)
+    if (kind, z) in (("ze", 0), ("zh", N - 1)) and n < STEPS - (kind == "ze") and (kind, n, c) != ("zh", STEPS - 1, 0):
         return ("ghosts", kind, n, c)
     return None
 
@@ -492,21 +518,21 @@
         if n < STEPS or s == 0:
             self.put(new, c, z, s, n, p_new)
 
-    def row(self, n, z, seen):
-        for field, step in (("h", self.step_h), ("e", self.step_e)):
-            for s in range(2):
-                for c in range(3):
-                    if (c, z, s) in NEED[(field, n)] and ((c, z, s) in LATE[(field, n)]) == self.second:
-                        step(n, c, z, s)
-                        if field == "e" and (c, z, s) == (c, N // 2, 0):
-                            seen[n - 1, c] = self.get("e", c, z, s, n)
+    def row(self, n, z, seen, field):
+        step = self.step_h if field == "h" else self.step_e
+        for s in range(2):
+            for c in range(3):
+                if (c, z, s) in NEED[(field, n)] and ((c, z, s) in LATE[(field, n)]) == self.second:
+                    step(n, c, z, s)
+                    if field == "e" and (z, s) == (N // 2, 0):
+                        seen[n - 1, c] = self.get("e", c, z, s, n)
         self.memo = {}
 
 
 def near_kernel(
     live, e_hbm, h_hbm, p_hbm, coef_in, tables, high, low, ghosts, g1, g0,
     e, h, a, b, coef, own, seen,
-    sems,
+    side, sems,
 ):
     above_first = lax.rem(lax.axis_index("grp"), 2) == 0
     mine = pl.ds(Z0, N)
@@ -523,9 +549,8 @@
         x, y = g0[i], g1[i]
         own[0, i] = jnp.where(above_first, x, y)
         own[1, i] = jnp.where(above_first, y, x)
-    narrow = sublane((N, LANES))
-    side = jnp.where(narrow < 3, high[12, :, 0:LANES], jnp.where(narrow > 3, low[12, :, 0:LANES], 0.0))
-    columns = [(z, 1, side, z) for z in range(N)]
+    ghost_materials(side, [(high, HX, HIGH), (low, LX, LOW)])
+    columns = [(z, 1, side[...], z) for z in range(N)]
     columns += [(z, 0, own[1 if z < 0 else 0, 8, :, 0:LANES], z % N) for z in (*range(-4, 0), *range(N, N + 3))]
     fill_coefficients(coef, columns, tables)
     for z in range(N):
@@ -538,7 +563,17 @@
     run = Pass(False, live, [(e, h, a, b)] * 2, [coef, None], polar, places, sublane((N, NY)))
     for n in range(1, STEPS + 1):
         for z in range(-4, N + 3):
-            run.row(n, z, seen)
+            run.row(n, z, seen, "h")
+        for z in range(-4, N + 3):
+            run.row(n, z, seen, "e")
+
+
+def ghost_materials(tile, found):
+    tile[...] = jnp.zeros((N, LANES), jnp.float32)
+    for source, table, places in found:
+        for x in places:
+            t, r = table[("mat", 0, 0, x)]
+            tile[x : x + 1, :] = source[t, r : r + 1, 0:LANES]
 
 
 def fill_coefficients(coef, columns, tables):
@@ -552,14 +587,16 @@
 def far_kernel(
     live, e_in, h_in, a_in, b_in, coef_in, own, seen_in, tables, high, low, ghosts, f1, f0, weights,
     e_out, h_out, p_out, s_out,
-    e, h, a, b, coef, seen, far, spectrum, sems,
+    e, h, a, b, coef, seen, far, corners, spectrum, sems,
 ):
     above_first = lax.rem(lax.axis_index("grp"), 2) == 0
     for i in range(FAR_TILES):
         x, y = f0[i], f1[i]
         far[0, i] = jnp.where(above_first, x, y)
         far[1, i] = jnp.where(above_first, y, x)
-    columns = [(z, 1, far[1 if z < 0 else 0, 7, :, 0:LANES], z % N) for z in (*range(-4, 0), *range(N, N + 3))]
+    for i, table in enumerate((HF, LF)):
+        ghost_materials(corners.at[i], [(far.at[i], table, HIGH + LOW)])
+    columns = [(z, 1, corners[1 if z < 0 else 0], z % N) for z in (*range(-4, 0), *range(N, N + 3))]
     fill_coefficients(coef, columns, tables)
     polar = [wide(tables[16 + j]) for j in range(3)]
     places = {"own": own, "far": far, "high": high, "low": low, "ghosts": ghosts}
@@ -571,19 +608,24 @@
                     last[c, Z0 + z, 0] = made[c, Z0 + z, 0]
     outs = []
     for n in range(1, STEPS + 1):
+        if n == STEPS:
+            outs += start_all([(b.at[:, pl.ds(Z0, N), 0], p_out.at[1])], sems.at[pl.ds(1, 1)])
         for z in range(-4, N + 3):
-            run.row(n, z, seen)
-            if n == STEPS and 0 <= z < N:
-                at = Z0 + z
-                outs += start_all(
-                    [
-                        (e.at[:, at, 0], e_out.at[:, z]),
-                        (h.at[:, at, 0], h_out.at[:, z]),
-                        (a.at[:, at, 0], p_out.at[0, :, z]),
-                        (b.at[:, at, 0], p_out.at[1, :, z]),
-                    ],
-                    sems.at[pl.ds(4 * z, 4)],
-                )
+            run.row(n, z, seen, "h")
+        if n == STEPS:
+            outs += start_all([(h.at[:, pl.ds(Z0, N), 0], h_out)], sems.at[pl.ds(0, 1)])
+            order = [*range(N // 2, N), *range(N // 2)]
+        else:
+            order = range(-4, N + 3)
+        for z in order:
+            run.row(n, z, seen, "e")
+            if n == STEPS:
+                if z % 4 == 3:
+                    at, to = pl.ds(Z0 + z - 3, 4), pl.ds(z - 3, 4)
+                    outs += start_all(
+                        [(e.at[:, at, 0], e_out.at[:, to]), (a.at[:, at, 0], p_out.at[0, :, to])],
+                        sems.at[pl.ds(3 + z // 4 * 2, 2)],
+                    )
                 if z == N // 2:
                     for c in range(3):
                         planes = [
@@ -591,11 +633,11 @@
                         ]
                         for f in range(FREQS):
                             for q in range(2):
-                                total = weights[0, f, q] * planes[0]
+                                total = wide(weights[2 * f + q]) * planes[0]
                                 for i in range(1, STEPS):
-                                    total = total + weights[i, f, q] * planes[i]
+                                    total = total + wide(weights[2 * FREQS * i + 2 * f + q]) * planes[i]
                                 spectrum[f, q, c, 0] = total
-                    outs += start_all([(spectrum, s_out)], sems.at[pl.ds(4 * N, 1)])
+                    outs += start_all([(spectrum, s_out)], sems.at[pl.ds(2, 1)])
     wait_all(outs)
 
 
@@ -665,7 +707,7 @@
         + [f32(5, ROWS, 2, N, LANES), f32(2, OWN_TILES, N, NY), f32(STEPS, 3, N, NY)],
         in_specs=[HBM] * 3 + [VMEM] * 7,
         out_specs=[VMEM] * 7,
-        scratch_shapes=[pltpu.SemaphoreType.DMA((4,))],
+        scratch_shapes=[vmem(N, LANES), pltpu.SemaphoreType.DMA((4,))],
         compiler_params=params(),
         cost_estimate=pl.CostEstimate(flops=20_000_000, bytes_accessed=20_000_000, transcendentals=0),
         name="near",
@@ -676,15 +718,16 @@
     return pl.pallas_call(
         functools.partial(far_kernel, live),
         out_shape=[f32(3, N, N, NY), f32(3, N, N, NY), f32(2, 3, N, N, NY), f32(FREQS, 2, 3, 1, N, NY)],
-        in_specs=[VMEM] * 13 + [SMEM],
+        in_specs=[VMEM] * 14,
         out_specs=[HBM] * 4,
         scratch_shapes=[vmem(3, ROWS, 2, N, NY)] * 4
         + [
             vmem(5, ROWS, 2, N, LANES),
             vmem(STEPS, 3, N, NY),
             vmem(2, FAR_TILES, N, NY),
+            vmem(2, N, LANES),
             vmem(FREQS, 2, 3, 1, N, NY),
-            pltpu.SemaphoreType.DMA((4 * N + 1,)),
+            pltpu.SemaphoreType.DMA((7,)),
         ],
         compiler_params=params(),
         name="far",
@@ -704,6 +747,7 @@
     f0 = swap(v0, "grp", 0)
     angles = freqs * jnp.arange(1, STEPS + 1, dtype=jnp.float32)[:, None]
     weights = jnp.stack([jnp.cos(angles), -jnp.sin(angles)], axis=2)
+    weights = jnp.broadcast_to(weights.reshape(-1, 1, 1), (2 * FREQS * STEPS, N, LANES))
     live = {}
     state = call_near(live, inputs[:3], coef, tables, (high, low, ghosts, g1, g0))
     return tuple(call_far(live, state, tables, (high, low, ghosts, f1, f0), weights))

time: 36 us -> 34.1 us (0.947)
  Pallas kernels: 11.9 us -> 10.2 us
  starting transfers between devices: 21.8 us -> 21.4 us
    pallas_call x1, Pallas kernels: 4.53 us -> 3.49 us  [call_far(): pl.pallas_call(functools.partial(far_kernel, live), out_shape=[f32(3, N,...]
    pallas_call x1, Pallas kernels: 3.65 us -> 3.17 us  [call_alone(): pl.pallas_call(alone_kernel, out_shape=[f32(X_TILES, N, NY)] * 2 + [f32(O...]
    ppermute x6, starting transfers between devices: 21.8 us -> 21.4 us  [swap(): return lax.ppermute(block, axis, route)]
  transfers between devices with their start and end apart: 6 -> 6, of which waited for: 1 -> 1; matrix products, arithmetic and copies ran while one was open for 1% -> 1% of each run, Pallas kernels for 11% -> 10%
where the time goes in v4:
time: 34.1 us; the launch traced here: 33.8 us
  starting transfers between devices  21.4 us (63%)
  Pallas kernels  10.2 us (30%)
  waiting for transfers between devices  1.03 us (3%)
  between operations  0.78 us (2%)
    ppermute x6, starting transfers between devices, swap(): return lax.ppermute(block, axis, route)  21.4 us
    pallas_call x1, Pallas kernels, call_far(): pl.pallas_call(functools.partial(far_kernel, live), out_shape=[f32(3, N,...  3.49 us
    pallas_call x1, Pallas kernels, call_near(): pl.pallas_call(functools.partial(near_kernel, live), out_shape=[state] *...  3.32 us
    pallas_call x1, Pallas kernels, call_alone(): pl.pallas_call(alone_kernel, out_shape=[f32(X_TILES, N, NY)] * 2 + [f32(O...  3.17 us
    ppermute x6, waiting for transfers between devices, swap(): return lax.ppermute(block, axis, route)  1.03 us
  transfers between devices with their start and end apart: 6, of which 1 were waited for; matrix products, arithmetic and copies ran while one was open for 1% of the time, Pallas kernels for 10%

profile of v4, /device:TPU:249, one launch (start us, length us, event | category | flops | bytes accessed | tf_op | source)
XLA Modules:
  0.0 33.8 jit_solution(5478102027113011261)
XLA Ops:
  0.6 0.0 copy-start
  0.6 3.2 %alone.1 = (f32[12,8,640]{2,1,0:T(8,128)S(1)}, f32[12,8,640]{2,1,0:T(8,128)S(1)}, f32[12,8,640]{2,1,0:T(8,128)S(1)}, f32[12,8,640]{2,1,0:T(8,128)S(1)}, f32[5,8,...) custom-call(f32[3,8,8,640]{3,2,1,0:T(8,128)} %e_hbm.3, f32[3,8,8,640]{3,2,1,0:T(8,128)} %h_hbm.3, ...), custom_call_target="tpu_custom_call" | custom-call | tf_op jit(solution)/shard_map/alone/pallas_call | solution.py:675
  3.8 6.0 %collective-permute-start = (f32[12,8,640]{2,1,0:T(8,128)S(1)}, f32[12,8,640]{2,1,0:T(8,128)S(1)}, u32[]{:S(2)}, u32[]{:S(2)}) collective-permute-start(f32[12,8,640]{2,1,0:T(8,128)S(1)} %get-tuple-element.24), channel_id=1, source_target_pairs={{1,2},{2,1},{3,4},{4,3},{5,6},{6,5},{7,8},{8,7},{9,10},{10,9},{11,... | collective-permute-start | bytes 737288 | tf_op jit(solution)/shard_map/ppermute | solution.py:670
  9.8 1.9 %collective-permute-start.1 = (f32[12,8,640]{2,1,0:T(8,128)S(1)}, f32[12,8,640]{2,1,0:T(8,128)S(1)}, u32[]{:S(2)}, u32[]{:S(2)}) collective-permute-start(f32[12,8,640]{2,1,0:T(8,128)S(1)} %get-tuple-element.25), channel_id=1, source_target_pairs={{0,1},{1,0},{2,3},{3,2},{4,5},{5,4},{6,7},{7,6},{8,9},{9,8},{10,11... | collective-permute-start | bytes 737288 | tf_op jit(solution)/shard_map/ppermute | solution.py:670
  11.7 4.3 %collective-permute-start.2 = (f32[12,8,640]{2,1,0:T(8,128)S(1)}, f32[12,8,640]{2,1,0:T(8,128)S(1)}, u32[]{:S(2)}, u32[]{:S(2)}) collective-permute-start(f32[12,8,640]{2,1,0:T(8,128)S(1)} %get-tuple-element.29), channel_id=1, source_target_pairs={{64,128},{128,64},{192,256},{256,192},{320,384},{384,320},{65,129}... | collective-permute-start | bytes 737288 | tf_op jit(solution)/shard_map/ppermute | solution.py:670
  16.0 2.0 %collective-permute-start.3 = (f32[12,8,640]{2,1,0:T(8,128)S(1)}, f32[12,8,640]{2,1,0:T(8,128)S(1)}, u32[]{:S(2)}, u32[]{:S(2)}) collective-permute-start(f32[12,8,640]{2,1,0:T(8,128)S(1)} %get-tuple-element.30), channel_id=1, source_target_pairs={{0,64},{64,0},{128,192},{192,128},{256,320},{320,256},{384,448},{4... | collective-permute-start | bytes 737288 | tf_op jit(solution)/shard_map/ppermute | solution.py:670
  18.0 0.0 collective-permute-done.r1
  18.0 0.0 collective-permute-done.1.r0
  18.0 0.2 forward.1
  18.2 5.3 %collective-permute-start.4 = (f32[7,8,640]{2,1,0:T(8,128)S(1)}, f32[7,8,640]{2,1,0:T(8,128)S(1)}, u32[]{:S(2)}, u32[]{:S(2)}) collective-permute-start(f32[7,8,640]{2,1,0:T(8,128)S(1)} %get-tuple-element.38), channel_id=1, source_target_pairs={{64,128},{128,64},{192,256},{256,192},{320,384},{384,320},{65,129}... | collective-permute-start | bytes 430088 | tf_op jit(solution)/shard_map/ppermute | solution.py:670
  23.6 1.9 %collective-permute-start.5 = (f32[7,8,640]{2,1,0:T(8,128)S(1)}, f32[7,8,640]{2,1,0:T(8,128)S(1)}, u32[]{:S(2)}, u32[]{:S(2)}) collective-permute-start(f32[7,8,640]{2,1,0:T(8,128)S(1)} %get-tuple-element.39), channel_id=1, source_target_pairs={{0,64},{64,0},{128,192},{192,128},{256,320},{320,256},{384,448},{4... | collective-permute-start | bytes 430088 | tf_op jit(solution)/shard_map/ppermute | solution.py:670
  25.5 0.0 copy-done
  25.5 0.1 multiply_cosine_fusion
  25.6 0.1 copy.12
  25.7 0.1 broadcast_in_dim.4
  25.8 0.0 collective-permute-done.2.g1
  25.8 0.0 collective-permute-done.3.g0
  25.8 3.3 %near.1 = (f32[3,17,2,8,640]{4,3,2,1,0:T(8,128)S(1)}, f32[3,17,2,8,640]{4,3,2,1,0:T(8,128)S(1)}, f32[3,17,2,8,640]{4,3,2,1,0:T(8,128)S(1)}, f32[3,17,2,8,640]{4,...) custom-call(f32[3,8,8,640]{3,2,1,0:T(8,128)} %e_hbm.3, ...), custom_call_target="tpu_custom_call" | custom-call | flops 20000000 | bytes 20000000 | tf_op jit(solution)/shard_map/near/pallas_call | solution.py:704
  29.2 0.0 collective-permute-done.4.f1
  29.2 1.0 %collective-permute-done.5.f0 = f32[7,8,640]{2,1,0:T(8,128)S(1)} collective-permute-done((f32[7,8,640]{2,1,0:T(8,128)S(1)}, f32[7,8,640]{2,1,0:T(8,128)S(1)}, u32[]{:S(2)}, u32[]{:S(2)}) %collective-permute-start.5) | collective-permute-done | bytes 143392 | tf_op jit(solution)/shard_map/ppermute | solution.py:670
  30.2 0.1 broadcast_in_dim.10.weights
  30.3 3.5 %far.1 = (f32[3,8,8,640]{3,2,1,0:T(8,128)}, f32[3,8,8,640]{3,2,1,0:T(8,128)}, f32[2,3,8,8,640]{4,3,2,1,0:T(8,128)}, f32[4,2,3,1,8,640]{5,4,3,2,1,0:T(8,128)}) custom-call(f32[3,17,2,8,640]{4,3,2,1,0:T(8,128)S(1)} %get-tuple-element.31.e_in, f32[3,17,2,8,640]{4,3,2,1,0:T(8,128)S(1)} %get-tuple-element.32.h_in, ...), custom_call_target="tpu_custom_call" | custom-call | tf_op jit(solution)/shard_map/far/pallas_call | solution.py:718
  (2 shorter events, 0.0 us)
Async XLA Ops:
  0.6 24.9 %copy-start = (f32[4]{0:T(128)S(1)}, f32[4]{0:T(128)}, u32[]{:S(2)}) copy-start(f32[4]{0:T(128)} %param.15) | copy-start | bytes 52
  3.8 14.2 %collective-permute-start = (f32[12,8,640]{2,1,0:T(8,128)S(1)}, f32[12,8,640]{2,1,0:T(8,128)S(1)}, u32[]{:S(2)}, u32[]{:S(2)}) collective-permute-start(f32[12,8,640]{2,1,0:T(8,128)S(1)} %get-tuple-element.24), channel_id=1, source_target_pairs={{1,2},{2,1},{3,4},{4,3},{5,6},{6,5},{7,8},{8,7},{9,10},{10,9},{11,... | collective-permute-start | bytes 737288 | tf_op jit(solution)/shard_map/ppermute | solution.py:670
  9.8 8.2 %collective-permute-start.1 = (f32[12,8,640]{2,1,0:T(8,128)S(1)}, f32[12,8,640]{2,1,0:T(8,128)S(1)}, u32[]{:S(2)}, u32[]{:S(2)}) collective-permute-start(f32[12,8,640]{2,1,0:T(8,128)S(1)} %get-tuple-element.25), channel_id=1, source_target_pairs={{0,1},{1,0},{2,3},{3,2},{4,5},{5,4},{6,7},{7,6},{8,9},{9,8},{10,11... | collective-permute-start | bytes 737288 | tf_op jit(solution)/shard_map/ppermute | solution.py:670
  11.7 14.1 %collective-permute-start.2 = (f32[12,8,640]{2,1,0:T(8,128)S(1)}, f32[12,8,640]{2,1,0:T(8,128)S(1)}, u32[]{:S(2)}, u32[]{:S(2)}) collective-permute-start(f32[12,8,640]{2,1,0:T(8,128)S(1)} %get-tuple-element.29), channel_id=1, source_target_pairs={{64,128},{128,64},{192,256},{256,192},{320,384},{384,320},{65,129}... | collective-permute-start | bytes 737288 | tf_op jit(solution)/shard_map/ppermute | solution.py:670
  16.0 9.8 %collective-permute-start.3 = (f32[12,8,640]{2,1,0:T(8,128)S(1)}, f32[12,8,640]{2,1,0:T(8,128)S(1)}, u32[]{:S(2)}, u32[]{:S(2)}) collective-permute-start(f32[12,8,640]{2,1,0:T(8,128)S(1)} %get-tuple-element.30), channel_id=1, source_target_pairs={{0,64},{64,0},{128,192},{192,128},{256,320},{320,256},{384,448},{4... | collective-permute-start | bytes 737288 | tf_op jit(solution)/shard_map/ppermute | solution.py:670
  18.2 11.0 %collective-permute-start.4 = (f32[7,8,640]{2,1,0:T(8,128)S(1)}, f32[7,8,640]{2,1,0:T(8,128)S(1)}, u32[]{:S(2)}, u32[]{:S(2)}) collective-permute-start(f32[7,8,640]{2,1,0:T(8,128)S(1)} %get-tuple-element.38), channel_id=1, source_target_pairs={{64,128},{128,64},{192,256},{256,192},{320,384},{384,320},{65,129}... | collective-permute-start | bytes 430088 | tf_op jit(solution)/shard_map/ppermute | solution.py:670
  23.6 6.6 %collective-permute-start.5 = (f32[7,8,640]{2,1,0:T(8,128)S(1)}, f32[7,8,640]{2,1,0:T(8,128)S(1)}, u32[]{:S(2)}, u32[]{:S(2)}) collective-permute-start(f32[7,8,640]{2,1,0:T(8,128)S(1)} %get-tuple-element.39), channel_id=1, source_target_pairs={{0,64},{64,0},{128,192},{192,128},{256,320},{320,256},{384,448},{4... | collective-permute-start | bytes 430088 | tf_op jit(solution)/shard_map/ppermute | solution.py:670

commit v5 on v4

--- a/solution.py
+++ b/solution.py
@@ -530,8 +530,8 @@
 
 
 def near_kernel(
-    live, e_hbm, h_hbm, p_hbm, coef_in, tables, high, low, ghosts, g1, g0,
-    e, h, a, b, coef, own, seen,
+    live, e_hbm, h_hbm, p_hbm, coef_in, tables, high, low, ghosts, g1, g0, weights,
+    e, h, a, b, coef, own, seen, tiles,
     side, sems,
 ):
     above_first = lax.rem(lax.axis_index("grp"), 2) == 0
@@ -545,6 +545,8 @@
         ],
         sems,
     )
+    for i in range(2 * FREQS * STEPS):
+        tiles[i] = jnp.broadcast_to(weights[0:1, i : i + 1], (N, LANES))
     for i in range(OWN_TILES):
         x, y = g0[i], g1[i]
         own[0, i] = jnp.where(above_first, x, y)
@@ -557,13 +559,15 @@
         for j in range(5):
             coef[j, Z0 + z, 0] = coef_in[j, z]
     polar = [wide(tables[16 + j]) for j in range(3)]
-    wait_all(large)
+    wait_all(large[:2])
     live.update({(field, c, z, 0): 0 for field in FIELDS for c in range(3) for z in range(N)})
     places = {"own": own, "high": high, "low": low, "ghosts": ghosts}
     run = Pass(False, live, [(e, h, a, b)] * 2, [coef, None], polar, places, sublane((N, NY)))
     for n in range(1, STEPS + 1):
         for z in range(-4, N + 3):
             run.row(n, z, seen, "h")
+        if n == 1:
+            wait_all(large[2:])
         for z in range(-4, N + 3):
             run.row(n, z, seen, "e")
 
@@ -699,19 +703,20 @@
     )(r1, r0)
 
 
-def call_near(live, fields, coef, tables, received):
+def call_near(live, fields, coef, tables, received, weights):
     state = f32(3, ROWS, 2, N, NY)
     return pl.pallas_call(
         functools.partial(near_kernel, live),
         out_shape=[state] * 4
-        + [f32(5, ROWS, 2, N, LANES), f32(2, OWN_TILES, N, NY), f32(STEPS, 3, N, NY)],
-        in_specs=[HBM] * 3 + [VMEM] * 7,
-        out_specs=[VMEM] * 7,
+        + [f32(5, ROWS, 2, N, LANES), f32(2, OWN_TILES, N, NY), f32(STEPS, 3, N, NY)]
+        + [f32(2 * FREQS * STEPS, N, LANES)],
+        in_specs=[HBM] * 3 + [VMEM] * 8,
+        out_specs=[VMEM] * 8,
         scratch_shapes=[vmem(N, LANES), pltpu.SemaphoreType.DMA((4,))],
         compiler_params=params(),
         cost_estimate=pl.CostEstimate(flops=20_000_000, bytes_accessed=20_000_000, transcendentals=0),
         name="near",
-    )(*fields, coef, tables, *received)
+    )(*fields, coef, tables, *received, weights)
 
 
 def call_far(live, state, tables, received, weights):
@@ -747,9 +752,9 @@
     f0 = swap(v0, "grp", 0)
     angles = freqs * jnp.arange(1, STEPS + 1, dtype=jnp.float32)[:, None]
     weights = jnp.stack([jnp.cos(angles), -jnp.sin(angles)], axis=2)
-    weights = jnp.broadcast_to(weights.reshape(-1, 1, 1), (2 * FREQS * STEPS, N, LANES))
+    weights = weights.reshape(1, 2 * FREQS * STEPS)
     live = {}
-    state = call_near(live, inputs[:3], coef, tables, (high, low, ghosts, g1, g0))
+    *state, weights = call_near(live, inputs[:3], coef, tables, (high, low, ghosts, g1, g0), weights)
     return tuple(call_far(live, state, tables, (high, low, ghosts, f1, f0), weights))
 
 

time: 34.1 us -> 34.1 us (level)
  no operation moved by 1% of the time
where the time goes in v5:
time: 34.1 us; the launch traced here: 33.8 us
  starting transfers between devices  21.4 us (63%)
  Pallas kernels  10.1 us (30%)
  waiting for transfers between devices  1.2 us (4%)
  between operations  0.77 us (2%)
    ppermute x6, starting transfers between devices, swap(): return lax.ppermute(block, axis, route)  21.4 us
    pallas_call x1, Pallas kernels, call_far(): pl.pallas_call(functools.partial(far_kernel, live), out_shape=[f32(3, N,...  3.57 us
    pallas_call x1, Pallas kernels, call_alone(): pl.pallas_call(alone_kernel, out_shape=[f32(X_TILES, N, NY)] * 2 + [f32(O...  3.17 us
    pallas_call x1, Pallas kernels, call_near(): pl.pallas_call(functools.partial(near_kernel, live), out_shape=[state] *...  3.15 us
    ppermute x6, waiting for transfers between devices, swap(): return lax.ppermute(block, axis, route)  1.2 us
  transfers between devices with their start and end apart: 6, of which 1 were waited for; matrix products, arithmetic and copies ran while one was open for 1% of the time, Pallas kernels for 10%

profile of v5, /device:TPU:249, one launch (start us, length us, event | category | flops | bytes accessed | tf_op | source)
XLA Modules:
  0.0 33.8 jit_solution(7904156846275079251)
XLA Ops:
  0.6 0.0 copy-start
  0.6 3.2 %alone.1 = (f32[12,8,640]{2,1,0:T(8,128)S(1)}, f32[12,8,640]{2,1,0:T(8,128)S(1)}, f32[12,8,640]{2,1,0:T(8,128)S(1)}, f32[12,8,640]{2,1,0:T(8,128)S(1)}, f32[5,8,...) custom-call(f32[3,8,8,640]{3,2,1,0:T(8,128)} %e_hbm.3, f32[3,8,8,640]{3,2,1,0:T(8,128)} %h_hbm.3, ...), custom_call_target="tpu_custom_call" | custom-call | tf_op jit(solution)/shard_map/alone/pallas_call | solution.py:679
  3.8 6.0 %collective-permute-start = (f32[12,8,640]{2,1,0:T(8,128)S(1)}, f32[12,8,640]{2,1,0:T(8,128)S(1)}, u32[]{:S(2)}, u32[]{:S(2)}) collective-permute-start(f32[12,8,640]{2,1,0:T(8,128)S(1)} %get-tuple-element.25), channel_id=1, source_target_pairs={{1,2},{2,1},{3,4},{4,3},{5,6},{6,5},{7,8},{8,7},{9,10},{10,9},{11,... | collective-permute-start | bytes 737288 | tf_op jit(solution)/shard_map/ppermute | solution.py:674
  9.8 1.9 %collective-permute-start.1 = (f32[12,8,640]{2,1,0:T(8,128)S(1)}, f32[12,8,640]{2,1,0:T(8,128)S(1)}, u32[]{:S(2)}, u32[]{:S(2)}) collective-permute-start(f32[12,8,640]{2,1,0:T(8,128)S(1)} %get-tuple-element.26), channel_id=1, source_target_pairs={{0,1},{1,0},{2,3},{3,2},{4,5},{5,4},{6,7},{7,6},{8,9},{9,8},{10,11... | collective-permute-start | bytes 737288 | tf_op jit(solution)/shard_map/ppermute | solution.py:674
  11.7 4.3 %collective-permute-start.2 = (f32[12,8,640]{2,1,0:T(8,128)S(1)}, f32[12,8,640]{2,1,0:T(8,128)S(1)}, u32[]{:S(2)}, u32[]{:S(2)}) collective-permute-start(f32[12,8,640]{2,1,0:T(8,128)S(1)} %get-tuple-element.30), channel_id=1, source_target_pairs={{64,128},{128,64},{192,256},{256,192},{320,384},{384,320},{65,129}... | collective-permute-start | bytes 737288 | tf_op jit(solution)/shard_map/ppermute | solution.py:674
  16.0 2.0 %collective-permute-start.3 = (f32[12,8,640]{2,1,0:T(8,128)S(1)}, f32[12,8,640]{2,1,0:T(8,128)S(1)}, u32[]{:S(2)}, u32[]{:S(2)}) collective-permute-start(f32[12,8,640]{2,1,0:T(8,128)S(1)} %get-tuple-element.31), channel_id=1, source_target_pairs={{0,64},{64,0},{128,192},{192,128},{256,320},{320,256},{384,448},{4... | collective-permute-start | bytes 737288 | tf_op jit(solution)/shard_map/ppermute | solution.py:674
  18.0 0.0 collective-permute-done.r1
  18.0 0.0 collective-permute-done.1.r0
  18.0 0.2 forward.1
  18.2 5.3 %collective-permute-start.4 = (f32[7,8,640]{2,1,0:T(8,128)S(1)}, f32[7,8,640]{2,1,0:T(8,128)S(1)}, u32[]{:S(2)}, u32[]{:S(2)}) collective-permute-start(f32[7,8,640]{2,1,0:T(8,128)S(1)} %get-tuple-element.39), channel_id=1, source_target_pairs={{64,128},{128,64},{192,256},{256,192},{320,384},{384,320},{65,129}... | collective-permute-start | bytes 430088 | tf_op jit(solution)/shard_map/ppermute | solution.py:674
  23.6 1.9 %collective-permute-start.5 = (f32[7,8,640]{2,1,0:T(8,128)S(1)}, f32[7,8,640]{2,1,0:T(8,128)S(1)}, u32[]{:S(2)}, u32[]{:S(2)}) collective-permute-start(f32[7,8,640]{2,1,0:T(8,128)S(1)} %get-tuple-element.40), channel_id=1, source_target_pairs={{0,64},{64,0},{128,192},{192,128},{256,320},{320,256},{384,448},{4... | collective-permute-start | bytes 430088 | tf_op jit(solution)/shard_map/ppermute | solution.py:674
  25.5 0.0 copy-done
  25.5 0.1 multiply_cosine_fusion
  25.6 0.1 copy.12
  25.7 0.1 reshape.103.weights
  25.8 0.0 collective-permute-done.2.g1
  25.8 0.0 collective-permute-done.3.g0
  25.8 3.1 %near.1 = (f32[3,17,2,8,640]{4,3,2,1,0:T(8,128)S(1)}, f32[3,17,2,8,640]{4,3,2,1,0:T(8,128)S(1)}, f32[3,17,2,8,640]{4,3,2,1,0:T(8,128)S(1)}, f32[3,17,2,8,640]{4,...) custom-call(f32[3,8,8,640]{3,2,1,0:T(8,128)} %e_hbm.3, ...), custom_call_target="tpu_custom_call" | custom-call | flops 20000000 | bytes 20000000 | tf_op jit(solution)/shard_map/near/pallas_call | solution.py:708
  29.0 0.0 collective-permute-done.4.f1
  29.0 1.2 %collective-permute-done.5.f0 = f32[7,8,640]{2,1,0:T(8,128)S(1)} collective-permute-done((f32[7,8,640]{2,1,0:T(8,128)S(1)}, f32[7,8,640]{2,1,0:T(8,128)S(1)}, u32[]{:S(2)}, u32[]{:S(2)}) %collective-permute-start.5) | collective-permute-done | bytes 143392 | tf_op jit(solution)/shard_map/ppermute | solution.py:674
  30.2 3.6 %far.1 = (f32[3,8,8,640]{3,2,1,0:T(8,128)}, f32[3,8,8,640]{3,2,1,0:T(8,128)}, f32[2,3,8,8,640]{4,3,2,1,0:T(8,128)}, f32[4,2,3,1,8,640]{5,4,3,2,1,0:T(8,128)}) custom-call(f32[3,17,2,8,640]{4,3,2,1,0:T(8,128)S(1)} %get-tuple-element.32.e_in, f32[3,17,2,8,640]{4,3,2,1,0:T(8,128)S(1)} %get-tuple-element.33.h_in, ...), custom_call_target="tpu_custom_call" | custom-call | tf_op jit(solution)/shard_map/far/pallas_call | solution.py:723
  (2 shorter events, 0.0 us)
Async XLA Ops:
  0.6 24.9 %copy-start = (f32[4]{0:T(128)S(1)}, f32[4]{0:T(128)}, u32[]{:S(2)}) copy-start(f32[4]{0:T(128)} %param.15) | copy-start | bytes 52
  3.8 14.2 %collective-permute-start = (f32[12,8,640]{2,1,0:T(8,128)S(1)}, f32[12,8,640]{2,1,0:T(8,128)S(1)}, u32[]{:S(2)}, u32[]{:S(2)}) collective-permute-start(f32[12,8,640]{2,1,0:T(8,128)S(1)} %get-tuple-element.25), channel_id=1, source_target_pairs={{1,2},{2,1},{3,4},{4,3},{5,6},{6,5},{7,8},{8,7},{9,10},{10,9},{11,... | collective-permute-start | bytes 737288 | tf_op jit(solution)/shard_map/ppermute | solution.py:674
  9.8 8.2 %collective-permute-start.1 = (f32[12,8,640]{2,1,0:T(8,128)S(1)}, f32[12,8,640]{2,1,0:T(8,128)S(1)}, u32[]{:S(2)}, u32[]{:S(2)}) collective-permute-start(f32[12,8,640]{2,1,0:T(8,128)S(1)} %get-tuple-element.26), channel_id=1, source_target_pairs={{0,1},{1,0},{2,3},{3,2},{4,5},{5,4},{6,7},{7,6},{8,9},{9,8},{10,11... | collective-permute-start | bytes 737288 | tf_op jit(solution)/shard_map/ppermute | solution.py:674
  11.7 14.1 %collective-permute-start.2 = (f32[12,8,640]{2,1,0:T(8,128)S(1)}, f32[12,8,640]{2,1,0:T(8,128)S(1)}, u32[]{:S(2)}, u32[]{:S(2)}) collective-permute-start(f32[12,8,640]{2,1,0:T(8,128)S(1)} %get-tuple-element.30), channel_id=1, source_target_pairs={{64,128},{128,64},{192,256},{256,192},{320,384},{384,320},{65,129}... | collective-permute-start | bytes 737288 | tf_op jit(solution)/shard_map/ppermute | solution.py:674
  16.0 9.8 %collective-permute-start.3 = (f32[12,8,640]{2,1,0:T(8,128)S(1)}, f32[12,8,640]{2,1,0:T(8,128)S(1)}, u32[]{:S(2)}, u32[]{:S(2)}) collective-permute-start(f32[12,8,640]{2,1,0:T(8,128)S(1)} %get-tuple-element.31), channel_id=1, source_target_pairs={{0,64},{64,0},{128,192},{192,128},{256,320},{320,256},{384,448},{4... | collective-permute-start | bytes 737288 | tf_op jit(solution)/shard_map/ppermute | solution.py:674
  18.2 10.8 %collective-permute-start.4 = (f32[7,8,640]{2,1,0:T(8,128)S(1)}, f32[7,8,640]{2,1,0:T(8,128)S(1)}, u32[]{:S(2)}, u32[]{:S(2)}) collective-permute-start(f32[7,8,640]{2,1,0:T(8,128)S(1)} %get-tuple-element.39), channel_id=1, source_target_pairs={{64,128},{128,64},{192,256},{256,192},{320,384},{384,320},{65,129}... | collective-permute-start | bytes 430088 | tf_op jit(solution)/shard_map/ppermute | solution.py:674
  23.6 6.6 %collective-permute-start.5 = (f32[7,8,640]{2,1,0:T(8,128)S(1)}, f32[7,8,640]{2,1,0:T(8,128)S(1)}, u32[]{:S(2)}, u32[]{:S(2)}) collective-permute-start(f32[7,8,640]{2,1,0:T(8,128)S(1)} %get-tuple-element.40), channel_id=1, source_target_pairs={{0,64},{64,0},{128,192},{192,128},{256,320},{320,256},{384,448},{4... | collective-permute-start | bytes 430088 | tf_op jit(solution)/shard_map/ppermute | solution.py:674

commit v6 on v5

--- a/solution.py
+++ b/solution.py
@@ -19,7 +19,7 @@
 Z0 = 5
 
 X_TILES = 12
-OWN_TILES = 12
+OWN_TILES = 11
 FAR_TILES = 7
 
 
@@ -47,10 +47,14 @@
     8,
 )
 HZ = ray_rows(
-    ladder("xe", 0, 0, 3, 0, 1) + ladder("xe", 1, 0, 3, 0, 1) + ladder("xh", 0, 1, 2, 0, 1) + ladder("xh", 1, 1, 2, 0, 1), 9
+    ladder("xe", 0, 0, 3, 0, 1) + ladder("xe", 1, 0, 3, 0, 1) + ladder("xh", 0, 1, 2, 0, 1) + ladder("xh", 1, 1, 2, 0, 1)
+    + materials([0]),
+    8,
 )
 LZ = ray_rows(
-    ladder("xe", 0, 0, 3, 7, -1) + ladder("xe", 1, 0, 3, 7, -1) + ladder("xh", 0, 1, 3, 7, -1) + ladder("xh", 1, 1, 2, 7, -1), 9
+    ladder("xe", 0, 0, 3, 7, -1) + ladder("xe", 1, 0, 3, 7, -1) + ladder("xh", 0, 1, 3, 7, -1) + ladder("xh", 1, 1, 2, 7, -1)
+    + materials([0]),
+    8,
 )
 HF = ray_rows(
     ladder("xhl", 0, 1, 2, 0, 1) + ladder("xhl", 1, 1, 3, 0, 1) + ladder("xeh", 0, 0, 3, 0, 1) + ladder("xeh", 1, 0, 3, 0, 1)
@@ -169,7 +173,7 @@
     g = jnp.full(shape, lorentz_ref[1], jnp.float32)
     s = jnp.full(shape, lorentz_ref[2], jnp.float32)
     scale = 1.0 / (1.0 + 0.5 * g)
-    return (1.0 - a * a - 0.5 * g) * scale, (1.0 - 0.5 * g) * scale, s * a * a * scale
+    return (1.0 - a * a - 0.5 * g) * scale, (1.0 - 0.5 * g) * scale, s * a * a * scale, a * a * scale
 
 
 def own_kinds(material_ref):
@@ -209,7 +213,7 @@
 def alone_kernel(
     e_hbm, h_hbm, p_hbm, material_hbm, eps_hbm, loss_hbm, lorentz_hbm,
     m0, m1, w0, w1, coef, shared,
-    e, h, a, b, ze, zh, xe, xh, rays, material, eps, loss, lorentz, sems,
+    e0, h0, p0, e, h, current, change, change_coef, packed_ref, ze, zh, xe, xh, rays, material, eps, loss, lorentz, sems,
 ):
     high_first = lax.rem(lax.axis_index("dev"), 2) == 0
     above_first = lax.rem(lax.axis_index("grp"), 2) == 0
@@ -217,56 +221,56 @@
         [(material_hbm, material), (eps_hbm, eps), (loss_hbm, loss), (lorentz_hbm, lorentz)], sems.at[pl.ds(0, 4)]
     )
     large = start_all(
-        [(e_hbm, e), (h_hbm, h), (p_hbm.at[0], a), (p_hbm.at[1], b)], sems.at[pl.ds(4, 4)]
+        [(e_hbm, e0), (h_hbm, h0), (p_hbm, p0)], sems.at[pl.ds(4, 3)]
     )
     wait_all(small)
     tables = kind_tables(eps, loss)
-    polar = polar_scalars(lorentz)
-    for i, v in enumerate([v for table in tables for v in table] + list(polar)):
+    p, q, r, t = polar_scalars(lorentz)
+    for i, v in enumerate([v for table in tables for v in table] + [p, q, r]):
         shared[i] = v
-    polar = [wide(v) for v in polar]
     ln = lane((N, LANES))
     packed = jnp.zeros((N, LANES), jnp.float32)
+    line = jnp.zeros((N, LANES), jnp.float32)
     for z, kind in enumerate(own_kinds(material)):
         packed = jnp.where(ln == z, kind, packed)
+        line = jnp.where(ln == sublane((N, LANES)) + N * z, kind, line)
         for j, v in enumerate(row_coefficients(kind, tables)):
             coef[j, z] = v
-    packed = wide(packed)
-    w0[8] = packed
-    w1[8] = packed
+        for j, v in enumerate((q, t, r)):
+            change_coef[j, z] = jnp.where(kind == 4.0, v, 0.0)
+    packed_ref[...] = packed
     wait_all(large[:2])
     row = sublane((N, NY))
     top = row == N - 1
     bottom = row == 0
 
     for n in range(1, STEPS + 1):
-        old, new = (a, b) if n % 2 == 1 else (b, a)
+        e_old, h_old = (e0, h0) if n == 1 else (e, h)
         for c in range(2):
-            ze[slot_e(n - 1, c)] = e[c, 0]
+            ze[slot_e(n - 1, c)] = e_old[c, 0]
         for z in range(N):
-            k = [wide(coef[j, z]) for j in range(5)]
-            retain, h_gain = k[0], k[1]
-            ex, ey, ez = (e[c, z] for c in range(3))
-            e1x, e1y = (e[c, z + 1] if z < N - 1 else None for c in range(2))
+            retain, h_gain = (wide(coef[j, z]) for j in range(2))
+            ex, ey, ez = (e_old[c, z] for c in range(3))
+            e1x, e1y = (e_old[c, z + 1] if z < N - 1 else None for c in range(2))
             r = slot_e(n - 1, 0)
             xe[z, r : r + 1, :] = ey[0:1, :]
             xe[z, r + 1 : r + 2, :] = ez[0:1, :]
             xa_y = choose(top, None, x_up(ey))
             xa_z = choose(top, None, x_up(ez))
-            hx = retain * h[0, z] - h_gain * ((y_ahead(ez) - ez) - sub(e1y, ey))
-            hy = retain * h[1, z] - h_gain * (sub(e1x, ex) - (xa_z - ez))
-            hz = retain * h[2, z] - h_gain * ((xa_y - ey) - (y_ahead(ex) - ex))
-            h[0, z] = hx
+            hy = retain * h_old[1, z] - h_gain * (sub(e1x, ex) - (xa_z - ez))
+            hz = retain * h_old[2, z] - h_gain * ((xa_y - ey) - (y_ahead(ex) - ex))
             h[1, z] = hy
             h[2, z] = hz
+            if n < STEPS or z == N - 1:
+                h[0, z] = retain * h_old[0, z] - h_gain * ((y_ahead(ez) - ez) - sub(e1y, ey))
             r = slot_h(n, 0)
             xh[z, r : r + 1, :] = hy[N - 1 : N, :]
             xh[z, r + 1 : r + 2, :] = hz[N - 1 : N, :]
         if n == 1:
             wait_all(large[2:])
         for z in range(N if n < STEPS else 0):
-            k = [wide(coef[j, z]) for j in range(5)]
-            ex, ey, ez = (e[c, z] for c in range(3))
+            retain, _, e_gain, inverse = (wide(coef[j, z]) for j in range(4))
+            q, t, r = (wide(change_coef[j, z]) for j in range(3))
             hx, hy, hz = (h[c, z] for c in range(3))
             lx, ly = (h[c, z - 1] if z else None for c in range(2))
             xb_y = choose(bottom, None, x_down(hy))
@@ -276,23 +280,35 @@
                 sub(hx, lx) - (hz - xb_z),
                 (hy - xb_y) - (hx - y_behind(hx)),
             )
-            for c, (curl, field) in enumerate(zip(curls, (ex, ey, ez))):
-                e[c, z], new[c, z] = e_update(curl, field, old[c, z], new[c, z], k, polar)
+            for c, curl in enumerate(curls):
+                if n == 1:
+                    cur, dif = p0[0, c, z], p0[0, c, z] - p0[1, c, z]
+                else:
+                    cur, dif = current[c, z], change[c, z]
+                field = e_old[c, z]
+                moved = q * dif - t * cur + r * field
+                e[c, z] = retain * field + e_gain * curl - inverse * moved
+                if n < STEPS - 1:
+                    current[c, z] = cur + moved
+                    change[c, z] = moved
         for c in range(2):
             zh[slot_h(n, c)] = h[c, N - 1]
 
     for i, table in enumerate((HX, LX)):
         for (kind, n, c, x), (tile, r) in table.items():
             if kind == "mat":
-                source = w0.at[8]
-            else:
-                source = ze.at[slot_e(n, c)] if kind == "ze" else zh.at[slot_h(n, c)]
+                rays[i, tile - 8, r : r + 1, 0:LANES] = packed_ref[x : x + 1, :]
+                continue
+            source = ze.at[slot_e(n, c)] if kind == "ze" else zh.at[slot_h(n, c)]
             rays[i, tile - 8, r : r + 1, :] = source[x : x + 1, :]
     for i, table in enumerate((HZ, LZ)):
         for (kind, n, c, z), (tile, r) in table.items():
+            if kind == "mat":
+                rays[2 + i, tile - 8, r : r + 1, 0:LANES] = jnp.sum(line, axis=0, keepdims=True)
+                continue
             at = slot_e(n, c) if kind == "xe" else slot_h(n, c)
             source = xe if kind == "xe" else xh
-            rays[2 + i, tile - 9, r : r + 1, :] = source[z, at : at + 1, :]
+            rays[2 + i, tile - 8, r : r + 1, :] = source[z, at : at + 1, :]
 
     def deal(first, one, other, tile, for_above, for_below):
         one[tile] = jnp.where(first, for_above, for_below)
@@ -304,7 +320,7 @@
     for i in range(4):
         deal(high_first, m0, m1, 8 + i, rays[1, i], rays[0, i])
     for i in range(3):
-        deal(above_first, w0, w1, 9 + i, rays[3, i], rays[2, i])
+        deal(above_first, w0, w1, 8 + i, rays[3, i], rays[2, i])
 
 
 def forward_kernel(r1, r0, v1, v0, high, low, ghosts, rays):
@@ -553,7 +569,12 @@
         own[1, i] = jnp.where(above_first, y, x)
     ghost_materials(side, [(high, HX, HIGH), (low, LX, LOW)])
     columns = [(z, 1, side[...], z) for z in range(N)]
-    columns += [(z, 0, own[1 if z < 0 else 0, 8, :, 0:LANES], z % N) for z in (*range(-4, 0), *range(N, N + 3))]
+    shape = (N, LANES)
+    for z in (*range(-4, 0), *range(N, N + 3)):
+        i, (t, r) = (1, LZ[("mat", 0, 0, 0)]) if z < 0 else (0, HZ[("mat", 0, 0, 0)])
+        line = jnp.broadcast_to(own[i, t, r : r + 1, 0:LANES], shape)
+        here = lane(shape) == sublane(shape) + N * (z % N)
+        columns.append((z, 0, jnp.sum(jnp.where(here, line, 0.0), axis=1, keepdims=True), 0))
     fill_coefficients(coef, columns, tables)
     for z in range(N):
         for j in range(5):
@@ -681,11 +702,13 @@
         out_shape=[f32(X_TILES, N, NY)] * 2 + [f32(OWN_TILES, N, NY)] * 2 + [f32(5, N, N, LANES), f32(19, N, LANES)],
         in_specs=[HBM] * 7,
         out_specs=[VMEM] * 6,
-        scratch_shapes=[vmem(3, N, N, NY)] * 4
+        scratch_shapes=[vmem(3, N, N, NY), vmem(3, N, N, NY), vmem(2, 3, N, N, NY)]
+        + [vmem(3, N, N, NY)] * 4
+        + [vmem(3, N, N, LANES), vmem(N, LANES)]
         + [vmem(*plane)] * 4
         + [vmem(4, 4, N, NY)]
         + small_tables()
-        + [pltpu.SemaphoreType.DMA((8,))],
+        + [pltpu.SemaphoreType.DMA((7,))],
         compiler_params=params(),
         name="alone",
     )(*inputs)

time: 34.1 us -> 34 us (level)
  no operation moved by 1% of the time
where the time goes in v6:
time: 34 us; the launch traced here: 33.7 us
  starting transfers between devices  21.4 us (63%)
  Pallas kernels  9.91 us (29%)
  waiting for transfers between devices  1.25 us (4%)
  between operations  0.77 us (2%)
    ppermute x6, starting transfers between devices, swap(): return lax.ppermute(block, axis, route)  21.4 us
    pallas_call x1, Pallas kernels, call_far(): pl.pallas_call(functools.partial(far_kernel, live), out_shape=[f32(3, N,...  3.58 us
    pallas_call x1, Pallas kernels, call_near(): pl.pallas_call(functools.partial(near_kernel, live), out_shape=[state] *...  3.1 us
    pallas_call x1, Pallas kernels, call_alone(): pl.pallas_call(alone_kernel, out_shape=[f32(X_TILES, N, NY)] * 2 + [f32(O...  3.04 us
    ppermute x6, waiting for transfers between devices, swap(): return lax.ppermute(block, axis, route)  1.25 us
  transfers between devices with their start and end apart: 6, of which 1 were waited for; matrix products, arithmetic and copies ran while one was open for 1% of the time, Pallas kernels for 10%

profile of v6, /device:TPU:249, one launch (start us, length us, event | category | flops | bytes accessed | tf_op | source)
XLA Modules:
  0.0 33.7 jit_solution(1849758557503131337)
XLA Ops:
  0.6 0.0 copy-start
  0.6 3.0 %alone.1 = (f32[12,8,640]{2,1,0:T(8,128)S(1)}, f32[12,8,640]{2,1,0:T(8,128)S(1)}, f32[11,8,640]{2,1,0:T(8,128)S(1)}, f32[11,8,640]{2,1,0:T(8,128)S(1)}, f32[5,8,...) custom-call(f32[3,8,8,640]{3,2,1,0:T(8,128)} %e_hbm.3, f32[3,8,8,640]{3,2,1,0:T(8,128)} %h_hbm.3, ...), custom_call_target="tpu_custom_call" | custom-call | tf_op jit(solution)/shard_map/alone/pallas_call | solution.py:700
  3.7 6.0 %collective-permute-start = (f32[12,8,640]{2,1,0:T(8,128)S(1)}, f32[12,8,640]{2,1,0:T(8,128)S(1)}, u32[]{:S(2)}, u32[]{:S(2)}) collective-permute-start(f32[12,8,640]{2,1,0:T(8,128)S(1)} %get-tuple-element.25), channel_id=1, source_target_pairs={{1,2},{2,1},{3,4},{4,3},{5,6},{6,5},{7,8},{8,7},{9,10},{10,9},{11,... | collective-permute-start | bytes 737288 | tf_op jit(solution)/shard_map/ppermute | solution.py:695
  9.7 1.9 %collective-permute-start.1 = (f32[12,8,640]{2,1,0:T(8,128)S(1)}, f32[12,8,640]{2,1,0:T(8,128)S(1)}, u32[]{:S(2)}, u32[]{:S(2)}) collective-permute-start(f32[12,8,640]{2,1,0:T(8,128)S(1)} %get-tuple-element.26), channel_id=1, source_target_pairs={{0,1},{1,0},{2,3},{3,2},{4,5},{5,4},{6,7},{7,6},{8,9},{9,8},{10,11... | collective-permute-start | bytes 737288 | tf_op jit(solution)/shard_map/ppermute | solution.py:695
  11.6 4.3 %collective-permute-start.2 = (f32[11,8,640]{2,1,0:T(8,128)S(1)}, f32[11,8,640]{2,1,0:T(8,128)S(1)}, u32[]{:S(2)}, u32[]{:S(2)}) collective-permute-start(f32[11,8,640]{2,1,0:T(8,128)S(1)} %get-tuple-element.30), channel_id=1, source_target_pairs={{64,128},{128,64},{192,256},{256,192},{320,384},{384,320},{65,129}... | collective-permute-start | bytes 675848 | tf_op jit(solution)/shard_map/ppermute | solution.py:695
  15.9 2.0 %collective-permute-start.3 = (f32[11,8,640]{2,1,0:T(8,128)S(1)}, f32[11,8,640]{2,1,0:T(8,128)S(1)}, u32[]{:S(2)}, u32[]{:S(2)}) collective-permute-start(f32[11,8,640]{2,1,0:T(8,128)S(1)} %get-tuple-element.31), channel_id=1, source_target_pairs={{0,64},{64,0},{128,192},{192,128},{256,320},{320,256},{384,448},{4... | collective-permute-start | bytes 675848 | tf_op jit(solution)/shard_map/ppermute | solution.py:695
  17.9 0.0 collective-permute-done.r1
  17.9 0.0 collective-permute-done.1.r0
  17.9 0.2 forward.1
  18.1 5.3 %collective-permute-start.4 = (f32[7,8,640]{2,1,0:T(8,128)S(1)}, f32[7,8,640]{2,1,0:T(8,128)S(1)}, u32[]{:S(2)}, u32[]{:S(2)}) collective-permute-start(f32[7,8,640]{2,1,0:T(8,128)S(1)} %get-tuple-element.39), channel_id=1, source_target_pairs={{64,128},{128,64},{192,256},{256,192},{320,384},{384,320},{65,129}... | collective-permute-start | bytes 430088 | tf_op jit(solution)/shard_map/ppermute | solution.py:695
  23.4 1.9 %collective-permute-start.5 = (f32[7,8,640]{2,1,0:T(8,128)S(1)}, f32[7,8,640]{2,1,0:T(8,128)S(1)}, u32[]{:S(2)}, u32[]{:S(2)}) collective-permute-start(f32[7,8,640]{2,1,0:T(8,128)S(1)} %get-tuple-element.40), channel_id=1, source_target_pairs={{0,64},{64,0},{128,192},{192,128},{256,320},{320,256},{384,448},{4... | collective-permute-start | bytes 430088 | tf_op jit(solution)/shard_map/ppermute | solution.py:695
  25.4 0.0 copy-done
  25.4 0.1 multiply_cosine_fusion
  25.5 0.1 copy.12
  25.6 0.1 reshape.103.weights
  25.7 0.0 collective-permute-done.2.g1
  25.7 0.0 collective-permute-done.3.g0
  25.7 3.1 %near.1 = (f32[3,17,2,8,640]{4,3,2,1,0:T(8,128)S(1)}, f32[3,17,2,8,640]{4,3,2,1,0:T(8,128)S(1)}, f32[3,17,2,8,640]{4,3,2,1,0:T(8,128)S(1)}, f32[3,17,2,8,640]{4,...) custom-call(f32[3,8,8,640]{3,2,1,0:T(8,128)} %e_hbm.3, ...), custom_call_target="tpu_custom_call" | custom-call | flops 20000000 | bytes 20000000 | tf_op jit(solution)/shard_map/near/pallas_call | solution.py:731
  28.8 0.0 collective-permute-done.4.f1
  28.8 1.2 %collective-permute-done.5.f0 = f32[7,8,640]{2,1,0:T(8,128)S(1)} collective-permute-done((f32[7,8,640]{2,1,0:T(8,128)S(1)}, f32[7,8,640]{2,1,0:T(8,128)S(1)}, u32[]{:S(2)}, u32[]{:S(2)}) %collective-permute-start.5) | collective-permute-done | bytes 143392 | tf_op jit(solution)/shard_map/ppermute | solution.py:695
  30.1 3.6 %far.1 = (f32[3,8,8,640]{3,2,1,0:T(8,128)}, f32[3,8,8,640]{3,2,1,0:T(8,128)}, f32[2,3,8,8,640]{4,3,2,1,0:T(8,128)}, f32[4,2,3,1,8,640]{5,4,3,2,1,0:T(8,128)}) custom-call(f32[3,17,2,8,640]{4,3,2,1,0:T(8,128)S(1)} %get-tuple-element.32.e_in, f32[3,17,2,8,640]{4,3,2,1,0:T(8,128)S(1)} %get-tuple-element.33.h_in, ...), custom_call_target="tpu_custom_call" | custom-call | tf_op jit(solution)/shard_map/far/pallas_call | solution.py:746
  (2 shorter events, 0.0 us)
Async XLA Ops:
  0.6 24.7 %copy-start = (f32[4]{0:T(128)S(1)}, f32[4]{0:T(128)}, u32[]{:S(2)}) copy-start(f32[4]{0:T(128)} %param.15) | copy-start | bytes 52
  3.7 14.2 %collective-permute-start = (f32[12,8,640]{2,1,0:T(8,128)S(1)}, f32[12,8,640]{2,1,0:T(8,128)S(1)}, u32[]{:S(2)}, u32[]{:S(2)}) collective-permute-start(f32[12,8,640]{2,1,0:T(8,128)S(1)} %get-tuple-element.25), channel_id=1, source_target_pairs={{1,2},{2,1},{3,4},{4,3},{5,6},{6,5},{7,8},{8,7},{9,10},{10,9},{11,... | collective-permute-start | bytes 737288 | tf_op jit(solution)/shard_map/ppermute | solution.py:695
  9.7 8.2 %collective-permute-start.1 = (f32[12,8,640]{2,1,0:T(8,128)S(1)}, f32[12,8,640]{2,1,0:T(8,128)S(1)}, u32[]{:S(2)}, u32[]{:S(2)}) collective-permute-start(f32[12,8,640]{2,1,0:T(8,128)S(1)} %get-tuple-element.26), channel_id=1, source_target_pairs={{0,1},{1,0},{2,3},{3,2},{4,5},{5,4},{6,7},{7,6},{8,9},{9,8},{10,11... | collective-permute-start | bytes 737288 | tf_op jit(solution)/shard_map/ppermute | solution.py:695
  11.6 14.1 %collective-permute-start.2 = (f32[11,8,640]{2,1,0:T(8,128)S(1)}, f32[11,8,640]{2,1,0:T(8,128)S(1)}, u32[]{:S(2)}, u32[]{:S(2)}) collective-permute-start(f32[11,8,640]{2,1,0:T(8,128)S(1)} %get-tuple-element.30), channel_id=1, source_target_pairs={{64,128},{128,64},{192,256},{256,192},{320,384},{384,320},{65,129}... | collective-permute-start | bytes 675848 | tf_op jit(solution)/shard_map/ppermute | solution.py:695
  15.9 9.8 %collective-permute-start.3 = (f32[11,8,640]{2,1,0:T(8,128)S(1)}, f32[11,8,640]{2,1,0:T(8,128)S(1)}, u32[]{:S(2)}, u32[]{:S(2)}) collective-permute-start(f32[11,8,640]{2,1,0:T(8,128)S(1)} %get-tuple-element.31), channel_id=1, source_target_pairs={{0,64},{64,0},{128,192},{192,128},{256,320},{320,256},{384,448},{4... | collective-permute-start | bytes 675848 | tf_op jit(solution)/shard_map/ppermute | solution.py:695
  18.1 10.7 %collective-permute-start.4 = (f32[7,8,640]{2,1,0:T(8,128)S(1)}, f32[7,8,640]{2,1,0:T(8,128)S(1)}, u32[]{:S(2)}, u32[]{:S(2)}) collective-permute-start(f32[7,8,640]{2,1,0:T(8,128)S(1)} %get-tuple-element.39), channel_id=1, source_target_pairs={{64,128},{128,64},{192,256},{256,192},{320,384},{384,320},{65,129}... | collective-permute-start | bytes 430088 | tf_op jit(solution)/shard_map/ppermute | solution.py:695
  23.4 6.6 %collective-permute-start.5 = (f32[7,8,640]{2,1,0:T(8,128)S(1)}, f32[7,8,640]{2,1,0:T(8,128)S(1)}, u32[]{:S(2)}, u32[]{:S(2)}) collective-permute-start(f32[7,8,640]{2,1,0:T(8,128)S(1)} %get-tuple-element.40), channel_id=1, source_target_pairs={{0,64},{64,0},{128,192},{192,128},{256,320},{320,256},{384,448},{4... | collective-permute-start | bytes 430088 | tf_op jit(solution)/shard_map/ppermute | solution.py:695
